TPU v7x, 32 devices: a whole 2x2x4 slice. The times are simulated.
32 devices in a mesh: dp: 8 (over z, y), chan: 4 (over x, core).
Axes of the slice: x: 2, y: 2, z: 4, core: 2. Of those that a mesh axis runs over, the one named last changes fastest.
Arguments:
- image_rows: float32 [8, 16, 16, 640], P('dp', 'chan'), may hold values from -6 to 6
- groups: int32 [8], P('dp'), may hold values from 0 to 1, as said below
- conv_first: float32 [3, 3, 640, 640], P(None, None, 'chan'), may hold values from -0.078125 to 0.078125
- conv_second: float32 [3, 3, 640, 640], P(None, None, 'chan'), may hold values from -0.078125 to 0.078125
- gain_first: float32 [640], P('chan'), may hold values from 0.25 to 1.75
- shift_first: float32 [640], P('chan'), may hold values from -3 to 3
- gain_second: float32 [640], P('chan'), may hold values from 0.25 to 1.75
- shift_second: float32 [640], P('chan'), may hold values from -3 to 3
- cotangent: float32 [8, 16, 16, 640], P('dp', None, None, 'chan'), may hold values from -6 to 6
Outputs:
- block_out: float32 [8, 16, 16, 640], P('dp', None, None, 'chan')
- input_grad: float32 [8, 16, 16, 640], P('dp', 'chan')
- conv_first_grad: float32 [3, 3, 640, 640], P(None, None, 'chan')
- conv_second_grad: float32 [3, 3, 640, 640], P(None, None, 'chan')
- gain_first_grad: float32 [640], P('chan')
- shift_first_grad: float32 [640], P('chan')
- gain_second_grad: float32 [640], P('chan')
- shift_second_grad: float32 [640], P('chan')
- grad_norm: float32 [], replicated
Inputs may be any that keep to these rules, and one draw needn't show every extreme that they name: `groups`: 1 marks a 16 x 16 map, 0 a map of half that side in the top left corner; each aligned block of 1 images holds at least one 1.
All inputs are finite; a program needn't handle non-finite values.
Results may differ from a plain program's by a relative error of at most 0.0003.
Values sent between devices are 32-bit elements; how exact they have to be, the bound alone decides.
A program may use at most 320 MiB of HBM per device.

v0:
```python
import jax
import jax.numpy as jnp
from jax import lax
from jax.sharding import PartitionSpec as P

epsilon = 1e-05
sam_radius = 0.05
norm_floor = 1e-06


def valid_pixels(groups, extent_full):
    places = jnp.arange(extent_full, dtype=jnp.int32)
    extent = jnp.where(groups == 1, extent_full, extent_full // 2).astype(jnp.int32)
    inside = places[None, :] < extent[:, None]
    return (inside[:, :, None] & inside[:, None, :]).astype(jnp.float32)[..., None]


def convolve(values, kernel):
    return lax.conv_general_dilated(
        values,
        kernel,
        (1, 1),
        "SAME",
        dimension_numbers=("NHWC", "HWIO", "NHWC"),
        precision=lax.Precision.HIGHEST,
    )


def silu_slope(preact):
    sigmoid = jax.nn.sigmoid(preact)
    return sigmoid * (1.0 + preact * (1.0 - sigmoid))


def moments(values, validity):
    summed, squares, pixels = lax.psum(
        (
            jnp.sum(values * validity, axis=(0, 1, 2)),
            jnp.sum(validity * values * values, axis=(0, 1, 2)),
            jnp.sum(validity),
        ),
        "dp",
    )
    center = summed / pixels
    spread = squares / pixels - center * center
    return (center, lax.rsqrt(spread + epsilon), pixels)


def project(values, kernel):
    return lax.psum_scatter(convolve(values, kernel), "chan", scatter_dimension=3, tiled=True)


def conv_backward(upstream, values, kernel):
    columns = lax.all_gather(upstream, "chan", axis=3, tiled=True)
    offset = jnp.int32(0)
    inputs_grad = jnp.zeros_like(values)
    kernel_grad = jnp.zeros_like(kernel)
    breadth = columns.shape[3]
    kernel_part = lax.dynamic_slice_in_dim(kernel, offset, breadth, 3)
    primal, pull = jax.vjp(convolve, values, kernel_part)
    values_part, kernel_part_grad = pull(columns)
    kernel_grad = lax.dynamic_update_slice_in_dim(kernel_grad, kernel_part_grad, offset, 3)
    return (inputs_grad + values_part, kernel_grad)


def batch_sums(dpre, scaled):
    return lax.psum((jnp.sum(dpre, axis=(0, 1, 2)), jnp.sum(dpre * scaled, axis=(0, 1, 2))), "dp")


def on_device(
    image_rows,
    groups,
    conv_first,
    conv_second,
    gain_first,
    shift_first,
    gain_second,
    shift_second,
    cotangent,
):
    inputs = lax.all_to_all(image_rows, "chan", split_axis=3, concat_axis=1, tiled=True)
    validity = valid_pixels(groups, inputs.shape[1])
    cot_valid = cotangent * validity
    center_one, rscale_one, pixels = moments(inputs, validity)
    scaled_one = (inputs - center_one) * rscale_one
    pre_one = scaled_one * gain_first + shift_first
    act_one = jax.nn.silu(pre_one) * validity
    inner = project(act_one, conv_first) * validity
    center_two, rscale_two, pixels_again = moments(inner, validity)
    scaled_two = (inner - center_two) * rscale_two
    pre_two = scaled_two * gain_second + shift_second
    act_two = jax.nn.silu(pre_two) * validity
    block_out = inputs * validity + project(act_two, conv_second) * validity
    dact_two, kernel_two_part = conv_backward(cot_valid, act_two, conv_second)
    dpre_two = dact_two * validity * silu_slope(pre_two)
    shift_two_grad, gain_two_grad = batch_sums(dpre_two, scaled_two)
    dinner = (
        gain_second
        * rscale_two
        * (dpre_two - validity * (shift_two_grad + scaled_two * gain_two_grad) / pixels)
    )
    dact_one, kernel_one_part = conv_backward(dinner, act_one, conv_first)
    dpre_one = dact_one * validity * silu_slope(pre_one)
    shift_one_grad, gain_one_grad = batch_sums(dpre_one, scaled_one)
    small_squares = (
        jnp.sum(gain_one_grad**2)
        + jnp.sum(shift_one_grad**2)
        + jnp.sum(gain_two_grad**2)
        + jnp.sum(shift_two_grad**2)
    )
    kernel_one_sum, kernel_two_sum = lax.psum((kernel_one_part, kernel_two_part), "dp")
    local_sq = jnp.sum(kernel_one_sum**2) + jnp.sum(kernel_two_sum**2) + small_squares
    squares = lax.psum(local_sq, "chan")
    factor = sam_radius * lax.rsqrt(squares + norm_floor)
    kernel_one = conv_first + factor * kernel_one_sum
    kernel_two = conv_second + factor * kernel_two_sum
    grad_norm = jnp.sqrt(squares)
    moved_gain_one = gain_first + factor * gain_one_grad
    moved_shift_one = shift_first + factor * shift_one_grad
    moved_gain_two = gain_second + factor * gain_two_grad
    moved_shift_two = shift_second + factor * shift_two_grad
    pre_one_new = scaled_one * moved_gain_one + moved_shift_one
    act_one_new = jax.nn.silu(pre_one_new) * validity
    inner_new = project(act_one_new, kernel_one) * validity
    scaled_two_new = (inner_new - center_two) * rscale_two
    pre_two_new = scaled_two_new * moved_gain_two + moved_shift_two
    act_two_new = jax.nn.silu(pre_two_new) * validity
    dact_two_new, kernel_two_grad = conv_backward(cot_valid, act_two_new, kernel_two)
    dpre_two_new = dact_two_new * validity * silu_slope(pre_two_new)
    gain_two_new_grad = jnp.sum(dpre_two_new * scaled_two_new, axis=(0, 1, 2))
    shift_two_new_grad = jnp.sum(dpre_two_new, axis=(0, 1, 2))
    dinner_new = moved_gain_two * rscale_two * dpre_two_new
    dact_one_new, kernel_one_grad = conv_backward(dinner_new, act_one_new, kernel_one)
    dpre_one_new = dact_one_new * validity * silu_slope(pre_one_new)
    gain_one_new_grad = jnp.sum(dpre_one_new * scaled_one, axis=(0, 1, 2))
    shift_one_new_grad = jnp.sum(dpre_one_new, axis=(0, 1, 2))
    inputs_grad = moved_gain_one * rscale_one * dpre_one_new + cot_valid
    input_grad = lax.all_to_all(inputs_grad, "chan", split_axis=1, concat_axis=3, tiled=True)
    (
        kernel_one_grad,
        kernel_two_grad,
        gain_one_new_grad,
        shift_one_new_grad,
        gain_two_new_grad,
        shift_two_new_grad,
    ) = lax.psum(
        (
            kernel_one_grad,
            kernel_two_grad,
            gain_one_new_grad,
            shift_one_new_grad,
            gain_two_new_grad,
            shift_two_new_grad,
        ),
        "dp",
    )
    return (
        block_out,
        input_grad,
        kernel_one_grad,
        kernel_two_grad,
        gain_one_new_grad,
        shift_one_new_grad,
        gain_two_new_grad,
        shift_two_new_grad,
        grad_norm,
    )


def solution(mesh):
    return jax.shard_map(
        on_device,
        mesh=mesh,
        in_specs=(
            P("dp", "chan", None, None),
            P("dp"),
            P(None, None, "chan", None),
            P(None, None, "chan", None),
            P("chan"),
            P("chan"),
            P("chan"),
            P("chan"),
            P("dp", None, None, "chan"),
        ),
        out_specs=(
            P("dp", None, None, "chan"),
            P("dp", "chan", None, None),
            P(None, None, "chan", None),
            P(None, None, "chan", None),
            P("chan"),
            P("chan"),
            P("chan"),
            P("chan"),
            P(),
        ),
        check_vma=False,
    )
```

profile of v0, /device:TPU:0, one launch (start us, length us, event | category | flops | bytes accessed | tf_op | source)
XLA Modules:
  0.0 1250.2 jit_solution(9023641063683597135)
XLA Ops:
  7.2 1.4 copy.186
  8.6 1.7 reshape.555
  10.3 4.3 all-to-all-start
  16.1 3.5 all-to-all-done
  20.1 1.1 reduce.161
  21.2 0.9 reshape.556
  23.1 23.3 %all-reduce.4 = (f32[160]{0:T(256)S(1)}, f32[]{:T(128)}, f32[160]{0:T(256)S(1)}) all-reduce(f32[160]{0:T(256)S(1)} %get-tuple-element.64, f32[]{:T(128)} %convert_reduce_fusion, f32[160]{0:T(256)S(1)} %get-tuple-element.63), channel_id=1, replica_groups=mesh['dp'=8,'chan'=4] {'dp'}, use_global_device_ids=true, to_apply=%region_1.2 | all-reduce | flops 321 | bytes 2568 | tf_op jit(solution)/shard_map/psum | solution.py:35
  47.5 9.5 convolution_select_fusion.1
  57.3 61.9 %copy.231 = f32[1,16,16,640]{0,2,1,3:T(8,128)} copy(f32[1,16,16,640]{3,1,2,0:T(8,128)S(1)} %slice_bitcast_fusion.2) | data formatting | bytes 1310720
  119.1 29.2 %bitcast_reduce_fusion.2 = f32[640,16,16]{2,1,0:T(8,128)} fusion(f32[1,16,16,640]{0,2,1,3:T(8,128)} %copy.231), kind=kLoop, calls=%fused_computation.2 | loop fusion | bytes 1310720
  148.3 17.2 %reshape.399 = f32[640,256]{1,0:T(8,128)} reshape(f32[640,16,16]{2,1,0:T(8,128)} %bitcast_reduce_fusion.2) | data formatting | bytes 1310720
  165.8 18.5 %reduce-scatter.10.cloned.1.call-done = f32[160,256]{1,0:T(8,128)} async-done(((f32[640,256]{1,0:T(8,128)}), f32[160,256]{1,0:T(8,128)}) %reduce-scatter.10.cloned.1.call-update) | async-done | bytes 163856
  184.3 21.6 %reshape.400 = f32[160,16,16,1]{3,2,1,0:T(8,128)} reshape(f32[160,256]{1,0:T(8,128)} %reduce-scatter.10.cloned.1.call-done) | data formatting | bytes 327680
  205.9 19.3 %copy.192 = f32[1,16,16,160]{3,1,2,0:T(8,128)S(1)} copy(f32[1,16,16,160]{0,2,1,3:T(8,128)} %bitcast.245) | data formatting | bytes 327680 | tf_op jit(solution)/shard_map/reduce_scatter | solution.py:49
  225.4 0.7 copy.199
  226.1 32.9 %all_gather.10 = f32[1,16,16,640]{2,1,0,3:T(8,128)} all-gather(f32[1,16,16,160]{2,1,0,3:T(8,128)S(1)} %copy.199), channel_id=1, replica_groups=mesh['dp'=8,'chan'=4] {'chan'}, dimensions={3}, use_global_device_ids=true | all-gather | bytes 819200 | tf_op jit(solution)/shard_map/all_gather | solution.py:53
  259.0 3.3 copy.200
  262.3 4.4 copy.208
  267.2 2.1 copy-done.47
  269.4 7.2 convolution_select_fusion.2
  276.8 21.4 %all-reduce.3 = (f32[160]{0:T(256)S(1)}, f32[160]{0:T(256)S(1)}) all-reduce(f32[160]{0:T(256)S(1)} %get-tuple-element.66, f32[160]{0:T(256)S(1)} %get-tuple-element.65), channel_id=1, replica_groups=mesh['dp'=8,'chan'=4] {'dp'}, use_global_device_ids=true, to_apply=%region_8.9 | all-reduce | flops 320 | bytes 2560 | tf_op jit(solution)/shard_map/psum | solution.py:35
  299.1 17.1 %all-reduce.2 = (f32[160]{0:T(256)S(1)}, f32[160]{0:T(256)S(1)}) all-reduce(f32[160]{0:T(256)S(1)} %get-tuple-element.74, f32[160]{0:T(256)S(1)} %get-tuple-element.73), channel_id=1, replica_groups=mesh['dp'=8,'chan'=4] {'dp'}, use_global_device_ids=true, to_apply=%region_15.16 | all-reduce | flops 320 | bytes 2560 | tf_op jit(solution)/shard_map/psum | solution.py:66
  316.3 0.8 subtract_multiply_fusion.1
  317.8 32.7 %all_gather.11 = f32[1,16,16,640]{2,1,0,3:T(8,128)} all-gather(f32[1,16,16,160]{2,1,0,3:T(8,128)S(1)} %copy.204), channel_id=1, replica_groups=mesh['dp'=8,'chan'=4] {'chan'}, dimensions={3}, use_global_device_ids=true | all-gather | bytes 819200 | tf_op jit(solution)/shard_map/all_gather | solution.py:53
  350.5 4.8 copy.206
  355.4 21.4 %fusion.68 = f32[3,3,160,640]{3,2,1,0:T(8,128)} fusion(f32[1,16,16,640]{3,0,2,1:T(1,128)S(1)} %copy.208, f32[1,16,16,160]{3,1,2,0:T(8,128)S(1)} %get-tuple-element.105), kind=kOutput, calls=%fused_computation.83 | convolution fusion | flops 2600140800 | bytes 4505600 | tf_op jit(solution)/shard_map/transpose(jvp())/conv_general_dilated | solution.py:19
  376.7 21.8 %fusion.70 = f32[3,3,160,640]{3,2,1,0:T(8,128)} fusion(f32[1,16,16,640]{3,0,2,1:T(1,128)S(1)} %copy.206, f32[1,16,16,160]{3,1,2,0:T(8,128)S(1)} %multiply_multiply_fusion.5), kind=kOutput, calls=%fused_computation.85 | convolution fusion | flops 2600140800 | bytes 4505600 | tf_op jit(solution)/shard_map/transpose(jvp())/conv_general_dilated | solution.py:19
  398.6 3.3 copy.209
  402.2 10.0 convolution_select_fusion
  412.8 1.4 copy-done.48
  414.3 7.5 fusion.17
  422.1 20.4 %all-reduce.1 = (f32[160]{0:T(256)S(1)}, f32[160]{0:T(256)S(1)}) all-reduce(f32[160]{0:T(256)S(1)} %get-tuple-element.72, f32[160]{0:T(256)S(1)} %get-tuple-element.71), channel_id=1, replica_groups=mesh['dp'=8,'chan'=4] {'dp'}, use_global_device_ids=true, to_apply=%region_21.22 | all-reduce | flops 320 | bytes 2560 | tf_op jit(solution)/shard_map/psum | solution.py:66
  447.6 192.4 %all-reduce.12.cloned.1.call-done = (f32[3,3,160,640]{3,2,1,0:T(8,128)}, f32[3,3,160,640]{3,2,1,0:T(8,128)}) async-done(((f32[3,3,160,640]{3,2,1,0:T(8,128)}, f32[3,3,160,640]{3,2,1,0:T(8,128)}), (f32[3,3,160,640]{3,2,1,0:T(8,128)}, f32[3,3,160,640]{3,2,1,0:T(8,128)})) %all-reduce.12.cloned.1.call-update) | async-done | bytes 7372816 | tf_op jit(solution)/shard_map/psum | solution.py:110
  640.1 3.7 multiply_reduce_fusion
  643.8 1.5 multiply_reduce_fusion.1
  646.7 61.9 %copy.233 = f32[1,16,16,640]{0,2,1,3:T(8,128)} copy(f32[1,16,16,640]{3,1,2,0:T(8,128)S(1)} %slice_bitcast_fusion.1) | data formatting | bytes 1310720
  708.5 7.7 psum.140
  717.9 10.9 fusion.16
  729.0 61.9 %copy.235 = f32[1,16,16,640]{0,2,1,3:T(8,128)} copy(f32[1,16,16,640]{3,1,2,0:T(8,128)S(1)} %slice_bitcast_fusion) | data formatting | bytes 1310720
  790.9 29.2 %bitcast_reduce_fusion = f32[640,16,16]{2,1,0:T(8,128)} fusion(f32[1,16,16,640]{0,2,1,3:T(8,128)} %copy.235), kind=kLoop, calls=%fused_computation | loop fusion | bytes 1310720
  820.1 5.0 reshape.403
  825.2 29.8 %bitcast_reduce_fusion.1 = f32[640,16,16]{2,1,0:T(8,128)} fusion(f32[1,16,16,640]{0,2,1,3:T(8,128)} %copy.233), kind=kLoop, calls=%fused_computation.1 | loop fusion | bytes 1310720
  855.0 5.1 reshape.401
  860.2 10.3 fusion.23
  870.9 21.6 %reshape.404 = f32[160,16,16,1]{3,2,1,0:T(8,128)} reshape(f32[160,256]{1,0:T(8,128)} %reduce-scatter.14.cloned.1.call-done) | data formatting | bytes 327680
  892.5 19.3 %copy.218 = f32[1,16,16,160]{3,1,2,0:T(8,128)S(1)} copy(f32[1,16,16,160]{0,2,1,3:T(8,128)} %bitcast.246) | data formatting | bytes 327680 | tf_op jit(solution)/shard_map/reduce_scatter | solution.py:49
  911.8 0.8 fusion.93
  913.4 32.4 %all_gather.12 = f32[1,16,16,640]{2,1,0,3:T(8,128)} all-gather(f32[1,16,16,160]{2,1,0,3:T(8,128)S(1)} %copy.219), channel_id=1, replica_groups=mesh['dp'=8,'chan'=4] {'chan'}, dimensions={3}, use_global_device_ids=true | all-gather | bytes 819200 | tf_op jit(solution)/shard_map/all_gather | solution.py:53
  945.8 4.9 copy.227
  950.6 21.4 %fusion.64 = f32[3,3,160,640]{3,2,1,0:T(8,128)} fusion(f32[1,16,16,640]{3,0,2,1:T(1,128)S(1)} %copy-done.16, f32[1,16,16,160]{3,1,2,0:T(8,128)S(1)} %get-tuple-element.104), kind=kOutput, calls=%fused_computation.79 | convolution fusion | flops 2600140800 | bytes 4505600 | tf_op jit(solution)/shard_map/transpose(jvp())/conv_general_dilated | solution.py:19
  972.0 21.8 %fusion.66 = f32[3,3,160,640]{3,2,1,0:T(8,128)} fusion(f32[1,16,16,640]{3,0,2,1:T(1,128)S(1)} %copy.227, f32[1,16,16,160]{3,1,2,0:T(8,128)S(1)} %multiply_multiply_fusion.3), kind=kOutput, calls=%fused_computation.81 | convolution fusion | flops 2600140800 | bytes 4505600 | tf_op jit(solution)/shard_map/transpose(jvp())/conv_general_dilated | solution.py:19
  993.9 21.6 %reshape.402 = f32[160,16,16,1]{3,2,1,0:T(8,128)} reshape(f32[160,256]{1,0:T(8,128)} %reduce-scatter.12.cloned.1.call-done) | data formatting | bytes 327680
  1015.5 19.4 %copy.197 = f32[1,16,16,160]{3,1,2,0:T(8,128)S(1)} copy(f32[1,16,16,160]{0,2,1,3:T(8,128)} %bitcast.247) | data formatting | bytes 327680 | tf_op jit(solution)/shard_map/reduce_scatter | solution.py:49
  1034.9 3.7 copy.220
  1039.1 1.8 copy-done.5
  1040.9 9.3 fusion.20
  1050.7 0.8 copy.224
  1051.6 3.4 all-to-all-start.1
  1055.7 0.9 copy.230
  1056.5 21.2 %all-reduce = (f32[160]{0:T(256)}, f32[160]{0:T(256)}, f32[160]{0:T(256)}, f32[160]{0:T(256)}) all-reduce(f32[160]{0:T(256)S(1)} %get-tuple-element.70, f32[160]{0:T(256)S(1)} %get-tuple-element.69, f32[160]{0:T(256)S(1)} %copy-done.46, f32[160]{0:T(256)S(1)} %copy-done.45), channel_id=1, replica_groups=mesh['dp'=8,'chan'=4] {'dp'}, use_global_device_ids=true, to_apply=%region_33.34 | all-reduce | flops 640 | bytes 5120 | tf_op jit(solution)/shard_map/psum | solution.py:145
  1078.0 0.9 all_to_all.33
  1078.8 157.4 %all-reduce.10.cloned.1.call-done = (f32[3,3,160,640]{3,2,1,0:T(8,128)}, f32[3,3,160,640]{3,2,1,0:T(8,128)}) async-done(((f32[3,3,160,640]{3,2,1,0:T(8,128)}, f32[3,3,160,640]{3,2,1,0:T(8,128)}), (f32[3,3,160,640]{3,2,1,0:T(8,128)}, f32[3,3,160,640]{3,2,1,0:T(8,128)})) %all-reduce.10.cloned.1.call-update) | async-done | bytes 7372816 | tf_op jit(solution)/shard_map/psum | solution.py:145
  1236.2 4.3 copy.410
  1240.5 1.8 copy.411
  (172 shorter events, 13.5 us)
Async XLA Ops:
  7.2 39.8 %copy-start.26 = (f32[160]{0:T(256)S(1)}, f32[160]{0:T(256)}, u32[]{:S(2)}) copy-start(f32[160]{0:T(256)} %param.13) | copy-start | bytes 1924
  7.2 39.8 %copy-start.28 = (f32[160]{0:T(256)S(1)}, f32[160]{0:T(256)}, u32[]{:S(2)}) copy-start(f32[160]{0:T(256)} %param.14) | copy-start | bytes 1924
  10.3 37.2 %copy-start.49 = (pred[8,3]{0,1:T(4,128)(4,1)S(1)}, pred[8,3]{0,1:T(4,128)(4,1)}, u32[]{:S(2)}) copy-start(pred[8,3]{0,1:T(4,128)(4,1)} %constant.56) | copy-start | bytes 76
  10.3 9.3 all-to-all-start
  14.6 169.7 %reduce-scatter.10.cloned.1.call-start = ((), (), s32[]{:S(2)}) async-start(), calls=%async_computation.5 | async-start | bytes 819200
  15.4 300.8 %copy-start.10 = (f32[16,16]{0,1:T(8,128)}, f32[16,16]{0,1:T(8,128)S(1)}, u32[]{:S(2)}) copy-start(f32[16,16]{0,1:T(8,128)S(1)} %and_convert_fusion.1) | copy-start | bytes 3076
  23.1 142.5 %copy-start = (f32[1,16,16,160]{3,1,2,0:T(8,128)}, f32[1,16,16,160]{3,1,2,0:T(8,128)S(1)}, u32[]{:S(2)}) copy-start(f32[1,16,16,160]{3,1,2,0:T(8,128)S(1)} %all_to_all.29) | copy-start | bytes 491524
  47.0 118.6 %copy-start.18 = (f32[160]{0:T(256)}, f32[160]{0:T(256)S(1)}, u32[]{:S(2)}) copy-start(f32[160]{0:T(256)S(1)} %get-tuple-element.102) | copy-start | bytes 1924
  47.0 118.6 %copy-start.21 = (f32[160]{0:T(256)}, f32[160]{0:T(256)S(1)}, u32[]{:S(2)}) copy-start(f32[160]{0:T(256)S(1)} %get-tuple-element.103) | copy-start | bytes 1924
  165.6 474.5 %all-reduce.12.cloned.1.call-start = ((), (), s32[]{:S(2)}) async-start(), calls=%async_computation.9 | async-start | bytes 14745600 | tf_op jit(solution)/shard_map/psum | solution.py:110
  205.9 19.3 %copy-start.17 = (f32[1,16,16,160]{3,2,1,0:T(8,128)S(1)}, f32[1,16,16,160]{3,2,1,0:T(8,128)}, u32[]{:S(2)}) copy-start(f32[1,16,16,160]{3,2,1,0:T(8,128)} %param.17) | copy-start | bytes 491524
  225.4 33.6 %copy-start.8 = (f32[1,16,16,160]{3,1,2,0:T(8,128)}, f32[1,16,16,160]{3,1,2,0:T(8,128)S(1)}, u32[]{:S(2)}) copy-start(f32[1,16,16,160]{3,1,2,0:T(8,128)S(1)} %get-tuple-element.107) | copy-start | bytes 491524
  266.7 88.6 %copy-start.15 = (f32[1,16,16,640]{3,0,2,1:T(1,128)}, f32[1,16,16,640]{3,0,2,1:T(1,128)S(1)}, u32[]{:S(2)}) copy-start(f32[1,16,16,640]{3,0,2,1:T(1,128)S(1)} %copy.208) | copy-start | bytes 1966084
  266.7 2.6 copy-start.47
  267.1 9.5 copy-start.6
  269.4 7.2 copy-start.13
  269.4 28.8 %copy-start.36 = (f32[160]{0:T(256)S(1)}, f32[160]{0:T(256)}, u32[]{:S(2)}) copy-start(f32[160]{0:T(256)} %param.15) | copy-start | bytes 1924
  269.4 29.5 %copy-start.43 = (f32[160]{0:T(256)S(1)}, f32[160]{0:T(256)}, u32[]{:S(2)}) copy-start(f32[160]{0:T(256)} %param.16) | copy-start | bytes 1924
  298.8 51.7 %copy-start.24 = (f32[160]{0:T(256)}, f32[160]{0:T(256)S(1)}, u32[]{:S(2)}) copy-start(f32[160]{0:T(256)S(1)} %get-tuple-element.99) | copy-start | bytes 1924
  298.8 51.7 %copy-start.34 = (f32[160]{0:T(256)}, f32[160]{0:T(256)S(1)}, u32[]{:S(2)}) copy-start(f32[160]{0:T(256)S(1)} %get-tuple-element.100) | copy-start | bytes 1924
  316.2 34.3 %copy-start.38 = (f32[160]{0:T(256)}, f32[160]{0:T(256)S(1)}, u32[]{:S(2)}) copy-start(f32[160]{0:T(256)S(1)} %get-tuple-element.81) | copy-start | bytes 1924
  316.2 34.3 %copy-start.40 = (f32[160]{0:T(256)}, f32[160]{0:T(256)S(1)}, u32[]{:S(2)}) copy-start(f32[160]{0:T(256)S(1)} %get-tuple-element.82) | copy-start | bytes 1924
  398.5 3.7 copy-start.50
  398.5 472.4 %reduce-scatter.14.cloned.1.call-start = ((), (), s32[]{:S(2)}) async-start(), calls=%async_computation.7 | async-start | bytes 819200
  412.1 2.1 copy-start.48
  414.2 7.7 copy-start.1
  414.2 7.7 copy-start.11
  414.2 7.7 copy-start.19
  414.2 7.7 copy-start.22
  414.2 7.7 copy-start.27
  414.2 7.7 copy-start.29
  414.2 30.8 %copy-start.39 = (f32[160]{0:T(256)S(1)}, f32[160]{0:T(256)}, u32[]{:S(2)}) copy-start(f32[160]{0:T(256)} %copy-done.38) | copy-start | bytes 1924
  414.2 32.1 %copy-start.41 = (f32[160]{0:T(256)S(1)}, f32[160]{0:T(256)}, u32[]{:S(2)}) copy-start(f32[160]{0:T(256)} %copy-done.40) | copy-start | bytes 1924
  640.1 3.7 copy-start.4
  717.5 153.1 %copy-start.30 = (f32[160]{0:T(256)}, f32[160]{0:T(256)S(1)}, u32[]{:S(2)}) copy-start(f32[160]{0:T(256)S(1)} %get-tuple-element.95) | copy-start | bytes 1924
  717.5 153.1 %copy-start.32 = (f32[160]{0:T(256)}, f32[160]{0:T(256)S(1)}, u32[]{:S(2)}) copy-start(f32[160]{0:T(256)S(1)} %get-tuple-element.109) | copy-start | bytes 1924
  825.2 168.7 %reduce-scatter.12.cloned.1.call-start = ((), (), s32[]{:S(2)}) async-start(), calls=%async_computation.6 | async-start | bytes 819200
  855.0 5.2 copy-start.7
  855.0 5.2 copy-start.14
  860.1 10.5 copy-start.25
  860.1 10.5 copy-start.37
  860.1 10.5 copy-start.44
  860.2 376.1 %all-reduce.10.cloned.1.call-start = ((), (), s32[]{:S(2)}) async-start(), calls=%async_computation.8 | async-start | bytes 14745600 | tf_op jit(solution)/shard_map/psum | solution.py:145
  892.5 19.3 %copy-start.35 = (f32[160]{0:T(256)S(1)}, f32[160]{0:T(256)}, u32[]{:S(2)}) copy-start(f32[160]{0:T(256)} %copy-done.34) | copy-start | bytes 1924
  945.8 4.9 copy-start.16
  1038.6 2.3 copy-start.5
  1038.6 2.3 copy-start.51
  1040.8 9.6 copy-start.2
  1040.8 9.6 copy-start.12
  1040.8 9.6 copy-start.20
  1040.8 9.6 copy-start.23
  1040.8 9.6 copy-start.31
  1040.9 9.6 copy-start.33
  1040.9 9.8 copy-start.9
  1040.9 9.8 copy-start.42
  1050.2 6.3 copy-start.45
  1050.3 6.3 copy-start.46
  1051.6 26.2 %all-to-all-start.1 = ((f32[1,16,16,160]{3,2,0,1:T(8,128)}), f32[1,16,16,160]{3,2,0,1:T(8,128)S(1)}, u32[]{:S(2)}, u32[]{:S(2)}) async-start(f32[1,16,16,160]{3,2,0,1:T(8,128)} %copy.224), calls=%async_computation.1 | async-start | bytes 524288 | tf_op jit(solution)/shard_map/all_to_all | solution.py:137
  1236.2 4.3 copy-start.3
Sparse Core Ops, SparseCore 0:
  165.7 18.5 reduce-scatter.9
  398.6 241.3 all-reduce.11
  825.3 20.6 reduce-scatter.13
  860.2 20.6 reduce-scatter.11
  994.0 242.2 all-reduce.9
where the time goes:
time: 1250 us
  local copies, waits for them, and re-layouts  473 us (38%)
  waiting for transfers between devices  372 us (30%)
  blocking collectives  209 us (17%)
  matrix products  151 us (12%)
  between operations  22.1 us (2%)
  other arithmetic  14.7 us (1%)
    unnamed x122, local copies, waits for them, and re-layouts  382 us
    psum x1, waiting for transfers between devices, on_device(): lax.psum((kernel_one_part, kernel_two_part), 'dp')  192 us
    psum x1, waiting for transfers between devices, on_device(): lax.psum((kernel_one_grad, kernel_two_grad, gain_one_new_grad, shift_one_...  157 us
    conv_general_dilated x11, matrix products, convolve(): lax.conv_general_dilated(values, kernel, (1, 1), 'SAME', dimension_number...  151 us
    all_gather x3, blocking collectives, conv_backward(): columns = lax.all_gather(upstream, 'chan', axis=3, tiled=True)  98 us
    reduce_scatter x3, local copies, waits for them, and re-layouts, project(): lax.psum_scatter(convolve(values, kernel), 'chan', scatter_dimension=3, t...  57.9 us
    psum x2, blocking collectives, moments(): lax.psum((jnp.sum(values * validity, axis=(0, 1, 2)), jnp.sum(validity *...  44.6 us
    psum x2, blocking collectives, batch_sums(): lax.psum((jnp.sum(dpre, axis=(0, 1, 2)), jnp.sum(dpre * scaled, axis=(0,...  37.6 us
  transfers between devices with their start and end apart: 7, of which 4 were waited for; matrix products, arithmetic and copies ran while one was open for 17% of the time, Pallas kernels for 0%

commit v1 on v0

--- a/solution.py
+++ b/solution.py
@@ -1,11 +1,772 @@
+import functools
+
 import jax
 import jax.numpy as jnp
 from jax import lax
+from jax.experimental import pallas as pl
+from jax.experimental.pallas import tpu as pltpu
 from jax.sharding import PartitionSpec as P
 
 epsilon = 1e-05
 sam_radius = 0.05
 norm_floor = 1e-06
+MESH = pl.DeviceIdType.MESH
+F32, BF16 = jnp.float32, jnp.bfloat16
+VMEM = pltpu.VMEM
+DMA = pltpu.SemaphoreType.DMA
+LIMIT = 60 << 20
+
+
+class Plan:
+    def __init__(self, nd, nc, channels, side):
+        self.nd, self.nc, self.ch, self.side = nd, nc, channels, side
+        self.cb, self.db, self.px = channels // nc, channels // nd, side * side
+        self.ny = 2
+        self.nz = nd // 2
+        self.offs = tuple((r, s) for r in (-1, 0, 1) for s in (-1, 0, 1))
+
+
+def split(v):
+    hi = v.astype(BF16)
+    return hi, (v - hi.astype(F32)).astype(BF16)
+
+
+def dot(a, b):
+    return lax.dot_general(a, b, (((1,), (0,)), ((), ())), preferred_element_type=F32)
+
+
+def dot_nt(a, b):
+    return lax.dot_general(a, b, (((1,), (1,)), ((), ())), preferred_element_type=F32)
+
+
+def edge_masks(side, px):
+    lane = lax.broadcasted_iota(jnp.int32, (1, px), 1)
+    col = lax.rem(lane, side)
+    row = lax.div(lane, side)
+    one = jnp.ones((1, px), F32)
+    zero = jnp.zeros((1, px), F32)
+    rows = {-1: jnp.where(row >= 1, one, zero), 0: None, 1: jnp.where(row < side - 1, one, zero)}
+    cols = {-1: jnp.where(col >= 1, one, zero), 0: None, 1: jnp.where(col < side - 1, one, zero)}
+    return rows, cols
+
+
+def moved(v, lanes, mask):
+    if lanes:
+        v = pltpu.roll(v, (-lanes) % v.shape[1], axis=1)
+    return v if mask is None else v * mask
+
+
+def shifts(v, side, sign=1):
+    rows, cols = edge_masks(side, v.shape[1])
+    by_col = {s: moved(v, s, cols[s]) for s in (-1, 0, 1)}
+    return [moved(by_col[sign * s], sign * r * side, rows[sign * r]) for r in (-1, 0, 1) for s in (-1, 0, 1)]
+
+
+def gather_taps(prod, side, n):
+    rows, cols = edge_masks(side, prod.shape[1])
+    total = None
+    for j, s in enumerate((-1, 0, 1)):
+        part = None
+        for i, r in enumerate((-1, 0, 1)):
+            t = 3 * i + j
+            m = moved(prod[t * n : (t + 1) * n], r * side, rows[r])
+            part = m if part is None else part + m
+        m = moved(part, s, cols[s])
+        total = m if total is None else total + m
+    return total
+
+
+def sigmoid(t):
+    return 1.0 / (1.0 + jnp.exp(-t))
+
+
+def slope(pre):
+    s = sigmoid(pre)
+    return s * (1.0 + pre * (1.0 - s))
+
+
+def lanes_sum(v):
+    return jnp.sum(v, axis=1, keepdims=True)
+
+
+def valid_map(flag, side, px):
+    lane = lax.broadcasted_iota(jnp.int32, (1, px), 1)
+    half = (lax.rem(lane, side) < side // 2) & (lax.div(lane, side) < side // 2)
+    return jnp.where(half, jnp.ones((1, px), F32), flag)
+
+
+def to_row(col):
+    n = col.shape[0]
+    eye = lax.broadcasted_iota(jnp.int32, (n, n), 0) == lax.broadcasted_iota(jnp.int32, (n, n), 1)
+    return jnp.sum(jnp.where(eye, col, 0.0), axis=0, keepdims=True)
+
+
+def to_col(row):
+    n = row.shape[1]
+    eye = lax.broadcasted_iota(jnp.int32, (n, n), 0) == lax.broadcasted_iota(jnp.int32, (n, n), 1)
+    return jnp.sum(jnp.where(eye, row, 0.0), axis=1, keepdims=True)
+
+
+def pack_cols(cols, n):
+    lane = lax.broadcasted_iota(jnp.int32, (n, 128), 1)
+    out = jnp.zeros((n, 128), F32)
+    for k, col in enumerate(cols):
+        out = jnp.where(lane == k, col, out)
+    return out
+
+
+def send(src, dst, ss, rs, device):
+    return pltpu.make_async_remote_copy(
+        src_ref=src, dst_ref=dst, send_sem=ss, recv_sem=rs, device_id=device, device_id_type=MESH
+    )
+
+
+def here():
+    return lax.axis_index("dp"), lax.axis_index("chan")
+
+
+def greet(plan):
+    d, c = here()
+    barrier = pltpu.get_barrier_semaphore()
+    for j in range(1, plan.nd):
+        pl.semaphore_signal(barrier, inc=1, device_id=(lax.rem(d + j, plan.nd), c), device_id_type=MESH)
+    for j in range(1, plan.nc):
+        pl.semaphore_signal(barrier, inc=1, device_id=(d, lax.rem(c + j, plan.nc)), device_id_type=MESH)
+    pl.semaphore_wait(barrier, plan.nd - 1 + plan.nc - 1)
+
+
+class LineGather:
+    def __init__(self, plan, buf, ss, rs):
+        self.p, self.buf, self.ss, self.rs = plan, buf, ss, rs
+        d, self.c = here()
+        self.z, self.y = lax.div(d, plan.ny), lax.rem(d, plan.ny)
+
+    def copy(self, kind, zs, z_to, y_to):
+        slot = zs * self.p.ny + self.y
+        return send(
+            self.buf.at[slot], self.buf.at[slot], self.ss.at[kind, zs], self.rs.at[slot], (z_to * self.p.ny + y_to, self.c)
+        )
+
+    def others(self, zs, do):
+        for j in range(1, self.p.ny):
+            do(self.copy(1 + j, zs, self.z, lax.rem(self.y + j, self.p.ny)))
+
+    def up(self, zs):
+        return self.copy(0, zs, lax.min(self.z + 1, self.p.nz - 1), self.y)
+
+    def down(self, zs):
+        return self.copy(1, zs, lax.max(self.z - 1, 0), self.y)
+
+    def got(self, slot):
+        partner = lax.rem(self.y + 1, self.p.ny)
+        send(self.buf.at[slot], self.buf.at[slot], self.ss.at[0, 0], self.rs.at[slot], (self.z * self.p.ny + partner, self.c)).wait_recv()
+
+    def start(self):
+        pl.when(self.z < self.p.nz - 1)(lambda: self.up(self.z).start())
+        pl.when(self.z > 0)(lambda: self.down(self.z).start())
+        self.others(self.z, lambda cp: cp.start())
+
+    def step(self, s):
+        z, nz = self.z, self.p.nz
+
+        @pl.when(z - s >= 0)
+        def _():
+            zs = z - s
+            self.got(zs * self.p.ny + self.y)
+            pl.when(z < nz - 1)(lambda: self.up(zs).start())
+            self.others(zs, lambda cp: cp.start())
+
+        @pl.when(z + s <= nz - 1)
+        def _():
+            zs = z + s
+            self.got(zs * self.p.ny + self.y)
+            pl.when(z > 0)(lambda: self.down(zs).start())
+            self.others(zs, lambda cp: cp.start())
+
+    def finish(self):
+        z, nz = self.z, self.p.nz
+        for zs in range(nz):
+            for j in range(1, self.p.ny):
+                self.got(zs * self.p.ny + lax.rem(self.y + j, self.p.ny))
+        for zs in range(nz):
+            self.others(zs, lambda cp: cp.wait_send())
+            pl.when((zs <= z) & (z < nz - 1))(lambda: self.up(zs).wait_send())
+            pl.when((zs >= z) & (z > 0))(lambda: self.down(zs).wait_send())
+
+
+def gather_kernel(p, x_ref, cot_ref, k2_ref, par_ref, flag_ref, x_out, c_out, a2_out, par_out, flag_out,
+                  xs, rx, ks, sx, rxs, sk, rk, sp, rp, sf, rf, s1, r1, s2, r2):
+    d, c = here()
+    rows = x_ref.shape[0]
+    greet(p)
+    owner = lax.div(d * p.db, p.cb)
+    inner = pl.multiple_of(lax.rem(d * p.db, p.cb), 8)
+
+    for j in range(p.nc):
+        xs[j] = x_ref[:, j * p.cb : (j + 1) * p.cb]
+    a2a = []
+    for j in range(1, p.nc):
+        to = lax.rem(c + j, p.nc)
+        a2a.append(send(xs.at[to], rx.at[c], sx.at[j], rxs.at[c], (d, to)))
+    for cp in a2a:
+        cp.start()
+    rx[c] = xs[c]
+
+    par_out[c] = par_ref[...]
+    flag_out[d] = flag_ref[...]
+    small = []
+    for j in range(1, p.nc):
+        small.append(send(par_ref, par_out.at[c], sp.at[j], rp.at[c], (d, lax.rem(c + j, p.nc))))
+    for j in range(1, p.nd):
+        small.append(send(flag_ref, flag_out.at[d], sf.at[j], rf.at[d], (lax.rem(d + j, p.nd), c)))
+    for cp in small:
+        cp.start()
+
+    c_out[d] = cot_ref[...].T
+    cots = LineGather(p, c_out, s2, r2)
+
+    for j in range(1, p.nc):
+        a2a[j - 1].wait_send()
+        other = lax.rem(c + j, p.nc)
+        send(xs.at[other], rx.at[other], sx.at[j], rxs.at[other], (d, other)).wait_recv()
+    x_out[d] = rx[...].reshape(p.nc * rows, p.cb).T
+    ins = LineGather(p, x_out, s1, r1)
+    ins.start()
+    cots.start()
+
+    @pl.when(c == owner)
+    def _():
+        for j in range(p.nc):
+            ks[j] = k2_ref[:, pl.ds(inner, p.db), j * p.cb : (j + 1) * p.cb].reshape(9 * p.db, p.cb)
+        a2_out[...] = ks[c]
+        for j in range(1, p.nc):
+            to = lax.rem(c + j, p.nc)
+            send(ks.at[to], a2_out, sk.at[j], rk, (d, to)).start()
+
+    for s in range(1, p.nz):
+        ins.step(s)
+    for s in range(1, p.nz):
+        cots.step(s)
+    ins.finish()
+    cots.finish()
+
+    @pl.when(c == owner)
+    def _():
+        for j in range(1, p.nc):
+            to = lax.rem(c + j, p.nc)
+            send(ks.at[to], a2_out, sk.at[j], rk, (d, to)).wait_send()
+
+    @pl.when(c != owner)
+    def _():
+        send(ks.at[0], a2_out, sk.at[0], rk, (d, owner)).wait_recv()
+
+    for cp in small:
+        cp.wait_send()
+    for j in range(1, p.nc):
+        other = lax.rem(c + j, p.nc)
+        send(par_ref, par_out.at[other], sp.at[0], rp.at[other], (d, other)).wait_recv()
+    for j in range(1, p.nd):
+        other = lax.rem(d + j, p.nd)
+        send(flag_ref, flag_out.at[other], sf.at[0], rf.at[other], (other, c)).wait_recv()
+
+
+def gather(p, x, cot, k2, par, flag):
+    rows = x.shape[0]
+    out = lambda *s: jax.ShapeDtypeStruct(s, F32)
+    return pl.pallas_call(
+        functools.partial(gather_kernel, p),
+        out_shape=(
+            out(p.nd, p.cb, p.px), out(p.nd, p.cb, p.px), out(9 * p.db, p.cb), out(p.nc, 8, p.cb), out(p.nd, 8, p.px),
+        ),
+        in_specs=[pl.BlockSpec(memory_space=VMEM)] * 5,
+        out_specs=tuple([pl.BlockSpec(memory_space=VMEM)] * 5),
+        scratch_shapes=[
+            VMEM((p.nc, rows, p.cb), F32), VMEM((p.nc, rows, p.cb), F32), VMEM((p.nc, 9 * p.db, p.cb), F32),
+            DMA((p.nc,)), DMA((p.nc,)), DMA((p.nc,)), DMA, DMA((p.nc,)), DMA((p.nc,)), DMA((p.nd,)), DMA((p.nd,)),
+            DMA((1 + p.ny, p.nz)), DMA((p.nd,)), DMA((1 + p.ny, p.nz)), DMA((p.nd,)),
+        ],
+        compiler_params=pltpu.CompilerParams(collective_id=0, has_side_effects=True, vmem_limit_bytes=LIMIT),
+    )(x, cot, k2, par, flag)
+
+
+def masked_stats(ref, flag_ref, p, n):
+    zero = jnp.zeros((n, 1), F32)
+
+    def first(i, carry):
+        total, pixels = carry
+        val = valid_map(flag_ref[i, :1], p.side, p.px)
+        return total + lanes_sum(ref[i] * val), pixels + lanes_sum(val)
+
+    total, pixels = lax.fori_loop(0, p.nd, first, (zero, jnp.zeros((1, 1), F32)))
+    center = total / pixels
+
+    def second(i, carry):
+        val = valid_map(flag_ref[i, :1], p.side, p.px)
+        off = ref[i] - center
+        return carry + lanes_sum(val * off * off)
+
+    spread = lax.fori_loop(0, p.nd, second, zero) / pixels
+    return center, lax.rsqrt(spread + epsilon), pixels
+
+
+def project_kernel(p, take_stats, x_ref, c_ref, a1_ref, a2_ref, par_ref, flag_ref, sums_out, *rest):
+    if take_stats:
+        stat_out, rest = rest[0], rest[1:]
+    a_cat, part, buf1, half, buf2, s1, r1, s2, r2, s3, r3 = rest
+    d, c = here()
+    k = lax.rem(c, 2)
+    across = (d, c + 1 - 2 * k)
+    far = (d, lax.rem(c + 2, 4))
+    hb = p.db // 2
+    mine = pl.multiple_of(k * hb, 8)
+    greet(p)
+
+    hi, lo = split(a1_ref[...])
+    a_cat[0] = jnp.concatenate([hi, hi, lo], axis=1)
+    for t in range(9):
+        hi, lo = split(a2_ref[(8 - t) * p.db : (9 - t) * p.db])
+        a_cat[1, t * p.db : (t + 1) * p.db] = jnp.concatenate([hi, hi, lo], axis=1)
+
+    if take_stats:
+        center, rscale, _ = masked_stats(x_ref, flag_ref, p, p.cb)
+        stat_out[...] = pack_cols([center, rscale], p.cb)
+        gain, shift = par_ref[:, 0:1], par_ref[:, 1:2]
+    else:
+        center, rscale, gain, shift = (par_ref[:, j : j + 1] for j in range(4))
+
+    n = 2 * p.nd
+
+    def produce(i):
+        @pl.when(i < p.nd)
+        def _():
+            val = valid_map(flag_ref[i, :1], p.side, p.px)
+            pre = (x_ref[i] - center) * rscale * gain + shift
+            act = pre * sigmoid(pre) * val
+            ah, al = split(act)
+            prod = dot(a_cat[0], jnp.concatenate([ah, al, ah], axis=0))
+            part[i] = gather_taps(prod, p.side, p.db) * val
+
+        @pl.when(i >= p.nd)
+        def _():
+            img = lax.max(i - p.nd, 0)
+            val = valid_map(flag_ref[img, :1], p.side, p.px)
+            ah, al = split(c_ref[img] * val)
+            prod = dot(a_cat[1], jnp.concatenate([ah, al, ah], axis=0))
+            part[i] = gather_taps(prod, p.side, p.db) * val
+
+        send(part.at[i], buf1.at[i], s1.at[i], r1.at[i], across).start()
+
+    def reduce_chip(i):
+        send(part.at[i], buf1.at[i], s1.at[i], r1.at[i], across).wait()
+        half[i] = part[i, pl.ds(mine, hb)] + buf1[i, pl.ds(mine, hb)]
+        send(half.at[i], buf2.at[i], s2.at[i], r2.at[i], far).start()
+
+    def reduce_far(i):
+        send(half.at[i], buf2.at[i], s2.at[i], r2.at[i], far).wait()
+        rows = sums_out.at[i, pl.ds(mine, hb)]
+        rows[...] = half[i] + buf2[i]
+        send(rows, rows, s3.at[i], r3.at[i], across).start()
+
+    def done(i):
+        rows = sums_out.at[i, pl.ds(mine, hb)]
+        cp = send(rows, sums_out.at[i, pl.ds(pl.multiple_of(hb - mine, 8), hb)], s3.at[i], r3.at[i], across)
+        cp.wait()
+
+    def body(i, _):
+        pl.when(i < n)(lambda: produce(lax.min(i, n - 1)))
+        pl.when((i >= 1) & (i < n + 1))(lambda: reduce_chip(lax.clamp(0, i - 1, n - 1)))
+        pl.when((i >= 3) & (i < n + 3))(lambda: reduce_far(lax.clamp(0, i - 3, n - 1)))
+        pl.when(i >= 4)(lambda: done(lax.clamp(0, i - 4, n - 1)))
+        return 0
+
+    lax.fori_loop(0, n + 4, body, 0)
+
+
+def project(p, take_stats, collective, x, cot, a1, a2, par, flags):
+    n = 2 * p.nd
+    out = lambda *s: jax.ShapeDtypeStruct(s, F32)
+    shapes = (out(n, p.db, p.px),) + ((out(p.cb, 128),) if take_stats else ())
+    return pl.pallas_call(
+        functools.partial(project_kernel, p, take_stats),
+        out_shape=shapes,
+        in_specs=[pl.BlockSpec(memory_space=VMEM)] * 6,
+        out_specs=tuple([pl.BlockSpec(memory_space=VMEM)] * len(shapes)),
+        scratch_shapes=[
+            VMEM((2, 9 * p.db, 3 * p.cb), BF16),
+            VMEM((n, p.db, p.px), F32), VMEM((n, p.db, p.px), F32),
+            VMEM((n, p.db // 2, p.px), F32), VMEM((n, p.db // 2, p.px), F32),
+        ] + [DMA((n,))] * 6,
+        compiler_params=pltpu.CompilerParams(collective_id=collective, has_side_effects=True, vmem_limit_bytes=LIMIT),
+    )(x, cot, a1, a2, par, flags)
+
+
+def scatter_images(p, part, buf, ss, rs, order):
+    d, c = here()
+    return send(part.at[order], buf.at[d], ss.at[order], rs.at[d], (order, c))
+
+
+def collect_images(p, part, buf, ss, rs):
+    d, c = here()
+    total = part[d]
+    for j in range(1, p.nd):
+        other = lax.rem(d + j, p.nd)
+        send(part.at[other], buf.at[other], ss.at[other], rs.at[other], (other, c)).wait()
+        total = total + buf[other]
+    return total
+
+
+def ascent_kernel(p, inner_ref, x_ref, c_ref, a1_ref, a2_ref, par1_ref, par2_ref, flag_ref,
+                  out_ref, a1_out, a2_out, par1_out, par2_out, norm_out,
+                  colh, coll, bm, part, buf, g1, g2, dpre_s, msg, rmsg, msg2, rmsg2, ss, rs, sm, rm, sm2, rm2):
+    d, c = here()
+    greet(p)
+    cb, db, px, side = p.cb, p.db, p.px, p.side
+    nd = p.nd
+    center1, rs1, gain1, shift1 = (par1_ref[:, j : j + 1] for j in range(4))
+    gain2, shift2 = par2_ref[:, 0:1], par2_ref[:, 1:2]
+    center2, rs2, pixels = masked_stats(inner_ref.at[pl.ds(0, nd)], flag_ref, p, db)
+
+    def val_of(i):
+        return valid_map(flag_ref[i, :1], side, px)
+
+    def dense(ref):
+        hi, lo = split(ref[...].T)
+        bm[0], bm[1] = hi, lo
+
+    def set_cols(maps):
+        for t, m in enumerate(maps):
+            hi, lo = split(m)
+            colh[t * db : (t + 1) * db] = hi
+            coll[t * db : (t + 1) * db] = lo
+
+    def im2col_dot():
+        return dot(bm[0], colh[...]) + dot(bm[0], coll[...]) + dot(bm[1], colh[...])
+
+    def wgrad(other):
+        oh, ol = split(other)
+        left = jnp.concatenate([colh[...], colh[...], coll[...]], axis=1)
+        return dot_nt(left, jnp.concatenate([oh, ol, oh], axis=1))
+
+    dense(a2_ref)
+    g2[...] = jnp.zeros_like(g2)
+    zero = jnp.zeros((db, 1), F32)
+
+    def forward(j, carry):
+        i = lax.rem(d + 1 + j, nd)
+        val = val_of(i)
+        scaled = (inner_ref[i] - center2) * rs2
+        pre = scaled * gain2 + shift2
+        sg = sigmoid(pre)
+        act = pre * sg * val
+        dpre = inner_ref[nd + i] * val * (sg * (1.0 + pre * (1.0 - sg)))
+        dpre_s[i] = dpre
+        set_cols(shifts(act, side))
+        part[i] = im2col_dot()
+        pl.when(i != d)(lambda: scatter_images(p, part, buf, ss, rs, i).start())
+        g2[...] += wgrad(c_ref[i] * val)
+        return carry[0] + lanes_sum(dpre), carry[1] + lanes_sum(dpre * scaled)
+
+    sh2, gg2 = lax.fori_loop(0, nd, forward, (zero, zero))
+
+    dense(a1_ref)
+    g1[...] = jnp.zeros_like(g1)
+    zero = jnp.zeros((cb, 1), F32)
+
+    def backward(i, carry):
+        val = val_of(i)
+        scaled = (inner_ref[i] - center2) * rs2
+        dinner = gain2 * rs2 * (dpre_s[i] - val * (sh2 + scaled * gg2) / pixels)
+        set_cols(shifts(dinner, side, -1))
+        scaled1 = (x_ref[i] - center1) * rs1
+        pre1 = scaled1 * gain1 + shift1
+        sg = sigmoid(pre1)
+        g1[...] += wgrad(pre1 * sg * val)
+        dpre1 = im2col_dot() * val * (sg * (1.0 + pre1 * (1.0 - sg)))
+        return carry[0] + lanes_sum(dpre1), carry[1] + lanes_sum(dpre1 * scaled1)
+
+    sh1, gg1 = lax.fori_loop(0, nd, backward, (zero, zero))
+
+    sq = jnp.sum(g1[...] * g1[...] + g2[...] * g2[...], keepdims=True)
+    small2 = jnp.sum(sh2 * sh2 + gg2 * gg2, keepdims=True)
+    sq = sq + jnp.where(c == 0, small2, 0.0)
+    row = lax.broadcasted_iota(jnp.int32, (8, cb), 0)
+    msg[...] = jnp.where(row == 0, to_row(sh1), jnp.where(row == 1, to_row(gg1), sq))
+    copies = [send(msg, rmsg.at[d], sm.at[j], rm.at[d], (lax.rem(d + j, nd), c)) for j in range(1, nd)]
+    for cp in copies:
+        cp.start()
+    total = msg[...]
+    for j in range(1, nd):
+        other = lax.rem(d + j, nd)
+        send(msg, rmsg.at[other], sm.at[0], rm.at[other], (other, c)).wait_recv()
+    rmsg[d] = msg[...]
+    total = rmsg[0]
+    for j in range(1, nd):
+        total = total + rmsg[j]
+    sh1, gg1 = to_col(total[0:1]), to_col(total[1:2])
+    sq = total[2:3, 0:1] + jnp.sum(sh1 * sh1 + gg1 * gg1, keepdims=True)
+    msg2[...] = jnp.broadcast_to(sq, (8, 128))
+    copies2 = [send(msg2, rmsg2.at[c], sm2.at[j], rm2.at[c], (d, lax.rem(c + j, p.nc))) for j in range(1, p.nc)]
+    for cp in copies2:
+        cp.start()
+    for j in range(1, p.nc):
+        other = lax.rem(c + j, p.nc)
+        send(msg2, rmsg2.at[other], sm2.at[0], rm2.at[other], (d, other)).wait_recv()
+    rmsg2[c] = msg2[...]
+    sq = rmsg2[0]
+    for j in range(1, p.nc):
+        sq = sq + rmsg2[j]
+    norm_out[...] = jnp.sqrt(sq)
+    factor = (sam_radius * lax.rsqrt(sq + norm_floor))[0:1, 0:1]
+
+    a1_out[...] = a1_ref[...] + factor * g1[...]
+    a2_out[...] = a2_ref[...] + factor * g2[...]
+    par1_out[...] = pack_cols([center1, rs1, gain1 + factor * gg1, shift1 + factor * sh1], cb)
+    par2_out[...] = pack_cols([center2, rs2, gain2 + factor * gg2, shift2 + factor * sh2], db)
+
+    total = collect_images(p, part, buf, ss, rs)
+    val = val_of(d)
+    out_ref[...] = ((x_ref[d] + total) * val).T
+    for cp in copies + copies2:
+        cp.wait_send()
+
+
+def ascent(p, inner, x, cot, a1, a2, par1, par2, flags):
+    out = lambda *s: jax.ShapeDtypeStruct(s, F32)
+    nd, cb, db, px = p.nd, p.cb, p.db, p.px
+    return pl.pallas_call(
+        functools.partial(ascent_kernel, p),
+        out_shape=(out(px, cb), out(9 * db, cb), out(9 * db, cb), out(cb, 128), out(db, 128), out(8, 128)),
+        in_specs=[pl.BlockSpec(memory_space=VMEM)] * 8,
+        out_specs=tuple([pl.BlockSpec(memory_space=VMEM)] * 6),
+        scratch_shapes=[
+            VMEM((9 * db, px), BF16), VMEM((9 * db, px), BF16), VMEM((2, cb, 9 * db), BF16),
+            VMEM((nd, cb, px), F32), VMEM((nd, cb, px), F32), VMEM((9 * db, cb), F32), VMEM((9 * db, cb), F32),
+            VMEM((nd, db, px), F32), VMEM((8, cb), F32), VMEM((nd, 8, cb), F32), VMEM((8, 128), F32), VMEM((p.nc, 8, 128), F32),
+            DMA((nd,)), DMA((nd,)), DMA((nd,)), DMA((nd,)), DMA((p.nc,)), DMA((p.nc,)),
+        ],
+        compiler_params=pltpu.CompilerParams(collective_id=2, has_side_effects=True, vmem_limit_bytes=LIMIT),
+    )(inner, x, cot, a1, a2, par1, par2, flags)
+
+
+def perturbed_kernel(p, inner_ref, x_ref, c_ref, a1_ref, par1_ref, par2_ref, flag_ref,
+                     in_out, g1_out, g2_out, vec_out,
+                     colh, coll, bm, part, buf, dall, call, act2, lefth, right, xs, rx, msg, rmsg,
+                     ss, rs, sg_, rg_, sc_, rc_, sb, rb, sx, rxs, sm, rm, dsem, stage):
+    d, c = here()
+    greet(p)
+    cb, db, px, side, nd, nc = p.cb, p.db, p.px, p.side, p.nd, p.nc
+    z, y = lax.div(d, p.ny), lax.rem(d, p.ny)
+    k = lax.rem(c, 2)
+    center1, rs1, gain1, shift1 = (par1_ref[:, j : j + 1] for j in range(4))
+    center2, rs2, gain2, shift2 = (par2_ref[:, j : j + 1] for j in range(4))
+
+    def val_of(i):
+        return valid_map(flag_ref[i, :1], side, px)
+
+    def masked(i, _):
+        call[c, i] = c_ref[i] * val_of(i)
+        return 0
+
+    lax.fori_loop(0, nd, masked, 0)
+    far, across = lax.rem(c + 2, 4), c + 1 - 2 * k
+    cot_far = send(call.at[c], call.at[c], sc_.at[0], rc_.at[c], (d, far))
+    cot_across = send(call.at[c], call.at[c], sc_.at[1], rc_.at[c], (d, across))
+    cot_far.start()
+    cot_across.start()
+
+    zero = jnp.zeros((db, 1), F32)
+
+    def inner_grad(i, carry):
+        val = val_of(i)
+        scaled = (inner_ref[i] - center2) * rs2
+        pre = scaled * gain2 + shift2
+        sg = sigmoid(pre)
+
+        @pl.when(z == c)
+        def _():
+            act2[y, i] = pre * sg * val
+
+        dpre = inner_ref[nd + i] * val * (sg * (1.0 + pre * (1.0 - sg)))
+        dall[d, i] = gain2 * rs2 * dpre
+        return carry[0] + lanes_sum(dpre), carry[1] + lanes_sum(dpre * scaled)
+
+    sh2, gg2 = lax.fori_loop(0, nd, inner_grad, (zero, zero))
+    grads = LineGather(p, dall, sg_, rg_)
+    grads.start()
+
+    def act_copy(kind, ys, z_to, y_to):
+        return send(act2.at[ys], act2.at[ys], sb.at[kind], rb.at[ys], (z_to * p.ny + y_to, c))
+
+    up = lambda: act_copy(0, y, lax.min(z + 1, p.nz - 1), y)
+    down = lambda: act_copy(1, y, lax.max(z - 1, 0), y)
+    side_copy = lambda: act_copy(2, y, z, 1 - y)
+
+    def act_hand_on():
+        pl.when((z >= c) & (z < p.nz - 1))(lambda: up().start())
+        pl.when((z <= c) & (z > 0))(lambda: down().start())
+        side_copy().start()
+
+    pl.when(z == c)(act_hand_on)
+
+    hi, lo = split(a1_ref[...].T)
+    bm[0], bm[1] = hi, lo
+
+    def backward(j, _):
+        i = lax.rem(d + 1 + j, nd)
+        for t, m in enumerate(shifts(dall[d, i], side, -1)):
+            hi, lo = split(m)
+            colh[t * db : (t + 1) * db] = hi
+            coll[t * db : (t + 1) * db] = lo
+        part[i] = dot(bm[0], colh[...]) + dot(bm[0], coll[...]) + dot(bm[1], colh[...])
+        pl.when(i != d)(lambda: scatter_images(p, part, buf, ss, rs, i).start())
+        return 0
+
+    lax.fori_loop(0, nd, backward, 0)
+
+    def norm_sums(i, carry):
+        val = val_of(i)
+        scaled = (x_ref[i] - center1) * rs1
+        dpre = part[i] * val * slope(scaled * gain1 + shift1)
+        return carry[0] + lanes_sum(dpre), carry[1] + lanes_sum(dpre * scaled)
+
+    zero = jnp.zeros((cb, 1), F32)
+    sh1, gg1 = lax.fori_loop(0, nd, norm_sums, (zero, zero))
+
+    row = lax.broadcasted_iota(jnp.int32, (8, cb), 0)
+    pad = jnp.zeros((1, cb - db), F32)
+    wide = lambda col: jnp.concatenate([to_row(col), pad], axis=1)
+    msg[...] = jnp.where(row == 0, to_row(sh1), jnp.where(row == 1, to_row(gg1), jnp.where(row == 2, wide(sh2), wide(gg2))))
+    copies = [send(msg, rmsg.at[d], sm.at[j], rm.at[d], (lax.rem(d + j, nd), c)) for j in range(1, nd)]
+    for cp in copies:
+        cp.start()
+
+    pl.when(z != c)(lambda: (act_copy(0, y, z, 1 - y).wait_recv(), act_hand_on()) and None)
+    for s in range(1, p.nz):
+        grads.step(s)
+
+    send(call.at[far], call.at[far], sc_.at[0], rc_.at[far], (d, far)).wait_recv()
+    cot_relay = send(call.at[far], call.at[far], sc_.at[2], rc_.at[far], (d, across))
+    cot_relay.start()
+
+    total = collect_images(p, part, buf, ss, rs)
+    val = val_of(d)
+    pre = (x_ref[d] - center1) * rs1 * gain1 + shift1
+    grad = (gain1 * rs1 * (total * val * slope(pre)) + c_ref[d] * val).T
+    rows = px // nc
+    for j in range(nc):
+        xs[j] = grad[j * rows : (j + 1) * rows]
+    a2a = []
+    for j in range(1, nc):
+        to = lax.rem(c + j, nc)
+        a2a.append(send(xs.at[to], rx.at[c], sx.at[j], rxs.at[c], (d, to)))
+    for cp in a2a:
+        cp.start()
+    rx[c] = xs[c]
+
+    for j in range(1, nd):
+        other = lax.rem(d + j, nd)
+        send(msg, rmsg.at[other], sm.at[0], rm.at[other], (other, c)).wait_recv()
+    rmsg[d] = msg[...]
+    total = rmsg[0]
+    for j in range(1, nd):
+        total = total + rmsg[j]
+    per = cb // db
+    both = jnp.concatenate([rmsg[per * c + j][:, :db] for j in range(per)], axis=1)
+    vec_out[...] = jnp.where(row < 2, total, both)
+
+    def kernel_grad(left_of, right_of, out_hbm):
+        stage[...] = jnp.zeros_like(stage)
+
+        def body(i, _):
+            for t, m in enumerate(shifts(left_of(i), side)):
+                hi, lo = split(m)
+                lefth[t * cb : (t + 1) * cb] = jnp.concatenate([hi, hi, lo], axis=1)
+            for q in range(p.ch // right_of(i, 0).shape[0]):
+                r = right_of(i, q)
+                n = r.shape[0]
+                hi, lo = split(r)
+                right[q * n : (q + 1) * n] = jnp.concatenate([hi, lo, hi], axis=1)
+            stage[...] += dot_nt(lefth[...], right[...])
+            return 0
+
+        lax.fori_loop(0, nd, body, 0)
+        cp = pltpu.make_async_copy(stage, out_hbm, dsem)
+        cp.start()
+        cp.wait()
+
+    def act_one(i):
+        pre = (x_ref[i] - center1) * rs1 * gain1 + shift1
+        return pre * sigmoid(pre) * val_of(i)
+
+    grads.finish()
+    kernel_grad(act_one, lambda i, q: dall[q, i], g1_out)
+
+    act_copy(2, 1 - y, z, 1 - y).wait_recv()
+    side_copy().wait_send()
+    pl.when((z >= c) & (z < p.nz - 1))(lambda: up().wait_send())
+    pl.when((z <= c) & (z > 0))(lambda: down().wait_send())
+    cot_far.wait_send()
+    cot_across.wait_send()
+    cot_relay.wait_send()
+    send(call.at[across], call.at[across], sc_.at[0], rc_.at[across], (d, across)).wait_recv()
+    last = 3 - c - far - across + 3
+    send(call.at[last], call.at[last], sc_.at[0], rc_.at[last], (d, across)).wait_recv()
+    kernel_grad(lambda i: jnp.concatenate([act2[0, i], act2[1, i]], axis=0), lambda i, q: call[q, i], g2_out)
+
+    for j in range(1, nc):
+        a2a[j - 1].wait_send()
+        other = lax.rem(c + j, nc)
+        send(xs.at[other], rx.at[other], sx.at[0], rxs.at[other], (d, other)).wait_recv()
+    for j in range(nc):
+        in_out[:, j * cb : (j + 1) * cb] = rx[j]
+    for cp in copies:
+        cp.wait_send()
+
+
+def perturbed(p, inner, x, cot, a1, par1, par2, flags):
+    out = lambda *s: jax.ShapeDtypeStruct(s, F32)
+    nd, nc, cb, db, px = p.nd, p.nc, p.cb, p.db, p.px
+    rows = px // nc
+    return pl.pallas_call(
+        functools.partial(perturbed_kernel, p),
+        out_shape=(out(rows, p.ch), out(9 * cb, p.ch), out(9 * cb, p.ch), out(8, cb)),
+        in_specs=[pl.BlockSpec(memory_space=VMEM)] * 7,
+        out_specs=(pl.BlockSpec(memory_space=VMEM), pl.BlockSpec(memory_space=pl.ANY), pl.BlockSpec(memory_space=pl.ANY),
+                   pl.BlockSpec(memory_space=VMEM)),
+        scratch_shapes=[
+            VMEM((9 * db, px), BF16), VMEM((9 * db, px), BF16), VMEM((2, cb, 9 * db), BF16),
+            VMEM((nd, cb, px), F32), VMEM((nd, cb, px), F32), VMEM((nd, nd, db, px), F32), VMEM((nc, nd, cb, px), F32),
+            VMEM((p.ny, nd, db, px), F32), VMEM((9 * cb, 3 * px), BF16), VMEM((p.ch, 3 * px), BF16),
+            VMEM((nc, rows, cb), F32), VMEM((nc, rows, cb), F32), VMEM((8, cb), F32), VMEM((nd, 8, cb), F32),
+            DMA((nd,)), DMA((nd,)), DMA((1 + p.ny, p.nz)), DMA((nd,)), DMA((3,)), DMA((nc,)), DMA((3,)), DMA((p.ny,)),
+            DMA((nc,)), DMA((nc,)), DMA((nd,)), DMA((nd,)), DMA, VMEM((9 * cb, p.ch), F32),
+        ],
+        compiler_params=pltpu.CompilerParams(collective_id=4, has_side_effects=True, vmem_limit_bytes=LIMIT),
+    )(inner, x, cot, a1, par1, par2, flags)
+
+
+def fused_on_device(p, image_rows, groups, conv_first, conv_second, gain_first, shift_first, gain_second, shift_second, cotangent):
+    d, c = lax.axis_index("dp"), lax.axis_index("chan")
+    cb, db, px, nc = p.cb, p.db, p.px, p.nc
+    x = image_rows.reshape(px // nc, p.ch)
+    cot = cotangent.reshape(px, cb)
+    pad = jnp.zeros((6, cb), F32)
+    par = jnp.concatenate([gain_second[None], shift_second[None], pad])
+    flag = jnp.broadcast_to(jnp.where(groups == 1, 1.0, 0.0).astype(F32)[:, None], (8, px))
+    xs, cs, a2, pars, flags = gather(p, x, cot, conv_second.reshape(9, cb, p.ch), par, flag)
+    a1 = lax.dynamic_slice_in_dim(conv_first, d * db, db, 3).reshape(9, cb, db).transpose(0, 2, 1).reshape(9 * db, cb)
+    par1 = jnp.pad(jnp.stack([gain_first, shift_first], axis=1), ((0, 0), (0, 126)))
+    sums, stat1 = project(p, True, 1, xs, cs, a1, a2, par1, flags)
+    par1 = jnp.pad(jnp.concatenate([stat1[:, :2], par1[:, :2]], axis=1), ((0, 0), (0, 124)))
+    both = lax.dynamic_slice_in_dim(pars.transpose(1, 0, 2).reshape(8, p.ch)[:2], d * db, db, 1)
+    par2 = jnp.pad(both.T, ((0, 0), (0, 126)))
+    block_out, a1_new, a2_new, par1, par2, norm = ascent(p, sums, xs, cs, a1, a2, par1, par2, flags)
+    (sums,) = project(p, False, 3, xs, cs, a1_new, a2_new, par1, flags)
+    input_grad, g1, g2, vec = perturbed(p, sums, xs, cs, a1_new, par1, par2, flags)
+    return (
+        block_out.reshape(cotangent.shape), input_grad.reshape(image_rows.shape),
+        g1.reshape(conv_first.shape), g2.reshape(conv_second.shape), vec[1], vec[0], vec[3], vec[2], norm[0, 0],
+    )
 
 
 def valid_pixels(groups, extent_full):
@@ -31,7 +792,7 @@
     return sigmoid * (1.0 + preact * (1.0 - sigmoid))
 
 
-def moments(values, validity):
+def batch_moments(values, validity):
     summed, squares, pixels = lax.psum(
         (
             jnp.sum(values * validity, axis=(0, 1, 2)),
@@ -45,7 +806,7 @@
     return (center, lax.rsqrt(spread + epsilon), pixels)
 
 
-def project(values, kernel):
+def project_over_chan(values, kernel):
     return lax.psum_scatter(convolve(values, kernel), "chan", scatter_dimension=3, tiled=True)
 
 
@@ -66,7 +827,7 @@
     return lax.psum((jnp.sum(dpre, axis=(0, 1, 2)), jnp.sum(dpre * scaled, axis=(0, 1, 2))), "dp")
 
 
-def on_device(
+def plain_on_device(
     image_rows,
     groups,
     conv_first,
@@ -80,16 +841,16 @@
     inputs = lax.all_to_all(image_rows, "chan", split_axis=3, concat_axis=1, tiled=True)
     validity = valid_pixels(groups, inputs.shape[1])
     cot_valid = cotangent * validity
-    center_one, rscale_one, pixels = moments(inputs, validity)
+    center_one, rscale_one, pixels = batch_moments(inputs, validity)
     scaled_one = (inputs - center_one) * rscale_one
     pre_one = scaled_one * gain_first + shift_first
     act_one = jax.nn.silu(pre_one) * validity
-    inner = project(act_one, conv_first) * validity
-    center_two, rscale_two, pixels_again = moments(inner, validity)
+    inner = project_over_chan(act_one, conv_first) * validity
+    center_two, rscale_two, pixels_again = batch_moments(inner, validity)
     scaled_two = (inner - center_two) * rscale_two
     pre_two = scaled_two * gain_second + shift_second
     act_two = jax.nn.silu(pre_two) * validity
-    block_out = inputs * validity + project(act_two, conv_second) * validity
+    block_out = inputs * validity + project_over_chan(act_two, conv_second) * validity
     dact_two, kernel_two_part = conv_backward(cot_valid, act_two, conv_second)
     dpre_two = dact_two * validity * silu_slope(pre_two)
     shift_two_grad, gain_two_grad = batch_sums(dpre_two, scaled_two)
@@ -120,7 +881,7 @@
     moved_shift_two = shift_second + factor * shift_two_grad
     pre_one_new = scaled_one * moved_gain_one + moved_shift_one
     act_one_new = jax.nn.silu(pre_one_new) * validity
-    inner_new = project(act_one_new, kernel_one) * validity
+    inner_new = project_over_chan(act_one_new, kernel_one) * validity
     scaled_two_new = (inner_new - center_two) * rscale_two
     pre_two_new = scaled_two_new * moved_gain_two + moved_shift_two
     act_two_new = jax.nn.silu(pre_two_new) * validity
@@ -167,6 +928,15 @@
 
 
 def solution(mesh):
+    nd, nc = mesh.shape["dp"], mesh.shape["chan"]
+
+    def on_device(image_rows, *rest):
+        images, side, channels = image_rows.shape[0], image_rows.shape[2], image_rows.shape[3]
+        fits = images == 1 and nc == 4 and nd == 2 * nc and channels // nd % 16 == 0 and side * side % 128 == 0
+        if not fits:
+            return plain_on_device(image_rows, *rest)
+        return fused_on_device(Plan(nd, nc, channels, side), image_rows, *rest)
+
     return jax.shard_map(
         on_device,
         mesh=mesh,

time: 1250 us -> 341 us (0.27)
  the two profiles are of different devices: /device:TPU:0 before, /device:TPU:3 now
where the time goes in v1:
time: 341 us; the launch traced here: 340 us
  Pallas kernels  317 us (93%)
  local copies, waits for them, and re-layouts  18.5 us (5%)
  other arithmetic  3.7 us (1%)
    pallas_call x1, Pallas kernels, perturbed(): pl.pallas_call(functools.partial(perturbed_kernel, p), out_shape=(out(row...  162 us
    pallas_call x2, Pallas kernels, project(): pl.pallas_call(functools.partial(project_kernel, p, take_stats), out_shap...  63.6 us
    pallas_call x1, Pallas kernels, ascent(): pl.pallas_call(functools.partial(ascent_kernel, p), out_shape=(out(px, cb...  45.7 us
    pallas_call x1, Pallas kernels, gather(): pl.pallas_call(functools.partial(gather_kernel, p), out_shape=(out(p.nd,...  45.5 us
    unnamed x8, local copies, waits for them, and re-layouts  8.42 us

profile of v1, /device:TPU:3, one launch (start us, length us, event | category | flops | bytes accessed | tf_op | source)
XLA Modules:
  0.0 340.1 jit_solution(335735814167916957)
XLA Ops:
  1.3 0.1 pad.22.clone
  1.4 0.7 pad_maximum_fusion
  2.1 1.4 maximum_maximum_fusion.par_ref
  3.4 0.6 broadcast_in_dim.25.flag_ref
  4.0 0.1 copy.31
  4.2 0.7 pad.12.par_ref
  4.8 0.8 copy.32
  5.6 0.8 copy.33
  6.4 1.6 constant_dynamic-slice_fusion
  8.0 1.2 copy.30
  9.3 45.5 %shard_map.160 = (f32[8,160,256]{2,1,0:T(8,128)}, f32[8,160,256]{2,1,0:T(8,128)}, f32[720,160]{1,0:T(8,128)}, f32[4,8,160]{2,1,0:T(8,128)}, f32[8,8,256]{2,1,0:T(8,128)}) custom-call(f32[64,640]{1,0:T(8,128)} %bitcast.35, f32[256,160]{1,0:T(8,128)} %bitcast.33, f32[9,160,640]{2,1,0:T(8,128)} %bitcast.30, f32[8,160]{1,0:T(8,128)} %maximum_maximum_fusion.par_ref, ...), custom_call_target="tpu_custom_call" | custom-call | tf_op jit(solution)/shard_map/pallas_call | solution.py:276
  54.7 0.8 slice.33
  55.5 0.2 copy.34
  55.7 0.6 pad.14.par2_ref
  56.3 33.0 %shard_map.161 = (f32[16,80,256]{2,1,0:T(8,128)}, f32[160,128]{1,0:T(8,128)}) custom-call(f32[8,160,256]{2,1,0:T(8,128)} %get-tuple-element.26.x_ref, f32[8,160,256]{2,1,0:T(8,128)} %get-tuple-element.27.c_ref, f32[720,160]{1,0:T(8,128)} %bitcast.26, f32[720,160]{1,0:T(8,128)} %get-tuple-element.28.a2_ref, f32[160,128]{1,0:T(8,128)} %pad.12.par_ref, ...), custom_call_target="tpu_custom_call" | custom-call | tf_op jit(solution)/shard_map/pallas_call | solution.py:389
  89.3 1.6 select_maximum_fusion.par1_ref
  90.9 45.7 %shard_map.162 = (f32[256,160]{1,0:T(8,128)}, f32[720,160]{1,0:T(8,128)}, f32[720,160]{1,0:T(8,128)}, f32[160,128]{1,0:T(8,128)}, f32[80,128]{1,0:T(8,128)}, /*index=5*/f32[8,128]{1,0:T(8,128)}) custom-call(f32[16,80,256]{2,1,0:T(8,128)} %get-tuple-element.30.inner_ref, f32[8,160,256]{2,1,0:T(8,128)} %get-tuple-element.26.x_ref, ...), custom_call_target="tpu_custom_call" | custom-call | tf_op jit(solution)/shard_map/pallas_call | solution.py:536
  136.7 1.2 slice.32
  137.9 30.6 %shard_map.163.inner_ref = f32[16,80,256]{2,1,0:T(8,128)} custom-call(f32[8,160,256]{2,1,0:T(8,128)} %get-tuple-element.26.x_ref, f32[8,160,256]{2,1,0:T(8,128)} %get-tuple-element.27.c_ref, f32[720,160]{1,0:T(8,128)} %get-tuple-element.34.a1_ref, f32[720,160]{1,0:T(8,128)} %get-tuple-element.35.a2_ref, f32[160,128]{1,0:T(8,128)} %get-tuple-element.36.par_ref.par1_ref, ...), custom_call_target="tpu_custom_call" | custom-call | tf_op jit(solution)/shard_map/pallas_call | solution.py:389
  168.5 0.0 copy-start.1
  168.5 161.7 %shard_map.164 = (f32[64,640]{1,0:T(8,128)}, f32[1440,640]{1,0:T(8,128)}, f32[1440,640]{1,0:T(8,128)}, f32[8,160]{1,0:T(8,128)}) custom-call(f32[16,80,256]{2,1,0:T(8,128)} %shard_map.163.inner_ref, f32[8,160,256]{2,1,0:T(8,128)} %get-tuple-element.26.x_ref, f32[8,160,256]{2,1,0:T(8,128)} %get-tuple-element.27.c_ref, f32[720,160]{1,0:T(8,128)} %get-tuple-element.34.a1_ref, ...), custom_call_target="tpu_custom_call" | custom-call | tf_op jit(solution)/shard_map/pallas_call | solution.py:730
  330.2 1.4 fusion
  331.7 0.0 copy-done.1
  331.7 0.7 copy.40
  332.4 1.6 copy.41
  334.0 0.0 copy-start
  334.0 4.3 %copy.42 = f32[3,3,160,640]{3,2,1,0:T(8,128)} copy(f32[3,3,160,640]{3,2,1,0:T(8,128)} %bitcast.29) | data formatting | bytes 7372800
  338.2 0.0 copy-done
  338.2 1.8 copy.43
  (2 shorter events, 0.0 us)
Async XLA Ops:
  168.5 163.2 %copy-start.1 = (f32[256,160]{1,0:T(8,128)S(1)}, f32[256,160]{1,0:T(8,128)}, u32[]{:S(2)}) copy-start(f32[256,160]{1,0:T(8,128)} %get-tuple-element.33) | copy-start | bytes 491524
  334.0 4.3 %copy-start = (f32[1440,640]{1,0:T(8,128)S(1)}, f32[1440,640]{1,0:T(8,128)}, u32[]{:S(2)}) copy-start(f32[1440,640]{1,0:T(8,128)} %get-tuple-element.40) | copy-start | bytes 11059204

commit v2 on v0

--- a/solution.py
+++ b/solution.py
@@ -1,11 +1,834 @@
+import functools
+import types
+
 import jax
 import jax.numpy as jnp
 from jax import lax
+from jax.experimental import pallas as pl
+from jax.experimental.pallas import tpu as pltpu
 from jax.sharding import PartitionSpec as P
 
 epsilon = 1e-05
 sam_radius = 0.05
 norm_floor = 1e-06
+MESH = pl.DeviceIdType.MESH
+F32, BF16 = jnp.float32, jnp.bfloat16
+VMEM, SMEM = pltpu.VMEM, pltpu.SMEM
+DMA = pltpu.SemaphoreType.DMA
+LIMIT = 60 << 20
+
+
+class Plan:
+    def __init__(self, nd, nc, channels, side):
+        self.nd, self.nc, self.ch, self.side = nd, nc, channels, side
+        self.cb, self.db, self.px = channels // nc, channels // nd, side * side
+        self.ny = 2
+        self.nz = nd // 2
+
+
+def split(v):
+    hi = v.astype(BF16)
+    return hi, (v - hi.astype(F32)).astype(BF16)
+
+
+def dot(a, b):
+    return lax.dot_general(a, b, (((1,), (0,)), ((), ())), preferred_element_type=F32)
+
+
+def dot_nt(a, b):
+    return lax.dot_general(a, b, (((1,), (1,)), ((), ())), preferred_element_type=F32)
+
+
+def edge_masks(side, px):
+    lane = lax.broadcasted_iota(jnp.int32, (1, px), 1)
+    col = lax.rem(lane, side)
+    row = lax.div(lane, side)
+    one = jnp.ones((1, px), F32)
+    zero = jnp.zeros((1, px), F32)
+    rows = {-1: jnp.where(row >= 1, one, zero), 0: None, 1: jnp.where(row < side - 1, one, zero)}
+    cols = {-1: jnp.where(col >= 1, one, zero), 0: None, 1: jnp.where(col < side - 1, one, zero)}
+    return rows, cols
+
+
+def moved(v, lanes, mask):
+    if lanes:
+        v = pltpu.roll(v, (-lanes) % v.shape[1], axis=1)
+    return v if mask is None else v * mask
+
+
+def shifts(v, side, sign=1):
+    rows, cols = edge_masks(side, v.shape[1])
+    by_col = {s: moved(v, s, cols[s]) for s in (-1, 0, 1)}
+    return [moved(by_col[sign * s], sign * r * side, rows[sign * r]) for r in (-1, 0, 1) for s in (-1, 0, 1)]
+
+
+def gather_taps(prod, side, n):
+    rows, cols = edge_masks(side, prod.shape[1])
+    total = None
+    for j, s in enumerate((-1, 0, 1)):
+        part = None
+        for i, r in enumerate((-1, 0, 1)):
+            t = 3 * i + j
+            m = moved(prod[t * n : (t + 1) * n], r * side, rows[r])
+            part = m if part is None else part + m
+        m = moved(part, s, cols[s])
+        total = m if total is None else total + m
+    return total
+
+
+def sigmoid(t):
+    return 1.0 / (1.0 + jnp.exp(-t))
+
+
+def silu_and_slope(pre):
+    s = sigmoid(pre)
+    return pre * s, s * (1.0 + pre * (1.0 - s))
+
+
+def lanes_sum(v):
+    return jnp.sum(v, axis=1, keepdims=True)
+
+
+def valid_map(flag, side, px):
+    lane = lax.broadcasted_iota(jnp.int32, (1, px), 1)
+    half = (lax.rem(lane, side) < side // 2) & (lax.div(lane, side) < side // 2)
+    return jnp.where(half, jnp.ones((1, px), F32), flag)
+
+
+def diagonal(n):
+    return lax.broadcasted_iota(jnp.int32, (n, n), 0) == lax.broadcasted_iota(jnp.int32, (n, n), 1)
+
+
+def to_row(col):
+    return jnp.sum(jnp.where(diagonal(col.shape[0]), col, 0.0), axis=0, keepdims=True)
+
+
+def to_col(row):
+    return jnp.sum(jnp.where(diagonal(row.shape[1]), row, 0.0), axis=1, keepdims=True)
+
+
+def stacked(rows, n):
+    at = lax.broadcasted_iota(jnp.int32, (8, n), 0)
+    out = jnp.zeros((8, n), F32)
+    for k, row in enumerate(rows):
+        out = jnp.where(at == k, row, out)
+    return out
+
+
+def send(src, dst, ss, rs, device):
+    return pltpu.make_async_remote_copy(
+        src_ref=src, dst_ref=dst, send_sem=ss, recv_sem=rs, device_id=device, device_id_type=MESH
+    )
+
+
+def here():
+    return lax.axis_index("dp"), lax.axis_index("chan")
+
+
+def greet(p):
+    d, c = here()
+    barrier = pltpu.get_barrier_semaphore()
+    for j in range(1, p.nd):
+        pl.semaphore_signal(barrier, inc=1, device_id=(lax.rem(d + j, p.nd), c), device_id_type=MESH)
+    for j in range(1, p.nc):
+        pl.semaphore_signal(barrier, inc=1, device_id=(d, lax.rem(c + j, p.nc)), device_id_type=MESH)
+    pl.semaphore_wait(barrier, p.nd - 1 + p.nc - 1)
+
+
+class ToAll:
+    def __init__(self, axis, n, tile, slots, ss, rs):
+        d, c = here()
+        self.n, self.tile, self.slots, self.ss, self.rs = n, tile, slots, ss, rs
+        self.me = d if axis == "dp" else c
+        self.device = (lambda o: (o, c)) if axis == "dp" else (lambda o: (d, o))
+
+    def start(self):
+        self.slots[self.me] = self.tile[...]
+        for j in range(1, self.n):
+            to = lax.rem(self.me + j, self.n)
+            send(self.tile, self.slots.at[self.me], self.ss.at[j], self.rs.at[self.me], self.device(to)).start()
+
+    def finish(self):
+        for j in range(1, self.n):
+            other = lax.rem(self.me + j, self.n)
+            send(self.tile, self.slots.at[other], self.ss.at[j], self.rs.at[other], self.device(other)).wait()
+
+    def total(self):
+        total = self.slots[0]
+        for j in range(1, self.n):
+            total = total + self.slots[j]
+        return total
+
+
+class Line:
+    def __init__(self, p, view, ss, rs):
+        self.p, self.view, self.ss, self.rs = p, view, ss, rs
+        d, self.c = here()
+        self.z, self.y = lax.div(d, p.ny), lax.rem(d, p.ny)
+
+    def copy(self, zs, sem, z_to, y_to):
+        slot = zs * self.p.ny + self.y
+        return send(self.view(slot), self.view(slot), self.ss.at[sem, zs], self.rs.at[slot], (z_to * self.p.ny + y_to, self.c))
+
+    def up(self, zs):
+        return self.copy(zs, 0, lax.min(self.z + 1, self.p.nz - 1), self.y)
+
+    def down(self, zs):
+        return self.copy(zs, 1, lax.max(self.z - 1, 0), self.y)
+
+    def side(self, zs):
+        return self.copy(zs, 2, self.z, 1 - self.y)
+
+    def got(self, zs, y):
+        slot = zs * self.p.ny + y
+        send(self.view(slot), self.view(slot), self.ss.at[0, 0], self.rs.at[slot], (self.z * self.p.ny + 1 - self.y, self.c)).wait_recv()
+
+    def hand_on(self, zs):
+        pl.when((zs <= self.z) & (self.z < self.p.nz - 1))(lambda: self.up(zs).start())
+        pl.when((zs >= self.z) & (self.z > 0))(lambda: self.down(zs).start())
+        self.side(zs).start()
+
+    def drain(self):
+        for zs in range(self.p.nz):
+            pl.when((zs <= self.z) & (self.z < self.p.nz - 1))(lambda: self.up(zs).wait_send())
+            pl.when((zs >= self.z) & (self.z > 0))(lambda: self.down(zs).wait_send())
+            self.side(zs).wait_send()
+
+
+def nearest(z, k):
+    t = lax.div(z, 2)
+    low = z + t * (3 - 2 * z)
+    first = 1 - lax.min(lax.div(k, 2), 1)
+    place = k + low * first * (1 - 2 * k)
+    return place * (1 - 2 * t) + 3 * t
+
+
+class ChanSum:
+    def __init__(self, p, r):
+        self.p, self.r = p, r
+        d, c = here()
+        k = lax.rem(c, 2)
+        self.hb = p.db // 2
+        self.across, self.far = (d, c + 1 - 2 * k), (d, lax.rem(c + 2, 4))
+        self.mine = pl.multiple_of(k * self.hb, 8)
+        self.yours = pl.multiple_of((1 - k) * self.hb, 8)
+
+    def first(self, i):
+        r = self.r
+        return send(r.part.at[i], r.near.at[i], r.cs1.at[i], r.cr1.at[i], self.across)
+
+    def second(self, i):
+        r = self.r
+        return send(r.half.at[i], r.away.at[i], r.cs2.at[i], r.cr2.at[i], self.far)
+
+    def third(self, i, rows):
+        r = self.r
+        mine = r.sums.at[i, pl.ds(self.mine, self.hb)]
+        return send(mine, r.sums.at[i, pl.ds(rows, self.hb)], r.cs3.at[i], r.cr3.at[i], self.across)
+
+    def chip(self, i):
+        r = self.r
+        self.first(i).wait()
+        r.half[i] = r.part[i, pl.ds(self.mine, self.hb)] + r.near[i, pl.ds(self.mine, self.hb)]
+        self.second(i).start()
+
+    def cross(self, i):
+        r = self.r
+        self.second(i).wait()
+        r.sums[i, pl.ds(self.mine, self.hb)] = r.half[i] + r.away[i]
+        self.third(i, self.mine).start()
+
+    def done(self, i):
+        self.third(i, self.yours).wait()
+
+    def advance(self, j, n, item):
+        at = lambda m: item(lax.clamp(0, m, n - 1))
+        pl.when((j >= 1) & (j < n + 1))(lambda: self.chip(at(j - 1)))
+        pl.when((j >= 3) & (j < n + 3))(lambda: self.cross(at(j - 3)))
+        pl.when((j >= 4) & (j < n + 4))(lambda: self.done(at(j - 4)))
+
+
+class ImageSum:
+    def __init__(self, p, part, near, acc, away, s1, r1, s2, r2):
+        self.p, self.part, self.buf1, self.acc, self.buf2 = p, part, near, acc, away
+        self.s1, self.r1, self.s2, self.r2 = s1, r1, s2, r2
+        d, self.c = here()
+        self.z, self.y = lax.div(d, p.ny), lax.rem(d, p.ny)
+
+    def near(self, zs):
+        side = 1 - self.y
+        return send(self.part.at[zs * self.p.ny + side], self.buf1.at[zs], self.s1.at[zs], self.r1.at[zs],
+                    (self.z * self.p.ny + side, self.c))
+
+    def away(self, zs, slot):
+        return send(self.acc.at[zs], self.buf2.at[slot], self.s2.at[zs], self.r2.at[slot], (zs * self.p.ny + self.y, self.c))
+
+    def spread(self):
+        for j in range(1, self.p.nz + 1):
+            zs = lax.rem(self.z + j, self.p.nz)
+            self.near(zs).wait()
+            self.acc[zs] = self.part[zs * self.p.ny + self.y] + self.buf1[zs]
+            if j < self.p.nz:
+                self.away(zs, self.z).start()
+
+    def total(self):
+        total = self.acc[self.z]
+        for j in range(1, self.p.nz):
+            other = lax.rem(self.z + j, self.p.nz)
+            self.away(other, other).wait()
+            total = total + self.buf2[other]
+        return total
+
+
+def scratch_of(p):
+    nd, nc, cb, db, px, nz, ny = p.nd, p.nc, p.cb, p.db, p.px, p.nz, p.ny
+    rows = px // nc
+    f = lambda *s: VMEM(s, F32)
+    h = lambda *s: VMEM(s, BF16)
+    return dict(
+        k1w=f(9, cb, 256), k2w=f(9, db, p.ch), ks=f(nc, cb, 9 * db), b2=f(cb, 9 * db),
+        a1=f(9 * db, cb), a2=f(9 * db, cb), g1=f(9 * db, cb), g2=f(9 * db, cb),
+        a_cat=h(2, 9 * db, 3 * cb), bm=h(2, cb, 9 * db), b2m=h(2, cb, 9 * db), colh=h(9 * db, px), coll=h(9 * db, px),
+        xs=f(nc, rows, cb), rx=f(nc, rows, cb), xin=f(nd, cb, px), act1=f(nd, cb, px), slope1=f(nd, cb, px),
+        call=f(nc, nd, cb, px),
+        part=f(2 * nd, db, px), near=f(2 * nd, db, px), half=f(2 * nd, db // 2, px), away=f(2 * nd, db // 2, px),
+        sums=f(2 * nd, db, px), slope2=f(nd, db, px), dpre=f(nd, db, px),
+        outp=f(nd, cb, px), outn=f(nz, cb, px), outc=f(nz, cb, px), outw=f(nz, cb, px),
+        inp=f(nd, cb, px), inn=f(nz, cb, px), inc=f(nz, cb, px), inw=f(nz, cb, px),
+        dall=f(nd, nd, db, px), act2=f(ny, nd, db, px), left=h(9 * cb, 6 * px), right=h(p.ch, 6 * px),
+        stage=f(9 * cb, p.ch),
+        par=f(8, cb), pars=f(nc, 8, cb), stat=f(8, cb), stats=f(nd, 8, cb), msg=f(8, cb), msgs=f(nd, 8, cb),
+        sq=f(8, 128), sqs=f(nc, 8, 128), vec=f(8, cb), vecs=f(nd, 8, cb),
+        k1_sem=DMA, k2_sem=DMA, g1_sem=DMA, g2_sem=DMA,
+        xs_s=DMA((nc,)), xs_r=DMA((nc,)), ks_s=DMA((nc,)), ks_r=DMA,
+        par_s=DMA((nc,)), par_r=DMA((nc,)), stat_s=DMA((nd,)), stat_r=DMA((nd,)), msg_s=DMA((nd,)), msg_r=DMA((nd,)),
+        sq_s=DMA((nc,)), sq_r=DMA((nc,)), vec_s=DMA((nd,)), vec_r=DMA((nd,)),
+        x_s=DMA((3, nz)), x_r=DMA((nd,)), c_s=DMA((3, nz)), c_r=DMA((nd,)), d_s=DMA((3, nz)), d_r=DMA((nd,)),
+        cs1=DMA((2 * nd,)), cr1=DMA((2 * nd,)), cs2=DMA((2 * nd,)), cr2=DMA((2 * nd,)), cs3=DMA((2 * nd,)), cr3=DMA((2 * nd,)),
+        o_s1=DMA((nz,)), o_r1=DMA((nz,)), o_s2=DMA((nz,)), o_r2=DMA((nz,)),
+        i_s1=DMA((nz,)), i_r1=DMA((nz,)), i_s2=DMA((nz,)), i_r2=DMA((nz,)),
+        call_s=DMA((3, nd)), call_r=DMA((nc, nd)), act_s=DMA((3, nd)), act_r=DMA((ny, nd)),
+        far_s=DMA((nd,)), far_r=DMA((nd,)), core_s=DMA((2, nd)), core_r=DMA((2, nd)), in_s=DMA((nc,)), in_r=DMA((nc,)),
+    )
+
+
+ARGS = ("x", "cot", "k1", "k2", "gain1", "shift1", "gain2", "shift2", "groups")
+OUTS = ("block_out", "input_grad", "g1_out", "g2_out", "gg1", "sh1", "gg2", "sh2", "norm")
+
+
+def step_kernel(p, names, *refs):
+    r = types.SimpleNamespace(**dict(zip(names, refs)))
+    cb, db, px, side, nd, nc, nz, ny = p.cb, p.db, p.px, p.side, p.nd, p.nc, p.nz, p.ny
+    d, c = here()
+    z, y = lax.div(d, ny), lax.rem(d, ny)
+    k = lax.rem(c, 2)
+    far, across = lax.rem(c + 2, 4), c + 1 - 2 * k
+    last = 6 - c - far - across
+    rows = px // nc
+    owner = lax.div(d * db, cb)
+    image = lambda j: nearest(z, lax.div(j, 2)) * ny + y + lax.rem(j, 2) * (1 - 2 * y)
+
+    base = lax.min(lax.div(d * db, 128), (p.ch - 256) // 128) * 128
+    k1_copy = pltpu.make_async_copy(r.k1.at[:, :, pl.ds(pl.multiple_of(base, 128), 256)], r.k1w, r.k1_sem)
+    k1_copy.start()
+    k2_rows = pl.ds(pl.multiple_of(d * db - owner * cb, 8), db)
+    k2_copy = pltpu.make_async_copy(r.k2.at[:, k2_rows], r.k2w, r.k2_sem)
+    pl.when(c == owner)(lambda: k2_copy.start())
+    greet(p)
+
+    for j in range(nc):
+        r.xs[j] = r.x[:, j * cb : (j + 1) * cb]
+    a2a = lambda j: send(r.xs.at[lax.rem(c + j, nc)], r.rx.at[c], r.xs_s.at[j], r.xs_r.at[c], (d, lax.rem(c + j, nc)))
+    for j in range(1, nc):
+        a2a(j).start()
+    r.rx[c] = r.xs[c]
+    r.par[...] = stacked([r.gain2[...].reshape(1, cb), r.shift2[...].reshape(1, cb)], cb)
+    params = ToAll("chan", nc, r.par, r.pars, r.par_s, r.par_r)
+    params.start()
+    flag = jnp.full((1, 1), jnp.where(r.groups[0] == 1, 1.0, 0.0), F32)
+    mine = valid_map(flag, side, px)
+    r.call[c, d] = r.cot[...].T * mine
+
+    @pl.when(c == owner)
+    def _():
+        k2_copy.wait()
+        for j in range(nc):
+            r.ks[j] = r.k2w[:, :, j * cb : (j + 1) * cb].reshape(9 * db, cb).T
+
+    for j in range(1, nc):
+        a2a(j).wait_send()
+        other = lax.rem(c + j, nc)
+        send(r.xs.at[other], r.rx.at[other], r.xs_s.at[j], r.xs_r.at[other], (d, other)).wait_recv()
+    r.xin[d] = r.rx[...].reshape(px, cb).T
+    ins = Line(p, lambda s: r.xin.at[s], r.x_s, r.x_r)
+    ins.hand_on(z)
+
+    count = lanes_sum(mine)
+    total = lanes_sum(r.xin[d] * mine)
+    off = r.xin[d] - total / count
+    r.stat[...] = stacked([to_row(total), to_row(lanes_sum(mine * off * off)), jnp.broadcast_to(flag, (1, cb))], cb)
+    stats = ToAll("dp", nd, r.stat, r.stats, r.stat_s, r.stat_r)
+    stats.start()
+
+    piece = lambda j: send(r.ks.at[lax.rem(c + j, nc)], r.b2, r.ks_s.at[j], r.ks_r, (d, lax.rem(c + j, nc)))
+
+    @pl.when(c == owner)
+    def _():
+        for j in range(1, nc):
+            piece(j).start()
+
+    k1_copy.wait()
+    turn = lax.rem(256 - (d * db - base), 256)
+    b1 = jnp.concatenate([pltpu.roll(r.k1w[t], turn, axis=1)[:, :db] for t in range(9)], axis=1)
+    hi, lo = split(b1)
+    r.bm[0], r.bm[1] = hi, lo
+    r.a1[...] = b1.T
+    hi, lo = split(r.a1[...])
+    r.a_cat[0] = jnp.concatenate([hi, hi, lo], axis=1)
+
+    stats.finish()
+
+    def val_of(i):
+        return valid_map(r.stats[i, 2:3, 0:1], side, px)
+
+    counts = [jnp.sum(val_of(i), keepdims=True) for i in range(nd)]
+    pixels = functools.reduce(jnp.add, counts)
+    center = functools.reduce(jnp.add, [r.stats[i, 0:1] for i in range(nd)]) / pixels
+    spread = [r.stats[i, 1:2] + counts[i] * (r.stats[i, 0:1] / counts[i] - center) ** 2 for i in range(nd)]
+    center1, rs1 = to_col(center), to_col(lax.rsqrt(functools.reduce(jnp.add, spread) / pixels + epsilon))
+    gain1, shift1 = to_col(r.gain1[...].reshape(1, cb)), to_col(r.shift1[...].reshape(1, cb))
+
+    chan = ChanSum(p, r)
+
+    def first_map(i, gain, shift):
+        val = val_of(i)
+        act, slope = silu_and_slope((r.xin[i] - center1) * rs1 * gain + shift)
+        act = act * val
+        r.act1[i], r.slope1[i] = act, slope * val
+        ah, al = split(act)
+        prod = dot(r.a_cat[0], jnp.concatenate([ah, al, ah], axis=0))
+        r.part[i] = gather_taps(prod, side, db) * val
+        chan.first(i).start()
+
+    def second_back(i):
+        ch, cl = split(r.call[c, i])
+        prod = dot(r.a_cat[1], jnp.concatenate([ch, cl, ch], axis=0))
+        r.part[nd + i] = gather_taps(prod, side, db) * val_of(i)
+        chan.first(nd + i).start()
+
+    def forward(kk, _):
+        zs = nearest(z, kk)
+
+        @pl.when(kk > 0)
+        def _():
+            ins.got(zs, y)
+            ins.hand_on(zs)
+
+        first_map(zs * ny + y, gain1, shift1)
+        chan.advance(2 * kk, nd, image)
+        ins.got(zs, 1 - y)
+        first_map(zs * ny + 1 - y, gain1, shift1)
+        chan.advance(2 * kk + 1, nd, image)
+        return 0
+
+    lax.fori_loop(0, nz, forward, 0)
+    cots = Line(p, lambda s: r.call.at[c, s], r.c_s, r.c_r)
+    cots.hand_on(z)
+
+    @pl.when(c == owner)
+    def _():
+        r.b2[...] = r.ks[c]
+
+    @pl.when(c != owner)
+    def _():
+        send(r.ks.at[0], r.b2, r.ks_s.at[0], r.ks_r, (d, owner)).wait_recv()
+
+    def set_back(a2):
+        for t in range(9):
+            hi, lo = split(a2[(8 - t) * db : (9 - t) * db])
+            r.a_cat[1, t * db : (t + 1) * db] = jnp.concatenate([hi, hi, lo], axis=1)
+
+    r.a2[...] = r.b2[...].T
+    set_back(r.a2)
+
+    def flush(j, _):
+        chan.advance(j, nd, image)
+        return 0
+
+    lax.fori_loop(nd, nd + 4, flush, 0)
+
+    params.finish()
+    both = [r.pars[owner, j : j + 1] for j in range(2)]
+    low = lax.rem(d * db, cb) == 0
+    gain2, shift2 = (to_col(jnp.where(low, v[:, :db], v[:, cb - db :])) for v in both)
+
+    def add_up(i, carry):
+        return carry + lanes_sum(r.sums[i] * val_of(i))
+
+    center2 = lax.fori_loop(0, nd, add_up, jnp.zeros((db, 1), F32)) / pixels
+
+    def add_squares(i, carry):
+        off = r.sums[i] - center2
+        return carry + lanes_sum(val_of(i) * off * off)
+
+    rs2 = lax.rsqrt(lax.fori_loop(0, nd, add_squares, jnp.zeros((db, 1), F32)) / pixels + epsilon)
+
+    outs = ImageSum(p, r.outp, r.outn, r.outc, r.outw, r.o_s1, r.o_r1, r.o_s2, r.o_r2)
+    b2h, b2l = split(r.b2[...])
+
+    def set_cols(maps):
+        for t, m in enumerate(maps):
+            hi, lo = split(m)
+            r.colh[t * db : (t + 1) * db] = hi
+            r.coll[t * db : (t + 1) * db] = lo
+
+    def im2col_dot(which):
+        return dot(which[0], r.colh[...]) + dot(which[0], r.coll[...]) + dot(which[1], r.colh[...])
+
+    def wgrad(other):
+        oh, ol = split(other)
+        left = jnp.concatenate([r.colh[...], r.colh[...], r.coll[...]], axis=1)
+        return dot_nt(left, jnp.concatenate([oh, ol, oh], axis=1))
+
+    call_copy = lambda which, sem, i, to: send(
+        r.call.at[which, i], r.call.at[which, i], r.call_s.at[sem, i], r.call_r.at[which, i], (d, to)
+    )
+    r.g2[...] = jnp.zeros_like(r.g2)
+
+    def second_map(i):
+        val = val_of(i)
+        act, slope = silu_and_slope((r.sums[i] - center2) * rs2 * gain2 + shift2)
+        r.slope2[i] = slope * val
+        set_cols(shifts(act * val, side))
+        r.outp[i] = im2col_dot((r.b2m[0], r.b2m[1]))
+        r.g2[...] += wgrad(r.call[c, i])
+
+    def back_item(j):
+        return nd + image(j)
+
+    def cotangent(kk, _):
+        zs = nearest(z, kk)
+
+        @pl.when(kk > 0)
+        def _():
+            cots.got(zs, y)
+            cots.hand_on(zs)
+
+        i = zs * ny + y
+        second_back(i)
+        call_copy(c, 0, i, far).start()
+        call_copy(c, 1, i, across).start()
+        chan.advance(2 * kk, nd, back_item)
+        second_map(i)
+        cots.got(zs, 1 - y)
+        i = zs * ny + 1 - y
+        second_back(i)
+        call_copy(c, 0, i, far).start()
+        call_copy(c, 1, i, across).start()
+        chan.advance(2 * kk + 1, nd, back_item)
+        second_map(i)
+        outs.near(zs).start()
+        return 0
+
+    r.b2m[0], r.b2m[1] = b2h, b2l
+    lax.fori_loop(0, nz, cotangent, 0)
+
+    def flush_back(j, _):
+        chan.advance(j, nd, back_item)
+        return 0
+
+    lax.fori_loop(nd, nd + 4, flush_back, 0)
+    outs.spread()
+
+    def inner_sums(i, carry):
+        dpre = r.sums[nd + i] * r.slope2[i]
+        r.dpre[i] = dpre
+        scaled = (r.sums[i] - center2) * rs2
+        return carry[0] + lanes_sum(dpre), carry[1] + lanes_sum(dpre * scaled)
+
+    zero = jnp.zeros((db, 1), F32)
+    sh2, gg2 = lax.fori_loop(0, nd, inner_sums, (zero, zero))
+    r.g1[...] = jnp.zeros_like(r.g1)
+
+    def backward(i, carry):
+        scaled = (r.sums[i] - center2) * rs2
+        dinner = gain2 * rs2 * (r.dpre[i] - val_of(i) * (sh2 + scaled * gg2) / pixels)
+        set_cols(shifts(dinner, side, -1))
+        r.g1[...] += wgrad(r.act1[i])
+        dpre1 = im2col_dot((r.bm[0], r.bm[1])) * r.slope1[i]
+        scaled1 = (r.xin[i] - center1) * rs1
+        return carry[0] + lanes_sum(dpre1), carry[1] + lanes_sum(dpre1 * scaled1)
+
+    zero = jnp.zeros((cb, 1), F32)
+    sh1, gg1 = lax.fori_loop(0, nd, backward, (zero, zero))
+
+    square = jnp.sum(r.g1[...] * r.g1[...] + r.g2[...] * r.g2[...], keepdims=True)
+    square = square + jnp.where(c == 0, jnp.sum(sh2 * sh2 + gg2 * gg2, keepdims=True), 0.0)
+    r.msg[...] = stacked([to_row(sh1), to_row(gg1), jnp.broadcast_to(square, (1, cb))], cb)
+    over_dp = ToAll("dp", nd, r.msg, r.msgs, r.msg_s, r.msg_r)
+    over_dp.start()
+    r.block_out[...] = ((r.xin[d] + outs.total()) * mine).T
+    over_dp.finish()
+    total = over_dp.total()
+    sh1, gg1 = to_col(total[0:1]), to_col(total[1:2])
+    square = total[2:3, 0:1] + jnp.sum(sh1 * sh1 + gg1 * gg1, keepdims=True)
+    r.sq[...] = jnp.broadcast_to(square, (8, 128))
+    over_chan = ToAll("chan", nc, r.sq, r.sqs, r.sq_s, r.sq_r)
+    over_chan.start()
+    over_chan.finish()
+    square = over_chan.total()[0:1, 0:1]
+    r.norm[0, 0] = jnp.sum(jnp.sqrt(square))
+    factor = sam_radius * lax.rsqrt(square + norm_floor)
+
+    gain1, shift1 = gain1 + factor * gg1, shift1 + factor * sh1
+    gain2, shift2 = gain2 + factor * gg2, shift2 + factor * sh2
+    r.a1[...] += factor * r.g1[...]
+    hi, lo = split(r.a1[...])
+    r.a_cat[0] = jnp.concatenate([hi, hi, lo], axis=1)
+    r.a2[...] += factor * r.g2[...]
+    set_back(r.a2)
+
+    act_copy = lambda sem, ys, i, z_to, y_to: send(
+        r.act2.at[ys, i], r.act2.at[ys, i], r.act_s.at[sem, i], r.act_r.at[ys, i], (z_to * ny + y_to, c)
+    )
+    act_up = lambda i: act_copy(0, y, i, lax.min(z + 1, nz - 1), y)
+    act_down = lambda i: act_copy(1, y, i, lax.max(z - 1, 0), y)
+    act_side = lambda i: act_copy(2, y, i, z, 1 - y)
+
+    def act_hand_on(i):
+        pl.when((z >= c) & (z < nz - 1))(lambda: act_up(i).start())
+        pl.when((z <= c) & (z > 0))(lambda: act_down(i).start())
+        act_side(i).start()
+
+    def second_act(i):
+        val = val_of(i)
+        act, slope = silu_and_slope((r.sums[i] - center2) * rs2 * gain2 + shift2)
+        r.slope2[i] = slope * val
+
+        @pl.when(z == c)
+        def _():
+            r.act2[y, i] = act * val
+            act_hand_on(i)
+
+    both_item = lambda j: j
+
+    def project(j, _):
+        pl.when(j < nd)(lambda: first_map(lax.min(j, nd - 1), gain1, shift1))
+        pl.when((j >= nd) & (j < 2 * nd))(lambda: second_back(lax.clamp(0, j - nd, nd - 1)))
+        chan.advance(j, 2 * nd, both_item)
+        pl.when((j >= 4) & (j < nd + 4))(lambda: second_act(lax.clamp(0, j - 4, nd - 1)))
+        return 0
+
+    lax.fori_loop(0, 2 * nd + 4, project, 0)
+
+    def inner_grad(i, carry):
+        dpre = r.sums[nd + i] * r.slope2[i]
+        r.dall[d, i] = gain2 * rs2 * dpre
+        scaled = (r.sums[i] - center2) * rs2
+        return carry[0] + lanes_sum(dpre), carry[1] + lanes_sum(dpre * scaled)
+
+    zero = jnp.zeros((db, 1), F32)
+    sh2, gg2 = lax.fori_loop(0, nd, inner_grad, (zero, zero))
+
+    pair = lambda s, q: r.dall.at[s, pl.ds(2 * q, 2)]
+    grads = Line(p, lambda s: pair(s, c), r.d_s, r.d_r)
+    grads.hand_on(z)
+    to_far = lambda s, q: send(pair(s, q), pair(s, q), r.far_s.at[s], r.far_r.at[s], (d, far))
+    to_core = lambda lane, s, q: send(pair(s, q), pair(s, q), r.core_s.at[lane, s], r.core_r.at[lane, s], (d, across))
+
+    def over_chan_too(s):
+        to_far(s, c).start()
+        to_core(0, s, c).start()
+
+    hi, lo = split(r.a1[...].T)
+    r.bm[0], r.bm[1] = hi, lo
+    ins_grad = ImageSum(p, r.inp, r.inn, r.inc, r.inw, r.i_s1, r.i_r1, r.i_s2, r.i_r2)
+
+    def input_grad(i):
+        set_cols(shifts(r.dall[d, i], side, -1))
+        r.inp[i] = im2col_dot((r.bm[0], r.bm[1]))
+
+    def to_partner(kk, _):
+        zs = nearest(z, kk)
+        input_grad(zs * ny + 1 - y)
+        ins_grad.near(zs).start()
+
+        @pl.when(z != c)
+        def _():
+            for j in range(2):
+                i = 2 * kk + j
+                act_copy(0, y, i, z, 1 - y).wait_recv()
+                act_hand_on(i)
+
+        return 0
+
+    lax.fori_loop(0, nz, to_partner, 0)
+
+    def at_home(kk, _):
+        zs = nearest(z, kk)
+        input_grad(zs * ny + y)
+
+        @pl.when(kk > 0)
+        def _():
+            grads.got(zs, y)
+            grads.hand_on(zs)
+            over_chan_too(zs * ny + y)
+
+        return 0
+
+    lax.fori_loop(0, nz, at_home, 0)
+    ins_grad.spread()
+
+    def norm_sums(i, carry):
+        dpre = r.inp[i] * r.slope1[i]
+        scaled = (r.xin[i] - center1) * rs1
+        return carry[0] + lanes_sum(dpre), carry[1] + lanes_sum(dpre * scaled)
+
+    zero = jnp.zeros((cb, 1), F32)
+    sh1, gg1 = lax.fori_loop(0, nd, norm_sums, (zero, zero))
+    pad = jnp.zeros((1, cb - db), F32)
+    wide = lambda col: jnp.concatenate([to_row(col), pad], axis=1)
+    r.vec[...] = stacked([to_row(sh1), to_row(gg1), wide(sh2), wide(gg2)], cb)
+    vectors = ToAll("dp", nd, r.vec, r.vecs, r.vec_s, r.vec_r)
+    vectors.start()
+
+    def relay_call(i, _):
+        call_copy(far, 0, i, far).wait_recv()
+        call_copy(far, 2, i, across).start()
+        return 0
+
+    lax.fori_loop(0, nd, relay_call, 0)
+
+    def call_here(i, _):
+        call_copy(across, 0, i, across).wait_recv()
+        call_copy(last, 0, i, across).wait_recv()
+        return 0
+
+    lax.fori_loop(0, nd, call_here, 0)
+
+    def kernel_grad(images, left_of, rights_of):
+        for j, i in enumerate(images):
+            lanes = slice(3 * j * px, 3 * (j + 1) * px)
+            for t, m in enumerate(shifts(left_of(i), side)):
+                hi, lo = split(m)
+                r.left[t * cb : (t + 1) * cb, lanes] = jnp.concatenate([hi, hi, lo], axis=1)
+            at = 0
+            for v in rights_of(i):
+                n = v.shape[0]
+                hi, lo = split(v)
+                r.right[at : at + n, lanes] = jnp.concatenate([hi, lo, hi], axis=1)
+                at += n
+        r.stage[...] += dot_nt(r.left[...], r.right[...])
+
+    r.stage[...] = jnp.zeros_like(r.stage)
+
+    def second_kernel(q, _):
+        for j in range(2):
+            act_copy(0, 1 - y, 2 * q + j, z, 1 - y).wait_recv()
+        kernel_grad(
+            [2 * q, 2 * q + 1],
+            lambda i: jnp.concatenate([r.act2[0, i], r.act2[1, i]], axis=0),
+            lambda i: [r.call[j, i] for j in range(nc)],
+        )
+        zs = nearest(z, q)
+        grads.got(zs, 1 - y)
+        over_chan_too(zs * ny + 1 - y)
+        return 0
+
+    lax.fori_loop(0, nz, second_kernel, 0)
+    g2_copy = pltpu.make_async_copy(r.stage, r.g2_out, r.g2_sem)
+    g2_copy.start()
+
+    for j in range(1, nd):
+        s = lax.rem(d + j, nd)
+        to_far(s, far).wait_recv()
+        to_core(1, s, far).start()
+
+    grad = (gain1 * rs1 * (ins_grad.total() * r.slope1[d]) + r.call[c, d]).T
+    for j in range(nc):
+        r.xs[j] = grad[j * rows : (j + 1) * rows]
+    back = lambda j: send(r.xs.at[lax.rem(c + j, nc)], r.rx.at[c], r.in_s.at[j], r.in_r.at[c], (d, lax.rem(c + j, nc)))
+    for j in range(1, nc):
+        back(j).start()
+    r.rx[c] = r.xs[c]
+
+    g2_copy.wait()
+    r.stage[...] = jnp.zeros_like(r.stage)
+
+    def first_kernel(q):
+        kernel_grad([2 * q, 2 * q + 1], lambda i: r.act1[i], lambda i: [r.dall[s, i] for s in range(nd)])
+
+    first_kernel(c)
+    for j in range(1, nd):
+        to_core(0, lax.rem(d + j, nd), across).wait_recv()
+    first_kernel(across)
+    first_kernel(far)
+    for j in range(1, nd):
+        to_core(1, lax.rem(d + j, nd), last).wait_recv()
+    first_kernel(last)
+    g1_copy = pltpu.make_async_copy(r.stage, r.g1_out, r.g1_sem)
+    g1_copy.start()
+
+    vectors.finish()
+    total = vectors.total()
+    per = cb // db
+    rows_of = lambda j: jnp.concatenate([r.vecs[per * c + q, j : j + 1, :db] for q in range(per)], axis=1)
+    r.sh1[...], r.gg1[...] = total[0:1].reshape(cb), total[1:2].reshape(cb)
+    r.sh2[...], r.gg2[...] = rows_of(2).reshape(cb), rows_of(3).reshape(cb)
+    for j in range(1, nc):
+        back(j).wait_send()
+        other = lax.rem(c + j, nc)
+        send(r.xs.at[other], r.rx.at[other], r.in_s.at[0], r.in_r.at[other], (d, other)).wait_recv()
+    for j in range(nc):
+        r.input_grad[:, j * cb : (j + 1) * cb] = r.rx[j]
+
+    for line in (ins, cots, grads):
+        line.drain()
+
+    @pl.when(c == owner)
+    def _():
+        for j in range(1, nc):
+            piece(j).wait_send()
+
+    def sent(i, _):
+        call_copy(c, 0, i, far).wait_send()
+        call_copy(c, 1, i, across).wait_send()
+        call_copy(far, 2, i, across).wait_send()
+        pl.when((z >= c) & (z < nz - 1))(lambda: act_up(i).wait_send())
+        pl.when((z <= c) & (z > 0))(lambda: act_down(i).wait_send())
+        act_side(i).wait_send()
+        return 0
+
+    lax.fori_loop(0, nd, sent, 0)
+    for j in range(1, nd):
+        s = lax.rem(d + j, nd)
+        to_far(s, c).wait_send()
+        to_core(0, s, c).wait_send()
+        to_core(1, s, far).wait_send()
+    g1_copy.wait()
+
+
+def fused_on_device(p, image_rows, groups, conv_first, conv_second, gain_first, shift_first, gain_second, shift_second, cotangent):
+    cb, px = p.cb, p.px
+    rows = px // p.nc
+    scratch = scratch_of(p)
+    out = lambda *s: jax.ShapeDtypeStruct(s, F32)
+    any_, vmem, smem = (pl.BlockSpec(memory_space=m) for m in (pl.ANY, VMEM, SMEM))
+    block_out, input_grad, g1, g2, gg1, sh1, gg2, sh2, norm = pl.pallas_call(
+        functools.partial(step_kernel, p, ARGS + OUTS + tuple(scratch)),
+        out_shape=(out(px, cb), out(rows, p.ch), out(9 * cb, p.ch), out(9 * cb, p.ch), out(cb), out(cb), out(cb), out(cb), out(1, 1)),
+        in_specs=[vmem, vmem, any_, any_, vmem, vmem, vmem, vmem, smem],
+        out_specs=(vmem, vmem, any_, any_, vmem, vmem, vmem, vmem, smem),
+        scratch_shapes=list(scratch.values()),
+        compiler_params=pltpu.CompilerParams(collective_id=0, has_side_effects=True, vmem_limit_bytes=LIMIT),
+    )(
+        image_rows.reshape(rows, p.ch), cotangent.reshape(px, cb), conv_first.reshape(9, cb, p.ch),
+        conv_second.reshape(9, cb, p.ch), gain_first, shift_first, gain_second, shift_second, groups,
+    )
+    return (
+        block_out.reshape(cotangent.shape), input_grad.reshape(image_rows.shape),
+        g1.reshape(conv_first.shape), g2.reshape(conv_second.shape), gg1, sh1, gg2, sh2, norm[0, 0],
+    )
 
 
 def valid_pixels(groups, extent_full):
@@ -31,7 +854,7 @@
     return sigmoid * (1.0 + preact * (1.0 - sigmoid))
 
 
-def moments(values, validity):
+def batch_moments(values, validity):
     summed, squares, pixels = lax.psum(
         (
             jnp.sum(values * validity, axis=(0, 1, 2)),
@@ -45,7 +868,7 @@
     return (center, lax.rsqrt(spread + epsilon), pixels)
 
 
-def project(values, kernel):
+def project_over_chan(values, kernel):
     return lax.psum_scatter(convolve(values, kernel), "chan", scatter_dimension=3, tiled=True)
 
 
@@ -66,7 +889,7 @@
     return lax.psum((jnp.sum(dpre, axis=(0, 1, 2)), jnp.sum(dpre * scaled, axis=(0, 1, 2))), "dp")
 
 
-def on_device(
+def plain_on_device(
     image_rows,
     groups,
     conv_first,
@@ -80,16 +903,16 @@
     inputs = lax.all_to_all(image_rows, "chan", split_axis=3, concat_axis=1, tiled=True)
     validity = valid_pixels(groups, inputs.shape[1])
     cot_valid = cotangent * validity
-    center_one, rscale_one, pixels = moments(inputs, validity)
+    center_one, rscale_one, pixels = batch_moments(inputs, validity)
     scaled_one = (inputs - center_one) * rscale_one
     pre_one = scaled_one * gain_first + shift_first
     act_one = jax.nn.silu(pre_one) * validity
-    inner = project(act_one, conv_first) * validity
-    center_two, rscale_two, pixels_again = moments(inner, validity)
+    inner = project_over_chan(act_one, conv_first) * validity
+    center_two, rscale_two, pixels_again = batch_moments(inner, validity)
     scaled_two = (inner - center_two) * rscale_two
     pre_two = scaled_two * gain_second + shift_second
     act_two = jax.nn.silu(pre_two) * validity
-    block_out = inputs * validity + project(act_two, conv_second) * validity
+    block_out = inputs * validity + project_over_chan(act_two, conv_second) * validity
     dact_two, kernel_two_part = conv_backward(cot_valid, act_two, conv_second)
     dpre_two = dact_two * validity * silu_slope(pre_two)
     shift_two_grad, gain_two_grad = batch_sums(dpre_two, scaled_two)
@@ -120,7 +943,7 @@
     moved_shift_two = shift_second + factor * shift_two_grad
     pre_one_new = scaled_one * moved_gain_one + moved_shift_one
     act_one_new = jax.nn.silu(pre_one_new) * validity
-    inner_new = project(act_one_new, kernel_one) * validity
+    inner_new = project_over_chan(act_one_new, kernel_one) * validity
     scaled_two_new = (inner_new - center_two) * rscale_two
     pre_two_new = scaled_two_new * moved_gain_two + moved_shift_two
     act_two_new = jax.nn.silu(pre_two_new) * validity
@@ -167,6 +990,15 @@
 
 
 def solution(mesh):
+    nd, nc = mesh.shape["dp"], mesh.shape["chan"]
+
+    def on_device(image_rows, *rest):
+        images, side, channels = image_rows.shape[0], image_rows.shape[2], image_rows.shape[3]
+        fits = images == 1 and nc == 4 and nd == 2 * nc and channels // nd % 16 == 0 and side * side == 256
+        if not fits:
+            return plain_on_device(image_rows, *rest)
+        return fused_on_device(Plan(nd, nc, channels, side), image_rows, *rest)
+
     return jax.shard_map(
         on_device,
         mesh=mesh,

time: 1250 us -> 235 us (0.19)
  local copies, waits for them, and re-layouts: 473 us -> 11.7 us
  waiting for transfers between devices: 372 us -> 0 us
  Pallas kernels: 0 us -> 220 us
  blocking collectives: 209 us -> 0 us
  matrix products: 151 us -> 0 us
  between operations: 22.1 us -> 3.14 us
  other arithmetic: 14.7 us -> 0 us
    unnamed x122 -> x18, local copies, waits for them, and re-layouts: 382 us -> 11.7 us
    psum x2 -> x0, waiting for transfers between devices: 350 us -> none  [the longest x1 192 us: on_device(): lax.psum((kernel_one_part, kernel_two_part), 'dp')]
    pallas_call x0 -> x1, Pallas kernels: none -> 220 us  [fused_on_device(): pl.pallas_call(functools.partial(step_kernel, p, ARGS + OUTS + tuple(scra...]
    conv_general_dilated x11 -> x0, matrix products: 151 us -> none  [convolve(): lax.conv_general_dilated(values, kernel, (1, 1), 'SAME', dimension_number...]
    psum x6 -> x0, blocking collectives: 111 us -> none  [the longest x2 44.6 us: moments(): lax.psum((jnp.sum(values * validity, axis=(0, 1, 2)), jnp.sum(validity *...]
    all_gather x3 -> x0, blocking collectives: 98 us -> none  [conv_backward(): columns = lax.all_gather(upstream, 'chan', axis=3, tiled=True)]
    reduce_scatter x3 -> x0, local copies, waits for them, and re-layouts: 57.9 us -> none  [project(): lax.psum_scatter(convolve(values, kernel), 'chan', scatter_dimension=3, t...]
    all_gather x9 -> x0, local copies, waits for them, and re-layouts: 24.5 us -> none  [conv_backward(): columns = lax.all_gather(upstream, 'chan', axis=3, tiled=True)]
  transfers between devices with their start and end apart: 7 -> 0, of which waited for: 4 -> 0; matrix products, arithmetic and copies ran while one was open for 17% -> 0% of each run, Pallas kernels for 0% -> 0%
where the time goes in v2:
time: 235 us; the launch traced here: 234 us
  Pallas kernels  220 us (94%)
  local copies, waits for them, and re-layouts  11.7 us (5%)
  between operations  3.14 us (1%)
    pallas_call x1, Pallas kernels, fused_on_device(): pl.pallas_call(functools.partial(step_kernel, p, ARGS + OUTS + tuple(scra...  220 us
    unnamed x18, local copies, waits for them, and re-layouts  11.7 us

profile of v2, /device:TPU:0, one launch (start us, length us, event | category | flops | bytes accessed | tf_op | source)
XLA Modules:
  0.0 234.4 jit_solution(2870626909795439481)
XLA Ops:
  1.3 219.6 %shard_map.160 = (f32[256,160]{1,0:T(8,128)}, f32[64,640]{1,0:T(8,128)}, f32[1440,640]{1,0:T(8,128)}, f32[1440,640]{1,0:T(8,128)}, f32[160]{0:T(256)}, /*index=5...) custom-call(f32[64,640]{1,0:T(8,128)} %bitcast.16, f32[256,160]{1,0:T(8,128)} %bitcast.13, ...), custom_call_target="tpu_custom_call" | custom-call | tf_op jit(solution)/shard_map/pallas_call | solution.py:817
  220.9 1.7 copy.28
  222.6 1.6 copy.29
  224.2 0.0 copy-start
  224.2 4.3 %copy.30 = f32[3,3,160,640]{3,2,1,0:T(8,128)} copy(f32[3,3,160,640]{3,2,1,0:T(8,128)} %bitcast.12) | data formatting | bytes 7372800
  228.4 0.0 copy-done
  228.4 0.0 copy-start.4
  228.4 0.0 copy-start.3
  228.4 0.0 copy-start.2
  228.4 0.0 copy-start.1
  228.5 1.8 copy.31
  230.3 0.0 copy-done.4
  230.3 0.6 copy.32
  230.9 0.0 copy-done.3
  230.9 0.6 copy.33
  231.4 0.0 copy-done.2
  231.4 0.6 copy.34
  232.0 0.0 copy-done.1
  232.0 0.6 copy.35
Async XLA Ops:
  224.2 4.3 %copy-start = (f32[1440,640]{1,0:T(8,128)S(1)}, f32[1440,640]{1,0:T(8,128)}, u32[]{:S(2)}) copy-start(f32[1440,640]{1,0:T(8,128)} %get-tuple-element.21) | copy-start | bytes 11059204
  228.4 1.9 copy-start.4
  228.4 2.4 %copy-start.3 = (f32[160]{0:T(256)S(1)}, f32[160]{0:T(256)}, u32[]{:S(2)}) copy-start(f32[160]{0:T(256)} %get-tuple-element.41) | copy-start | bytes 1924
  228.4 3.0 %copy-start.2 = (f32[160]{0:T(256)S(1)}, f32[160]{0:T(256)}, u32[]{:S(2)}) copy-start(f32[160]{0:T(256)} %get-tuple-element.42) | copy-start | bytes 1924
  228.4 3.6 %copy-start.1 = (f32[160]{0:T(256)S(1)}, f32[160]{0:T(256)}, u32[]{:S(2)}) copy-start(f32[160]{0:T(256)} %get-tuple-element.43) | copy-start | bytes 1924

commit v3 on v2

--- a/solution.py
+++ b/solution.py
@@ -161,8 +161,8 @@
 
 
 class Line:
-    def __init__(self, p, view, ss, rs):
-        self.p, self.view, self.ss, self.rs = p, view, ss, rs
+    def __init__(self, p, view, ss, rs, sides=True):
+        self.p, self.view, self.ss, self.rs, self.sides = p, view, ss, rs, sides
         d, self.c = here()
         self.z, self.y = lax.div(d, p.ny), lax.rem(d, p.ny)
 
@@ -186,13 +186,15 @@
     def hand_on(self, zs):
         pl.when((zs <= self.z) & (self.z < self.p.nz - 1))(lambda: self.up(zs).start())
         pl.when((zs >= self.z) & (self.z > 0))(lambda: self.down(zs).start())
-        self.side(zs).start()
+        if self.sides:
+            self.side(zs).start()
 
     def drain(self):
         for zs in range(self.p.nz):
             pl.when((zs <= self.z) & (self.z < self.p.nz - 1))(lambda: self.up(zs).wait_send())
             pl.when((zs >= self.z) & (self.z > 0))(lambda: self.down(zs).wait_send())
-            self.side(zs).wait_send()
+            if self.sides:
+                self.side(zs).wait_send()
 
 
 def nearest(z, k):
@@ -215,7 +217,7 @@
 
     def first(self, i):
         r = self.r
-        return send(r.part.at[i], r.near.at[i], r.cs1.at[i], r.cr1.at[i], self.across)
+        return send(r.part.at[i, pl.ds(self.yours, self.hb)], r.near.at[i], r.cs1.at[i], r.cr1.at[i], self.across)
 
     def second(self, i):
         r = self.r
@@ -229,7 +231,7 @@
     def chip(self, i):
         r = self.r
         self.first(i).wait()
-        r.half[i] = r.part[i, pl.ds(self.mine, self.hb)] + r.near[i, pl.ds(self.mine, self.hb)]
+        r.half[i] = r.part[i, pl.ds(self.mine, self.hb)] + r.near[i]
         self.second(i).start()
 
     def cross(self, i):
@@ -263,13 +265,10 @@
     def away(self, zs, slot):
         return send(self.acc.at[zs], self.buf2.at[slot], self.s2.at[zs], self.r2.at[slot], (zs * self.p.ny + self.y, self.c))
 
-    def spread(self):
-        for j in range(1, self.p.nz + 1):
-            zs = lax.rem(self.z + j, self.p.nz)
-            self.near(zs).wait()
-            self.acc[zs] = self.part[zs * self.p.ny + self.y] + self.buf1[zs]
-            if j < self.p.nz:
-                self.away(zs, self.z).start()
+    def spread(self, zs):
+        self.near(zs).wait()
+        self.acc[zs] = self.part[zs * self.p.ny + self.y] + self.buf1[zs]
+        pl.when(zs != self.z)(lambda: self.away(zs, self.z).start())
 
     def total(self):
         total = self.acc[self.z]
@@ -291,11 +290,11 @@
         a_cat=h(2, 9 * db, 3 * cb), bm=h(2, cb, 9 * db), b2m=h(2, cb, 9 * db), colh=h(9 * db, px), coll=h(9 * db, px),
         xs=f(nc, rows, cb), rx=f(nc, rows, cb), xin=f(nd, cb, px), act1=f(nd, cb, px), slope1=f(nd, cb, px),
         call=f(nc, nd, cb, px),
-        part=f(2 * nd, db, px), near=f(2 * nd, db, px), half=f(2 * nd, db // 2, px), away=f(2 * nd, db // 2, px),
-        sums=f(2 * nd, db, px), slope2=f(nd, db, px), dpre=f(nd, db, px),
+        part=f(3 * nd, db, px), near=f(3 * nd, db // 2, px), half=f(3 * nd, db // 2, px), away=f(3 * nd, db // 2, px),
+        sums=f(3 * nd, db, px), slope2=f(nd, db, px), dpre=f(nd, db, px), add1=f(2, cb, px), add2=f(2, db, px),
         outp=f(nd, cb, px), outn=f(nz, cb, px), outc=f(nz, cb, px), outw=f(nz, cb, px),
         inp=f(nd, cb, px), inn=f(nz, cb, px), inc=f(nz, cb, px), inw=f(nz, cb, px),
-        dall=f(nd, nd, db, px), act2=f(ny, nd, db, px), left=h(9 * cb, 6 * px), right=h(p.ch, 6 * px),
+        dall=f(nd, nd, db, px), act2=f(ny, nd, db, px), own2=f(nd, db, px), left=h(9 * cb, 6 * px), right=h(p.ch, 6 * px),
         stage=f(9 * cb, p.ch),
         par=f(8, cb), pars=f(nc, 8, cb), stat=f(8, cb), stats=f(nd, 8, cb), msg=f(8, cb), msgs=f(nd, 8, cb),
         sq=f(8, 128), sqs=f(nc, 8, 128), vec=f(8, cb), vecs=f(nd, 8, cb),
@@ -304,16 +303,16 @@
         par_s=DMA((nc,)), par_r=DMA((nc,)), stat_s=DMA((nd,)), stat_r=DMA((nd,)), msg_s=DMA((nd,)), msg_r=DMA((nd,)),
         sq_s=DMA((nc,)), sq_r=DMA((nc,)), vec_s=DMA((nd,)), vec_r=DMA((nd,)),
         x_s=DMA((3, nz)), x_r=DMA((nd,)), c_s=DMA((3, nz)), c_r=DMA((nd,)), d_s=DMA((3, nz)), d_r=DMA((nd,)),
-        cs1=DMA((2 * nd,)), cr1=DMA((2 * nd,)), cs2=DMA((2 * nd,)), cr2=DMA((2 * nd,)), cs3=DMA((2 * nd,)), cr3=DMA((2 * nd,)),
+        cs1=DMA((3 * nd,)), cr1=DMA((3 * nd,)), cs2=DMA((3 * nd,)), cr2=DMA((3 * nd,)), cs3=DMA((3 * nd,)), cr3=DMA((3 * nd,)),
         o_s1=DMA((nz,)), o_r1=DMA((nz,)), o_s2=DMA((nz,)), o_r2=DMA((nz,)),
         i_s1=DMA((nz,)), i_r1=DMA((nz,)), i_s2=DMA((nz,)), i_r2=DMA((nz,)),
-        call_s=DMA((3, nd)), call_r=DMA((nc, nd)), act_s=DMA((3, nd)), act_r=DMA((ny, nd)),
+        call_s=DMA((2, nd)), call_r=DMA((2, nd)), own_s=DMA, f_s=DMA((3, nz)), f_r=DMA((nd,)), act_s=DMA((3, nd)), act_r=DMA((ny, nd)),
         far_s=DMA((nd,)), far_r=DMA((nd,)), core_s=DMA((2, nd)), core_r=DMA((2, nd)), in_s=DMA((nc,)), in_r=DMA((nc,)),
     )
 
 
 ARGS = ("x", "cot", "k1", "k2", "gain1", "shift1", "gain2", "shift2", "groups")
-OUTS = ("block_out", "input_grad", "g1_out", "g2_out", "gg1", "sh1", "gg2", "sh2", "norm")
+OUTS = ("block_out", "input_grad", "g1_out", "g2_out", "small")
 
 
 def step_kernel(p, names, *refs):
@@ -410,30 +409,46 @@
         r.part[i] = gather_taps(prod, side, db) * val
         chan.first(i).start()
 
-    def second_back(i):
+    def second_back(i, first):
         ch, cl = split(r.call[c, i])
         prod = dot(r.a_cat[1], jnp.concatenate([ch, cl, ch], axis=0))
-        r.part[nd + i] = gather_taps(prod, side, db) * val_of(i)
-        chan.first(nd + i).start()
+        r.part[first + i] = gather_taps(prod, side, db) * val_of(i)
+        chan.first(first + i).start()
+
+    def meet(line, step, then=None):
+        def one(zs):
+            line.got(zs, y)
+            line.hand_on(zs)
+            if then is not None:
+                then(zs)
+
+        pl.when(z >= step)(lambda: one(lax.max(z - step, 0)))
+        pl.when(z + step < nz)(lambda: one(lax.min(z + step, nz - 1)))
+
+    cots = Line(p, lambda s: r.call.at[c, s], r.c_s, r.c_r)
 
     def forward(kk, _):
         zs = nearest(z, kk)
-
-        @pl.when(kk > 0)
-        def _():
-            ins.got(zs, y)
-            ins.hand_on(zs)
-
         first_map(zs * ny + y, gain1, shift1)
         chan.advance(2 * kk, nd, image)
+        meet(ins, kk + 1)
+        pl.when(kk == nz - 2)(lambda: cots.hand_on(z))
         ins.got(zs, 1 - y)
         first_map(zs * ny + 1 - y, gain1, shift1)
         chan.advance(2 * kk + 1, nd, image)
         return 0
 
     lax.fori_loop(0, nz, forward, 0)
-    cots = Line(p, lambda s: r.call.at[c, s], r.c_s, r.c_r)
-    cots.hand_on(z)
+
+    own_cot = lambda q: send(r.call.at[q, d], r.call.at[q, d], r.own_s, r.f_r.at[d], (d, far))
+    own_cot(c).start()
+    fars = Line(p, lambda s: r.call.at[far, s], r.f_s, r.f_r, False)
+    far_side = lambda zs: fars.side(zs)
+    call_copy = lambda lane, q, i: send(
+        r.call.at[q, i], r.call.at[q, i], r.call_s.at[lane, i], r.call_r.at[lane, i], (d, across)
+    )
+
+    meet(cots, 1)
 
     @pl.when(c == owner)
     def _():
@@ -448,14 +463,16 @@
             hi, lo = split(a2[(8 - t) * db : (9 - t) * db])
             r.a_cat[1, t * db : (t + 1) * db] = jnp.concatenate([hi, hi, lo], axis=1)
 
+    chan.advance(nd, nd, image)
     r.a2[...] = r.b2[...].T
+    chan.advance(nd + 1, nd, image)
     set_back(r.a2)
-
-    def flush(j, _):
-        chan.advance(j, nd, image)
-        return 0
-
-    lax.fori_loop(nd, nd + 4, flush, 0)
+    chan.advance(nd + 2, nd, image)
+    b2h, b2l = split(r.b2[...])
+    r.b2m[0], r.b2m[1] = b2h, b2l
+    chan.advance(nd + 3, nd, image)
+
+    meet(cots, 2)
 
     params.finish()
     both = [r.pars[owner, j : j + 1] for j in range(2)]
@@ -474,7 +491,6 @@
     rs2 = lax.rsqrt(lax.fori_loop(0, nd, add_squares, jnp.zeros((db, 1), F32)) / pixels + epsilon)
 
     outs = ImageSum(p, r.outp, r.outn, r.outc, r.outw, r.o_s1, r.o_r1, r.o_s2, r.o_r2)
-    b2h, b2l = split(r.b2[...])
 
     def set_cols(maps):
         for t, m in enumerate(maps):
@@ -490,9 +506,6 @@
         left = jnp.concatenate([r.colh[...], r.colh[...], r.coll[...]], axis=1)
         return dot_nt(left, jnp.concatenate([oh, ol, oh], axis=1))
 
-    call_copy = lambda which, sem, i, to: send(
-        r.call.at[which, i], r.call.at[which, i], r.call_s.at[sem, i], r.call_r.at[which, i], (d, to)
-    )
     r.g2[...] = jnp.zeros_like(r.g2)
 
     def second_map(i):
@@ -508,37 +521,37 @@
 
     def cotangent(kk, _):
         zs = nearest(z, kk)
+        second_back(zs * ny + y, nd)
+        chan.advance(2 * kk, nd, back_item)
 
         @pl.when(kk > 0)
         def _():
-            cots.got(zs, y)
-            cots.hand_on(zs)
-
-        i = zs * ny + y
-        second_back(i)
-        call_copy(c, 0, i, far).start()
-        call_copy(c, 1, i, across).start()
-        chan.advance(2 * kk, nd, back_item)
-        second_map(i)
+            before = nearest(z, lax.max(kk - 1, 0))
+            second_map(before * ny + 1 - y)
+            outs.near(before).start()
+
+        pl.when(kk == 0)(lambda: meet(cots, 3))
+
+        @pl.when(kk == nz - 2)
+        def _():
+            own_cot(far).wait_recv()
+            fars.hand_on(z)
+
         cots.got(zs, 1 - y)
-        i = zs * ny + 1 - y
-        second_back(i)
-        call_copy(c, 0, i, far).start()
-        call_copy(c, 1, i, across).start()
+        second_back(zs * ny + 1 - y, nd)
         chan.advance(2 * kk + 1, nd, back_item)
-        second_map(i)
-        outs.near(zs).start()
+        second_map(zs * ny + y)
         return 0
 
-    r.b2m[0], r.b2m[1] = b2h, b2l
     lax.fori_loop(0, nz, cotangent, 0)
-
-    def flush_back(j, _):
-        chan.advance(j, nd, back_item)
-        return 0
-
-    lax.fori_loop(nd, nd + 4, flush_back, 0)
-    outs.spread()
+    chan.advance(nd, nd, back_item)
+    furthest = nearest(z, nz - 1)
+    second_map(furthest * ny + 1 - y)
+    outs.near(furthest).start()
+    chan.advance(nd + 1, nd, back_item)
+    set_back(r.g2)
+    chan.advance(nd + 2, nd, back_item)
+    chan.advance(nd + 3, nd, back_item)
 
     def inner_sums(i, carry):
         dpre = r.sums[nd + i] * r.slope2[i]
@@ -550,13 +563,21 @@
     sh2, gg2 = lax.fori_loop(0, nd, inner_sums, (zero, zero))
     r.g1[...] = jnp.zeros_like(r.g1)
 
+    change_item = lambda j: 2 * nd + j
+
     def backward(i, carry):
+        call_copy(0, c, i).start()
+
+        pl.when(i == 0)(lambda: far_side(z).start())
+        pl.when(i >= nz)(lambda: outs.spread(nearest(z, lax.max(nd - 1 - i, 0))))
         scaled = (r.sums[i] - center2) * rs2
         dinner = gain2 * rs2 * (r.dpre[i] - val_of(i) * (sh2 + scaled * gg2) / pixels)
         set_cols(shifts(dinner, side, -1))
         r.g1[...] += wgrad(r.act1[i])
         dpre1 = im2col_dot((r.bm[0], r.bm[1])) * r.slope1[i]
         scaled1 = (r.xin[i] - center1) * rs1
+        pl.when(i == 2)(lambda: meet(fars, 1, lambda zs: far_side(zs).start()))
+        pl.when(i == 6)(lambda: meet(fars, 2, lambda zs: far_side(zs).start()))
         return carry[0] + lanes_sum(dpre1), carry[1] + lanes_sum(dpre1 * scaled1)
 
     zero = jnp.zeros((cb, 1), F32)
@@ -567,7 +588,13 @@
     r.msg[...] = stacked([to_row(sh1), to_row(gg1), jnp.broadcast_to(square, (1, cb))], cb)
     over_dp = ToAll("dp", nd, r.msg, r.msgs, r.msg_s, r.msg_r)
     over_dp.start()
-    r.block_out[...] = ((r.xin[d] + outs.total()) * mine).T
+
+    def change(j, _):
+        second_back(j, 2 * nd)
+        chan.advance(j, nd, change_item)
+        return 0
+
+    lax.fori_loop(0, nd // 2, change, 0)
     over_dp.finish()
     total = over_dp.total()
     sh1, gg1 = to_col(total[0:1]), to_col(total[1:2])
@@ -575,9 +602,10 @@
     r.sq[...] = jnp.broadcast_to(square, (8, 128))
     over_chan = ToAll("chan", nc, r.sq, r.sqs, r.sq_s, r.sq_r)
     over_chan.start()
+    lax.fori_loop(nd // 2, nd, change, 0)
     over_chan.finish()
     square = over_chan.total()[0:1, 0:1]
-    r.norm[0, 0] = jnp.sum(jnp.sqrt(square))
+    norm = jnp.sqrt(square)
     factor = sam_radius * lax.rsqrt(square + norm_floor)
 
     gain1, shift1 = gain1 + factor * gg1, shift1 + factor * sh1
@@ -585,8 +613,6 @@
     r.a1[...] += factor * r.g1[...]
     hi, lo = split(r.a1[...])
     r.a_cat[0] = jnp.concatenate([hi, hi, lo], axis=1)
-    r.a2[...] += factor * r.g2[...]
-    set_back(r.a2)
 
     act_copy = lambda sem, ys, i, z_to, y_to: send(
         r.act2.at[ys, i], r.act2.at[ys, i], r.act_s.at[sem, i], r.act_r.at[ys, i], (z_to * ny + y_to, c)
@@ -604,35 +630,25 @@
         val = val_of(i)
         act, slope = silu_and_slope((r.sums[i] - center2) * rs2 * gain2 + shift2)
         r.slope2[i] = slope * val
-
-        @pl.when(z == c)
-        def _():
-            r.act2[y, i] = act * val
-            act_hand_on(i)
-
-    both_item = lambda j: j
-
-    def project(j, _):
-        pl.when(j < nd)(lambda: first_map(lax.min(j, nd - 1), gain1, shift1))
-        pl.when((j >= nd) & (j < 2 * nd))(lambda: second_back(lax.clamp(0, j - nd, nd - 1)))
-        chan.advance(j, 2 * nd, both_item)
-        pl.when((j >= 4) & (j < nd + 4))(lambda: second_act(lax.clamp(0, j - 4, nd - 1)))
-        return 0
-
-    lax.fori_loop(0, 2 * nd + 4, project, 0)
-
-    def inner_grad(i, carry):
-        dpre = r.sums[nd + i] * r.slope2[i]
-        r.dall[d, i] = gain2 * rs2 * dpre
-        scaled = (r.sums[i] - center2) * rs2
-        return carry[0] + lanes_sum(dpre), carry[1] + lanes_sum(dpre * scaled)
-
-    zero = jnp.zeros((db, 1), F32)
-    sh2, gg2 = lax.fori_loop(0, nd, inner_grad, (zero, zero))
+        r.own2[i] = act * val
+
+    def far_to_core(j):
+        zs = nearest(z, lax.div(j, 2))
+        pl.when(lax.rem(j, 2) == 1)(lambda: fars.got(zs, 1 - y))
+        call_copy(1, far, image(j)).start()
+
+    away = lax.max(z - c, c - z)
+
+    def act_step(t):
+        for i in range(nd):
+
+            @pl.when((away > 0) & (t == lax.div(16 + 8 * away + 5 * i, 4)))
+            def _():
+                act_copy(0, y, i, z, 1 - y).wait_recv()
+                act_hand_on(i)
 
     pair = lambda s, q: r.dall.at[s, pl.ds(2 * q, 2)]
     grads = Line(p, lambda s: pair(s, c), r.d_s, r.d_r)
-    grads.hand_on(z)
     to_far = lambda s, q: send(pair(s, q), pair(s, q), r.far_s.at[s], r.far_r.at[s], (d, far))
     to_core = lambda lane, s, q: send(pair(s, q), pair(s, q), r.core_s.at[lane, s], r.core_r.at[lane, s], (d, across))
 
@@ -640,73 +656,80 @@
         to_far(s, c).start()
         to_core(0, s, c).start()
 
+    def meet_sides(step):
+        def one(zs):
+            grads.got(zs, 1 - y)
+            over_chan_too(zs * ny + 1 - y)
+
+        pl.when(z >= step)(lambda: one(lax.max(z - step, 0)))
+        if step > 0:
+            pl.when(z + step < nz)(lambda: one(lax.min(z + step, nz - 1)))
+
     hi, lo = split(r.a1[...].T)
     r.bm[0], r.bm[1] = hi, lo
     ins_grad = ImageSum(p, r.inp, r.inn, r.inc, r.inw, r.i_s1, r.i_r1, r.i_s2, r.i_r2)
-
-    def input_grad(i):
-        set_cols(shifts(r.dall[d, i], side, -1))
-        r.inp[i] = im2col_dot((r.bm[0], r.bm[1]))
-
-    def to_partner(kk, _):
-        zs = nearest(z, kk)
-        input_grad(zs * ny + 1 - y)
-        ins_grad.near(zs).start()
-
-        @pl.when(z != c)
+    r.add1[...] = jnp.zeros_like(r.add1)
+    r.add2[...] = jnp.zeros_like(r.add2)
+
+    def inner_grad(i):
+        second_act(i)
+        dpre = (r.sums[nd + i] + factor * r.sums[2 * nd + i]) * r.slope2[i]
+        dinner = gain2 * rs2 * dpre
+        r.dall[d, i] = dinner
+        r.add2[0] += dpre
+        r.add2[1] += dpre * ((r.sums[i] - center2) * rs2)
+        set_cols(shifts(dinner, side, -1))
+        dact1 = im2col_dot((r.bm[0], r.bm[1]))
+        r.inp[i] = dact1
+        dpre1 = dact1 * r.slope1[i]
+        r.add1[0] += dpre1
+        r.add1[1] += dpre1 * ((r.xin[i] - center1) * rs1)
+
+        @pl.when(z == c)
         def _():
-            for j in range(2):
-                i = 2 * kk + j
-                act_copy(0, y, i, z, 1 - y).wait_recv()
-                act_hand_on(i)
-
+            r.act2[y, i] = r.own2[i]
+            act_hand_on(i)
+
+
+    same = lambda j: j
+
+    def start(j, _):
+        pl.when(j == 2)(lambda: meet(fars, 3, lambda zs: far_side(zs).start()))
+        first_map(j, gain1, shift1)
+        chan.advance(nd + j, nd, change_item)
+        chan.advance(j, nd, same)
         return 0
 
-    lax.fori_loop(0, nz, to_partner, 0)
-
-    def at_home(kk, _):
-        zs = nearest(z, kk)
-        input_grad(zs * ny + y)
-
-        @pl.when(kk > 0)
-        def _():
-            grads.got(zs, y)
-            grads.hand_on(zs)
-            over_chan_too(zs * ny + y)
-
+    def steady(j, _):
+        first_map(j, gain1, shift1)
+        chan.advance(j, nd, same)
+        inner_grad(j - 4)
+        far_to_core(j - 4)
+        act_step(j)
         return 0
 
-    lax.fori_loop(0, nz, at_home, 0)
-    ins_grad.spread()
-
-    def norm_sums(i, carry):
-        dpre = r.inp[i] * r.slope1[i]
-        scaled = (r.xin[i] - center1) * rs1
-        return carry[0] + lanes_sum(dpre), carry[1] + lanes_sum(dpre * scaled)
-
-    zero = jnp.zeros((cb, 1), F32)
-    sh1, gg1 = lax.fori_loop(0, nd, norm_sums, (zero, zero))
+    def end(j, _):
+        chan.advance(j, nd, same)
+        inner_grad(j - 4)
+        ins_grad.near(j - nd).start()
+        far_to_core(j - 4)
+        act_step(j)
+        return 0
+
+    lax.fori_loop(0, 4, start, 0)
+    lax.fori_loop(4, nd, steady, 0)
+    lax.fori_loop(nd, nd + 4, end, 0)
+    grads.hand_on(z)
+    sh1, gg1 = lanes_sum(r.add1[0]), lanes_sum(r.add1[1])
+    sh2, gg2 = lanes_sum(r.add2[0]), lanes_sum(r.add2[1])
+
     pad = jnp.zeros((1, cb - db), F32)
     wide = lambda col: jnp.concatenate([to_row(col), pad], axis=1)
     r.vec[...] = stacked([to_row(sh1), to_row(gg1), wide(sh2), wide(gg2)], cb)
     vectors = ToAll("dp", nd, r.vec, r.vecs, r.vec_s, r.vec_r)
     vectors.start()
 
-    def relay_call(i, _):
-        call_copy(far, 0, i, far).wait_recv()
-        call_copy(far, 2, i, across).start()
-        return 0
-
-    lax.fori_loop(0, nd, relay_call, 0)
-
-    def call_here(i, _):
-        call_copy(across, 0, i, across).wait_recv()
-        call_copy(last, 0, i, across).wait_recv()
-        return 0
-
-    lax.fori_loop(0, nd, call_here, 0)
-
-    def kernel_grad(images, left_of, rights_of):
+    def kernel_grad(images, left_of, rights_of, between=None):
         for j, i in enumerate(images):
             lanes = slice(3 * j * px, 3 * (j + 1) * px)
             for t, m in enumerate(shifts(left_of(i), side)):
@@ -718,54 +741,88 @@
                 hi, lo = split(v)
                 r.right[at : at + n, lanes] = jnp.concatenate([hi, lo, hi], axis=1)
                 at += n
-        r.stage[...] += dot_nt(r.left[...], r.right[...])
+
+        def add(m, _):
+            third = pl.ds(pl.multiple_of(m * 3 * cb, 16), 3 * cb)
+            r.stage[third] += dot_nt(r.left[third], r.right[...])
+            if between is not None:
+                between(m)
+            return 0
+
+        lax.fori_loop(0, 3, add, 0)
 
     r.stage[...] = jnp.zeros_like(r.stage)
 
     def second_kernel(q, _):
+        zs = nearest(z, q)
         for j in range(2):
             act_copy(0, 1 - y, 2 * q + j, z, 1 - y).wait_recv()
+            call_copy(0, across, 2 * q + j).wait_recv()
+            call_copy(1, last, 2 * q + j).wait_recv()
+
+        def between(m):
+            act_step(nd + 4 + 3 * q + m)
+
+            for o in range(nz):
+                pl.when(3 * q + m == 2 * o + 5)(lambda: ins_grad.spread(o))
+            for step in range(1, nz):
+                pl.when((q == step) & (m == 0))(lambda: meet(grads, step, lambda zs: over_chan_too(zs * ny + y)))
+                pl.when((q == step) & (m == 2))(lambda: meet_sides(step - 1))
+
         kernel_grad(
             [2 * q, 2 * q + 1],
             lambda i: jnp.concatenate([r.act2[0, i], r.act2[1, i]], axis=0),
             lambda i: [r.call[j, i] for j in range(nc)],
+            between,
         )
-        zs = nearest(z, q)
-        grads.got(zs, 1 - y)
-        over_chan_too(zs * ny + 1 - y)
         return 0
 
     lax.fori_loop(0, nz, second_kernel, 0)
     g2_copy = pltpu.make_async_copy(r.stage, r.g2_out, r.g2_sem)
     g2_copy.start()
 
-    for j in range(1, nd):
-        s = lax.rem(d + j, nd)
-        to_far(s, far).wait_recv()
-        to_core(1, s, far).start()
-
-    grad = (gain1 * rs1 * (ins_grad.total() * r.slope1[d]) + r.call[c, d]).T
-    for j in range(nc):
-        r.xs[j] = grad[j * rows : (j + 1) * rows]
+    r.block_out[...] = ((r.xin[d] + outs.total()) * mine).T
+    meet_sides(nz - 1)
     back = lambda j: send(r.xs.at[lax.rem(c + j, nc)], r.rx.at[c], r.in_s.at[j], r.in_r.at[c], (d, lax.rem(c + j, nc)))
-    for j in range(1, nc):
-        back(j).start()
-    r.rx[c] = r.xs[c]
+
+    def input_rows():
+        grad = (gain1 * rs1 * (ins_grad.total() * r.slope1[d]) + r.call[c, d]).T
+        for j in range(nc):
+            r.xs[j] = grad[j * rows : (j + 1) * rows]
+        for j in range(1, nc):
+            back(j).start()
+        r.rx[c] = r.xs[c]
 
     g2_copy.wait()
     r.stage[...] = jnp.zeros_like(r.stage)
 
-    def first_kernel(q):
-        kernel_grad([2 * q, 2 * q + 1], lambda i: r.act1[i], lambda i: [r.dall[s, i] for s in range(nd)])
-
-    first_kernel(c)
-    for j in range(1, nd):
-        to_core(0, lax.rem(d + j, nd), across).wait_recv()
-    first_kernel(across)
-    first_kernel(far)
-    for j in range(1, nd):
-        to_core(1, lax.rem(d + j, nd), last).wait_recv()
-    first_kernel(last)
+    def first_kernel(j, _):
+        @pl.when(j == 1)
+        def _():
+            for o in range(1, nd):
+                to_core(0, lax.rem(d + o, nd), across).wait_recv()
+
+        @pl.when(j == 2)
+        def _():
+            for o in range(1, nd):
+                s = lax.rem(d + o, nd)
+                to_far(s, far).wait_recv()
+                to_core(1, s, far).start()
+
+        @pl.when(j == 3)
+        def _():
+            for o in range(1, nd):
+                to_core(1, lax.rem(d + o, nd), last).wait_recv()
+
+        q = jnp.where(j == 0, c, jnp.where(j == 1, across, jnp.where(j == 2, far, last)))
+
+        def between(m):
+            pl.when((j == 2) & (m == 1))(input_rows)
+
+        kernel_grad([2 * q, 2 * q + 1], lambda i: r.act1[i], lambda i: [r.dall[s, i] for s in range(nd)], between)
+        return 0
+
+    lax.fori_loop(0, nc, first_kernel, 0)
     g1_copy = pltpu.make_async_copy(r.stage, r.g1_out, r.g1_sem)
     g1_copy.start()
 
@@ -773,8 +830,7 @@
     total = vectors.total()
     per = cb // db
     rows_of = lambda j: jnp.concatenate([r.vecs[per * c + q, j : j + 1, :db] for q in range(per)], axis=1)
-    r.sh1[...], r.gg1[...] = total[0:1].reshape(cb), total[1:2].reshape(cb)
-    r.sh2[...], r.gg2[...] = rows_of(2).reshape(cb), rows_of(3).reshape(cb)
+    r.small[...] = stacked([total[0:1], total[1:2], rows_of(2), rows_of(3), jnp.broadcast_to(norm, (1, cb))], cb)
     for j in range(1, nc):
         back(j).wait_send()
         other = lax.rem(c + j, nc)
@@ -782,8 +838,11 @@
     for j in range(nc):
         r.input_grad[:, j * cb : (j + 1) * cb] = r.rx[j]
 
-    for line in (ins, cots, grads):
+    own_cot(c).wait_send()
+    for line in (ins, cots, fars, grads):
         line.drain()
+    for zs in range(nz):
+        far_side(zs).wait_send()
 
     @pl.when(c == owner)
     def _():
@@ -791,9 +850,8 @@
             piece(j).wait_send()
 
     def sent(i, _):
-        call_copy(c, 0, i, far).wait_send()
-        call_copy(c, 1, i, across).wait_send()
-        call_copy(far, 2, i, across).wait_send()
+        call_copy(0, c, i).wait_send()
+        call_copy(1, far, i).wait_send()
         pl.when((z >= c) & (z < nz - 1))(lambda: act_up(i).wait_send())
         pl.when((z <= c) & (z > 0))(lambda: act_down(i).wait_send())
         act_side(i).wait_send()
@@ -808,26 +866,66 @@
     g1_copy.wait()
 
 
+def close_kernel(pieces, small, block_in, rows_in, first_in, second_in, block_out, rows_out, first_out, second_out,
+                 gg1, sh1, gg2, sh2, norm, first, second, vec, sems, side_sems):
+    cut = first_in.shape[0] // pieces
+    legs = []
+    for j in range(pieces):
+        part = pl.ds(j * cut, cut)
+        for k, (src, mid, dst) in enumerate(((second_in, second, second_out), (first_in, first, first_out))):
+            legs.append((
+                pltpu.make_async_copy(src.at[part], mid.at[part], sems.at[0, k, j]),
+                pltpu.make_async_copy(mid.at[part], dst.at[part], sems.at[1, k, j]),
+            ))
+    sides = [pltpu.make_async_copy(a, b, side_sems.at[j])
+             for j, (a, b) in enumerate(((small, vec), (block_in, block_out), (rows_in, rows_out)))]
+    for cp in sides:
+        cp.start()
+    for come, _ in legs:
+        come.start()
+    sides[0].wait()
+    for j, ref in enumerate((sh1, gg1, sh2, gg2)):
+        ref[...] = vec[j : j + 1].reshape(vec.shape[1])
+    norm[0] = jnp.sum(vec[4:5, 0:1])
+    for come, go in legs:
+        come.wait()
+        go.start()
+    for _, go in legs:
+        go.wait()
+    for cp in sides[1:]:
+        cp.wait()
+
+
 def fused_on_device(p, image_rows, groups, conv_first, conv_second, gain_first, shift_first, gain_second, shift_second, cotangent):
     cb, px = p.cb, p.px
     rows = px // p.nc
     scratch = scratch_of(p)
     out = lambda *s: jax.ShapeDtypeStruct(s, F32)
     any_, vmem, smem = (pl.BlockSpec(memory_space=m) for m in (pl.ANY, VMEM, SMEM))
-    block_out, input_grad, g1, g2, gg1, sh1, gg2, sh2, norm = pl.pallas_call(
+    large = (out(px, cb), out(rows, p.ch), out(9 * cb, p.ch), out(9 * cb, p.ch))
+    block_out, input_grad, g1, g2, small = pl.pallas_call(
         functools.partial(step_kernel, p, ARGS + OUTS + tuple(scratch)),
-        out_shape=(out(px, cb), out(rows, p.ch), out(9 * cb, p.ch), out(9 * cb, p.ch), out(cb), out(cb), out(cb), out(cb), out(1, 1)),
+        out_shape=large + (out(8, cb),),
         in_specs=[vmem, vmem, any_, any_, vmem, vmem, vmem, vmem, smem],
-        out_specs=(vmem, vmem, any_, any_, vmem, vmem, vmem, vmem, smem),
+        out_specs=(vmem, vmem, any_, any_, vmem),
         scratch_shapes=list(scratch.values()),
         compiler_params=pltpu.CompilerParams(collective_id=0, has_side_effects=True, vmem_limit_bytes=LIMIT),
     )(
         image_rows.reshape(rows, p.ch), cotangent.reshape(px, cb), conv_first.reshape(9, cb, p.ch),
         conv_second.reshape(9, cb, p.ch), gain_first, shift_first, gain_second, shift_second, groups,
     )
+    pieces = 6
+    block_out, input_grad, g1, g2, gg1, sh1, gg2, sh2, norm = pl.pallas_call(
+        functools.partial(close_kernel, pieces),
+        out_shape=large + (out(cb),) * 4 + (out(1),),
+        in_specs=[any_] * 5,
+        out_specs=(vmem, vmem, any_, any_) + (vmem,) * 4 + (smem,),
+        scratch_shapes=[VMEM((9 * cb, p.ch), F32), VMEM((9 * cb, p.ch), F32), VMEM((8, cb), F32), DMA((2, 2, pieces)), DMA((3,))],
+        compiler_params=pltpu.CompilerParams(vmem_limit_bytes=LIMIT),
+    )(small, block_out, input_grad, g1, g2)
     return (
         block_out.reshape(cotangent.shape), input_grad.reshape(image_rows.shape),
-        g1.reshape(conv_first.shape), g2.reshape(conv_second.shape), gg1, sh1, gg2, sh2, norm[0, 0],
+        g1.reshape(conv_first.shape), g2.reshape(conv_second.shape), gg1, sh1, gg2, sh2, norm.reshape(()),
     )
 
 

time: 235 us -> 192 us (0.82); the launches traced: 234 us -> 188 us
  Pallas kernels: 220 us -> 187 us
  local copies, waits for them, and re-layouts: 11.7 us -> 0 us
    pallas_call x1, Pallas kernels: 220 us -> 181 us  [fused_on_device(): pl.pallas_call(functools.partial(step_kernel, p, ARGS + OUTS + tuple(scra...]
    unnamed x18 -> x0, local copies, waits for them, and re-layouts: 11.7 us -> none
    pallas_call x0 -> x1, Pallas kernels: none -> 6.39 us  [fused_on_device(): pl.pallas_call(functools.partial(close_kernel, pieces), out_shape=large +...]
where the time goes in v3:
time: 192 us; the launch traced here: 188 us
  Pallas kernels  187 us (97%)
    pallas_call x1, Pallas kernels, fused_on_device(): pl.pallas_call(functools.partial(step_kernel, p, ARGS + OUTS + tuple(scra...  181 us
    pallas_call x1, Pallas kernels, fused_on_device(): pl.pallas_call(functools.partial(close_kernel, pieces), out_shape=large +...  6.39 us

profile of v3, /device:TPU:0, one launch (start us, length us, event | category | flops | bytes accessed | tf_op | source)
XLA Modules:
  0.0 188.4 jit_solution(7193433353222389590)
XLA Ops:
  1.3 180.5 %shard_map.160 = (f32[256,160]{1,0:T(8,128)}, f32[64,640]{1,0:T(8,128)}, f32[1440,640]{1,0:T(8,128)}, f32[1440,640]{1,0:T(8,128)}, f32[8,160]{1,0:T(8,128)}) custom-call(f32[64,640]{1,0:T(8,128)} %bitcast.12, f32[256,160]{1,0:T(8,128)} %bitcast.11, f32[9,160,640]{2,1,0:T(8,128)} %bitcast.9, f32[9,160,640]{2,1,0:T(8,128)} %bitcast.10, f32[160]{0:T(256)} %refs_4_.1, ...), custom_call_target="tpu_custom_call" | custom-call | tf_op jit(solution)/shard_map/pallas_call | solution.py:906
  181.8 6.4 %shard_map.161 = (f32[256,160]{1,0:T(8,128)}, f32[64,640]{1,0:T(8,128)}, f32[1440,640]{1,0:T(8,128)}, f32[1440,640]{1,0:T(8,128)}, f32[160]{0:T(256)}, /*index=5...) custom-call(f32[8,160]{1,0:T(8,128)} %get-tuple-element.23.small, f32[256,160]{1,0:T(8,128)} %get-tuple-element.24.block_in, ...), custom_call_target="tpu_custom_call" | custom-call | tf_op jit(solution)/shard_map/pallas_call | solution.py:918

commit v4 on v3

--- a/solution.py
+++ b/solution.py
@@ -287,7 +287,7 @@
     return dict(
         k1w=f(9, cb, 256), k2w=f(9, db, p.ch), ks=f(nc, cb, 9 * db), b2=f(cb, 9 * db),
         a1=f(9 * db, cb), a2=f(9 * db, cb), g1=f(9 * db, cb), g2=f(9 * db, cb),
-        a_cat=h(2, 9 * db, 3 * cb), bm=h(2, cb, 9 * db), b2m=h(2, cb, 9 * db), colh=h(9 * db, px), coll=h(9 * db, px),
+        a_cat=h(2, 9 * db, 3 * cb), bm=h(2, cb, 9 * db), b2m=h(2, cb, 9 * db), colh=h(2, 9 * db, px), coll=h(2, 9 * db, px),
         xs=f(nc, rows, cb), rx=f(nc, rows, cb), xin=f(nd, cb, px), act1=f(nd, cb, px), slope1=f(nd, cb, px),
         call=f(nc, nd, cb, px),
         part=f(3 * nd, db, px), near=f(3 * nd, db // 2, px), half=f(3 * nd, db // 2, px), away=f(3 * nd, db // 2, px),
@@ -306,10 +306,19 @@
         cs1=DMA((3 * nd,)), cr1=DMA((3 * nd,)), cs2=DMA((3 * nd,)), cr2=DMA((3 * nd,)), cs3=DMA((3 * nd,)), cr3=DMA((3 * nd,)),
         o_s1=DMA((nz,)), o_r1=DMA((nz,)), o_s2=DMA((nz,)), o_r2=DMA((nz,)),
         i_s1=DMA((nz,)), i_r1=DMA((nz,)), i_s2=DMA((nz,)), i_r2=DMA((nz,)),
-        call_s=DMA((2, nd)), call_r=DMA((2, nd)), own_s=DMA, f_s=DMA((3, nz)), f_r=DMA((nd,)), act_s=DMA((3, nd)), act_r=DMA((ny, nd)),
+        call_s=DMA((2, nd)), call_r=DMA((2, nd)), own_s=DMA, f_s=DMA((3, nz)), f_r=DMA((nd,)), col_s=DMA((nz,)), act_s=DMA((3, nd)), act_r=DMA((ny, nd)),
         far_s=DMA((nd,)), far_r=DMA((nd,)), core_s=DMA((2, nd)), core_r=DMA((2, nd)), in_s=DMA((nc,)), in_r=DMA((nc,)),
     )
 
+
+FARS = (3, 6, 12)
+OUTS_AT = (9, 10, 11, 13)
+ACT = (44, 8, 4)
+LINE_AT = (5, 9, 12)
+SIDE_AT = (6, 11, 14, 17)
+NEAR_AT = 14
+SUMS_AT = (18, 20, 22, 24)
+ROWS_AT = 28
 
 ARGS = ("x", "cot", "k1", "k2", "gain1", "shift1", "gain2", "shift2", "groups")
 OUTS = ("block_out", "input_grad", "g1_out", "g2_out", "small")
@@ -324,13 +333,17 @@
     far, across = lax.rem(c + 2, 4), c + 1 - 2 * k
     last = 6 - c - far - across
     rows = px // nc
-    owner = lax.div(d * db, cb)
+    owner = (1 - lax.div(z, 2)) * (2 - 2 * lax.rem(z, 2)) + lax.div(z, 2) * (1 + 2 * lax.rem(z, 2))
+    origin = lambda c: (1 - c // 2) * (1 + c % 2) + c // 2 * 3 * (c % 2)
+    start_z = (1 - lax.div(c, 2)) * (1 + k) + lax.div(c, 2) * 3 * k
+    first = owner * cb + y * db
+    slots = [origin(q) * ny + j for q in range(nc) for j in range(ny)]
     image = lambda j: nearest(z, lax.div(j, 2)) * ny + y + lax.rem(j, 2) * (1 - 2 * y)
 
-    base = lax.min(lax.div(d * db, 128), (p.ch - 256) // 128) * 128
+    base = lax.min(lax.div(first, 128), (p.ch - 256) // 128) * 128
     k1_copy = pltpu.make_async_copy(r.k1.at[:, :, pl.ds(pl.multiple_of(base, 128), 256)], r.k1w, r.k1_sem)
     k1_copy.start()
-    k2_rows = pl.ds(pl.multiple_of(d * db - owner * cb, 8), db)
+    k2_rows = pl.ds(pl.multiple_of(y * db, 8), db)
     k2_copy = pltpu.make_async_copy(r.k2.at[:, k2_rows], r.k2w, r.k2_sem)
     pl.when(c == owner)(lambda: k2_copy.start())
     greet(p)
@@ -348,6 +361,27 @@
     mine = valid_map(flag, side, px)
     r.call[c, d] = r.cot[...].T * mine
 
+    def meet(line, step, then=None):
+        def one(zs):
+            line.got(zs, y)
+            line.hand_on(zs)
+            if then is not None:
+                then(zs)
+
+        pl.when(z >= step)(lambda: one(lax.max(z - step, 0)))
+        pl.when(z + step < nz)(lambda: one(lax.min(z + step, nz - 1)))
+
+    cots = Line(p, lambda s: r.call.at[c, s], r.c_s, r.c_r)
+    cots.hand_on(z)
+    own_cot = lambda q: send(r.call.at[q, d], r.call.at[q, d], r.own_s, r.f_r.at[d], (d, far))
+    fars = Line(p, lambda s: r.call.at[far, s], r.f_s, r.f_r, False)
+    column = lambda q, zs: send(
+        r.call.at[q, zs * ny + 1 - y], r.call.at[q, zs * ny + 1 - y], r.col_s.at[zs], r.f_r.at[zs * ny + 1 - y], (d, far)
+    )
+    call_copy = lambda lane, q, i: send(
+        r.call.at[q, i], r.call.at[q, i], r.call_s.at[lane, i], r.call_r.at[lane, i], (d, across)
+    )
+
     @pl.when(c == owner)
     def _():
         k2_copy.wait()
@@ -377,7 +411,7 @@
             piece(j).start()
 
     k1_copy.wait()
-    turn = lax.rem(256 - (d * db - base), 256)
+    turn = lax.rem(256 - (first - base), 256)
     b1 = jnp.concatenate([pltpu.roll(r.k1w[t], turn, axis=1)[:, :db] for t in range(9)], axis=1)
     hi, lo = split(b1)
     r.bm[0], r.bm[1] = hi, lo
@@ -385,6 +419,8 @@
     hi, lo = split(r.a1[...])
     r.a_cat[0] = jnp.concatenate([hi, hi, lo], axis=1)
 
+    meet(cots, 1)
+    own_cot(c).start()
     stats.finish()
 
     def val_of(i):
@@ -415,173 +451,143 @@
         r.part[first + i] = gather_taps(prod, side, db) * val_of(i)
         chan.first(first + i).start()
 
-    def meet(line, step, then=None):
-        def one(zs):
-            line.got(zs, y)
-            line.hand_on(zs)
-            if then is not None:
-                then(zs)
-
-        pl.when(z >= step)(lambda: one(lax.max(z - step, 0)))
-        pl.when(z + step < nz)(lambda: one(lax.min(z + step, nz - 1)))
-
-    cots = Line(p, lambda s: r.call.at[c, s], r.c_s, r.c_r)
+    def back_item(j):
+        return nd + image(j)
+
+    def set_back(a2):
+        for t in range(9):
+            hi, lo = split(a2[(8 - t) * db : (9 - t) * db])
+            r.a_cat[1, t * db : (t + 1) * db] = jnp.concatenate([hi, hi, lo], axis=1)
+
+    def second_block():
+        @pl.when(c == owner)
+        def _():
+            r.b2[...] = r.ks[c]
+
+        @pl.when(c != owner)
+        def _():
+            send(r.ks.at[0], r.b2, r.ks_s.at[0], r.ks_r, (d, owner)).wait_recv()
+
+        r.a2[...] = r.b2[...].T
+        set_back(r.a2)
+        b2h, b2l = split(r.b2[...])
+        r.b2m[0], r.b2m[1] = b2h, b2l
 
     def forward(kk, _):
         zs = nearest(z, kk)
         first_map(zs * ny + y, gain1, shift1)
         chan.advance(2 * kk, nd, image)
         meet(ins, kk + 1)
-        pl.when(kk == nz - 2)(lambda: cots.hand_on(z))
+        pl.when(kk == 0)(lambda: meet(cots, 2))
+        pl.when(kk == 1)(lambda: meet(cots, 3))
+        pl.when(kk == 1)(second_block)
         ins.got(zs, 1 - y)
         first_map(zs * ny + 1 - y, gain1, shift1)
         chan.advance(2 * kk + 1, nd, image)
+
+        @pl.when(kk > 0)
+        def _():
+            before = nearest(z, lax.max(kk - 1, 0))
+            second_back(before * ny + y, nd)
+            chan.advance(2 * kk - 2, nd, back_item)
+            cots.got(before, 1 - y)
+            second_back(before * ny + 1 - y, nd)
+            chan.advance(2 * kk - 1, nd, back_item)
+
         return 0
 
     lax.fori_loop(0, nz, forward, 0)
-
-    own_cot = lambda q: send(r.call.at[q, d], r.call.at[q, d], r.own_s, r.f_r.at[d], (d, far))
-    own_cot(c).start()
-    fars = Line(p, lambda s: r.call.at[far, s], r.f_s, r.f_r, False)
-    far_side = lambda zs: fars.side(zs)
-    call_copy = lambda lane, q, i: send(
-        r.call.at[q, i], r.call.at[q, i], r.call_s.at[lane, i], r.call_r.at[lane, i], (d, across)
-    )
-
-    meet(cots, 1)
-
-    @pl.when(c == owner)
-    def _():
-        r.b2[...] = r.ks[c]
-
-    @pl.when(c != owner)
-    def _():
-        send(r.ks.at[0], r.b2, r.ks_s.at[0], r.ks_r, (d, owner)).wait_recv()
-
-    def set_back(a2):
-        for t in range(9):
-            hi, lo = split(a2[(8 - t) * db : (9 - t) * db])
-            r.a_cat[1, t * db : (t + 1) * db] = jnp.concatenate([hi, hi, lo], axis=1)
-
+    furthest = nearest(z, nz - 1)
     chan.advance(nd, nd, image)
-    r.a2[...] = r.b2[...].T
+    second_back(furthest * ny + y, nd)
+    chan.advance(nd - 2, nd, back_item)
     chan.advance(nd + 1, nd, image)
-    set_back(r.a2)
+    cots.got(furthest, 1 - y)
+    second_back(furthest * ny + 1 - y, nd)
+    chan.advance(nd - 1, nd, back_item)
     chan.advance(nd + 2, nd, image)
-    b2h, b2l = split(r.b2[...])
-    r.b2m[0], r.b2m[1] = b2h, b2l
+    chan.advance(nd, nd, back_item)
     chan.advance(nd + 3, nd, image)
-
-    meet(cots, 2)
 
     params.finish()
     both = [r.pars[owner, j : j + 1] for j in range(2)]
-    low = lax.rem(d * db, cb) == 0
-    gain2, shift2 = (to_col(jnp.where(low, v[:, :db], v[:, cb - db :])) for v in both)
+    gain2, shift2 = (to_col(jnp.where(y == 0, v[:, :db], v[:, cb - db :])) for v in both)
 
     def add_up(i, carry):
         return carry + lanes_sum(r.sums[i] * val_of(i))
 
+    chan.advance(nd + 1, nd, back_item)
     center2 = lax.fori_loop(0, nd, add_up, jnp.zeros((db, 1), F32)) / pixels
 
     def add_squares(i, carry):
         off = r.sums[i] - center2
         return carry + lanes_sum(val_of(i) * off * off)
 
+    chan.advance(nd + 2, nd, back_item)
     rs2 = lax.rsqrt(lax.fori_loop(0, nd, add_squares, jnp.zeros((db, 1), F32)) / pixels + epsilon)
 
+    chan.advance(nd + 3, nd, back_item)
+    own_cot(far).wait_recv()
+    fars.hand_on(z)
+    for zs in range(nz):
+        column(c, zs).start()
+
+    def inner_sums(i, carry):
+        val = val_of(i)
+        scaled = (r.sums[i] - center2) * rs2
+        act, slope = silu_and_slope(scaled * gain2 + shift2)
+        r.own2[i] = act * val
+        dpre = r.sums[nd + i] * (slope * val)
+        r.dpre[i] = dpre
+        return carry[0] + lanes_sum(dpre), carry[1] + lanes_sum(dpre * scaled)
+
+    zero = jnp.zeros((db, 1), F32)
+    sh2, gg2 = lax.fori_loop(0, nd, inner_sums, (zero, zero))
+
     outs = ImageSum(p, r.outp, r.outn, r.outc, r.outw, r.o_s1, r.o_r1, r.o_s2, r.o_r2)
 
-    def set_cols(maps):
+    def set_cols(w, maps):
         for t, m in enumerate(maps):
             hi, lo = split(m)
-            r.colh[t * db : (t + 1) * db] = hi
-            r.coll[t * db : (t + 1) * db] = lo
-
-    def im2col_dot(which):
-        return dot(which[0], r.colh[...]) + dot(which[0], r.coll[...]) + dot(which[1], r.colh[...])
-
-    def wgrad(other):
+            r.colh[w, t * db : (t + 1) * db] = hi
+            r.coll[w, t * db : (t + 1) * db] = lo
+
+    def im2col_dot(w, which):
+        return dot(which[0], r.colh[w]) + dot(which[0], r.coll[w]) + dot(which[1], r.colh[w])
+
+    def wgrad(w, other):
         oh, ol = split(other)
-        left = jnp.concatenate([r.colh[...], r.colh[...], r.coll[...]], axis=1)
+        left = jnp.concatenate([r.colh[w], r.colh[w], r.coll[w]], axis=1)
         return dot_nt(left, jnp.concatenate([oh, ol, oh], axis=1))
 
+    r.g1[...] = jnp.zeros_like(r.g1)
     r.g2[...] = jnp.zeros_like(r.g2)
-
-    def second_map(i):
-        val = val_of(i)
-        act, slope = silu_and_slope((r.sums[i] - center2) * rs2 * gain2 + shift2)
-        r.slope2[i] = slope * val
-        set_cols(shifts(act * val, side))
-        r.outp[i] = im2col_dot((r.b2m[0], r.b2m[1]))
-        r.g2[...] += wgrad(r.call[c, i])
-
-    def back_item(j):
-        return nd + image(j)
-
-    def cotangent(kk, _):
-        zs = nearest(z, kk)
-        second_back(zs * ny + y, nd)
-        chan.advance(2 * kk, nd, back_item)
-
-        @pl.when(kk > 0)
-        def _():
-            before = nearest(z, lax.max(kk - 1, 0))
-            second_map(before * ny + 1 - y)
-            outs.near(before).start()
-
-        pl.when(kk == 0)(lambda: meet(cots, 3))
-
-        @pl.when(kk == nz - 2)
-        def _():
-            own_cot(far).wait_recv()
-            fars.hand_on(z)
-
-        cots.got(zs, 1 - y)
-        second_back(zs * ny + 1 - y, nd)
-        chan.advance(2 * kk + 1, nd, back_item)
-        second_map(zs * ny + y)
-        return 0
-
-    lax.fori_loop(0, nz, cotangent, 0)
-    chan.advance(nd, nd, back_item)
-    furthest = nearest(z, nz - 1)
-    second_map(furthest * ny + 1 - y)
-    outs.near(furthest).start()
-    chan.advance(nd + 1, nd, back_item)
-    set_back(r.g2)
-    chan.advance(nd + 2, nd, back_item)
-    chan.advance(nd + 3, nd, back_item)
-
-    def inner_sums(i, carry):
-        dpre = r.sums[nd + i] * r.slope2[i]
-        r.dpre[i] = dpre
-        scaled = (r.sums[i] - center2) * rs2
-        return carry[0] + lanes_sum(dpre), carry[1] + lanes_sum(dpre * scaled)
-
-    zero = jnp.zeros((db, 1), F32)
-    sh2, gg2 = lax.fori_loop(0, nd, inner_sums, (zero, zero))
-    r.g1[...] = jnp.zeros_like(r.g1)
-
     change_item = lambda j: 2 * nd + j
 
-    def backward(i, carry):
-        call_copy(0, c, i).start()
-
-        pl.when(i == 0)(lambda: far_side(z).start())
-        pl.when(i >= nz)(lambda: outs.spread(nearest(z, lax.max(nd - 1 - i, 0))))
+    def settle(t):
+        for step in range(1, nz):
+            pl.when(t == FARS[step - 1])(lambda: meet(fars, step))
+        for zs in range(nz):
+            pl.when(t == OUTS_AT[zs])(lambda: outs.spread(zs))
+
+    def gradients(i, carry):
         scaled = (r.sums[i] - center2) * rs2
         dinner = gain2 * rs2 * (r.dpre[i] - val_of(i) * (sh2 + scaled * gg2) / pixels)
-        set_cols(shifts(dinner, side, -1))
-        r.g1[...] += wgrad(r.act1[i])
-        dpre1 = im2col_dot((r.bm[0], r.bm[1])) * r.slope1[i]
+        set_cols(0, shifts(r.own2[i], side))
+        set_cols(1, shifts(dinner, side, -1))
+        r.outp[i] = im2col_dot(0, (r.b2m[0], r.b2m[1]))
+        r.g2[...] += wgrad(0, r.call[c, i])
+        r.g1[...] += wgrad(1, r.act1[i])
+        dpre1 = im2col_dot(1, (r.bm[0], r.bm[1])) * r.slope1[i]
         scaled1 = (r.xin[i] - center1) * rs1
-        pl.when(i == 2)(lambda: meet(fars, 1, lambda zs: far_side(zs).start()))
-        pl.when(i == 6)(lambda: meet(fars, 2, lambda zs: far_side(zs).start()))
+        pl.when(lax.rem(i, 2) == 1 - y)(lambda: outs.near(lax.div(i, 2)).start())
+        call_copy(0, c, i).start()
+        settle(i)
         return carry[0] + lanes_sum(dpre1), carry[1] + lanes_sum(dpre1 * scaled1)
 
     zero = jnp.zeros((cb, 1), F32)
-    sh1, gg1 = lax.fori_loop(0, nd, backward, (zero, zero))
+    sh1, gg1 = lax.fori_loop(0, nd, gradients, (zero, zero))
+    set_back(r.g2)
 
     square = jnp.sum(r.g1[...] * r.g1[...] + r.g2[...] * r.g2[...], keepdims=True)
     square = square + jnp.where(c == 0, jnp.sum(sh2 * sh2 + gg2 * gg2, keepdims=True), 0.0)
@@ -622,8 +628,8 @@
     act_side = lambda i: act_copy(2, y, i, z, 1 - y)
 
     def act_hand_on(i):
-        pl.when((z >= c) & (z < nz - 1))(lambda: act_up(i).start())
-        pl.when((z <= c) & (z > 0))(lambda: act_down(i).start())
+        pl.when((z >= start_z) & (z < nz - 1))(lambda: act_up(i).start())
+        pl.when((z <= start_z) & (z > 0))(lambda: act_down(i).start())
         act_side(i).start()
 
     def second_act(i):
@@ -634,15 +640,15 @@
 
     def far_to_core(j):
         zs = nearest(z, lax.div(j, 2))
-        pl.when(lax.rem(j, 2) == 1)(lambda: fars.got(zs, 1 - y))
+        pl.when(lax.rem(j, 2) == 1)(lambda: column(far, zs).wait_recv())
         call_copy(1, far, image(j)).start()
 
-    away = lax.max(z - c, c - z)
+    away = lax.max(z - start_z, start_z - z)
 
     def act_step(t):
         for i in range(nd):
 
-            @pl.when((away > 0) & (t == lax.div(16 + 8 * away + 5 * i, 4)))
+            @pl.when((away > 0) & (t == lax.div(ACT[0] + ACT[1] * away + ACT[2] * i, 4)))
             def _():
                 act_copy(0, y, i, z, 1 - y).wait_recv()
                 act_hand_on(i)
@@ -674,27 +680,27 @@
     def inner_grad(i):
         second_act(i)
         dpre = (r.sums[nd + i] + factor * r.sums[2 * nd + i]) * r.slope2[i]
-        dinner = gain2 * rs2 * dpre
-        r.dall[d, i] = dinner
+        r.dall[d, i] = gain2 * rs2 * dpre
         r.add2[0] += dpre
         r.add2[1] += dpre * ((r.sums[i] - center2) * rs2)
-        set_cols(shifts(dinner, side, -1))
-        dact1 = im2col_dot((r.bm[0], r.bm[1]))
+
+        @pl.when(z == start_z)
+        def _():
+            r.act2[y, i] = r.own2[i]
+            act_hand_on(i)
+
+    def rows_grad(i):
+        set_cols(1, shifts(r.dall[d, i], side, -1))
+        dact1 = im2col_dot(1, (r.bm[0], r.bm[1]))
         r.inp[i] = dact1
         dpre1 = dact1 * r.slope1[i]
         r.add1[0] += dpre1
         r.add1[1] += dpre1 * ((r.xin[i] - center1) * rs1)
 
-        @pl.when(z == c)
-        def _():
-            r.act2[y, i] = r.own2[i]
-            act_hand_on(i)
-
-
     same = lambda j: j
 
     def start(j, _):
-        pl.when(j == 2)(lambda: meet(fars, 3, lambda zs: far_side(zs).start()))
+        settle(nd + j)
         first_map(j, gain1, shift1)
         chan.advance(nd + j, nd, change_item)
         chan.advance(j, nd, same)
@@ -703,6 +709,7 @@
     def steady(j, _):
         first_map(j, gain1, shift1)
         chan.advance(j, nd, same)
+        settle(nd + j)
         inner_grad(j - 4)
         far_to_core(j - 4)
         act_step(j)
@@ -710,8 +717,8 @@
 
     def end(j, _):
         chan.advance(j, nd, same)
+        settle(nd + j)
         inner_grad(j - 4)
-        ins_grad.near(j - nd).start()
         far_to_core(j - 4)
         act_step(j)
         return 0
@@ -720,6 +727,38 @@
     lax.fori_loop(4, nd, steady, 0)
     lax.fori_loop(nd, nd + 4, end, 0)
     grads.hand_on(z)
+    back = lambda j: send(r.xs.at[lax.rem(c + j, nc)], r.rx.at[c], r.in_s.at[j], r.in_r.at[c], (d, lax.rem(c + j, nc)))
+
+    def input_rows():
+        grad = (gain1 * rs1 * (ins_grad.total() * r.slope1[d]) + r.call[c, d]).T
+        for j in range(nc):
+            r.xs[j] = grad[j * rows : (j + 1) * rows]
+        for j in range(1, nc):
+            back(j).start()
+        r.rx[c] = r.xs[c]
+
+    def gather_grads(u):
+        for step in range(1, nz):
+            pl.when(u == LINE_AT[step - 1])(lambda: meet(grads, step, lambda zs: over_chan_too(zs * ny + y)))
+        for step in range(nz):
+            pl.when(u == SIDE_AT[step])(lambda: meet_sides(step))
+
+        @pl.when(u == NEAR_AT)
+        def _():
+            for o in range(nz):
+                ins_grad.near(nearest(z, nz - 1 - o)).start()
+
+        for o in range(nz):
+            pl.when(u == SUMS_AT[o])(lambda: ins_grad.spread(nearest(z, nz - 1 - o)))
+        pl.when(u == ROWS_AT)(input_rows)
+
+    def all_rows(i, _):
+        rows_grad(i)
+        act_step(nd + 4 + i)
+        gather_grads(i)
+        return 0
+
+    lax.fori_loop(0, nd, all_rows, 0)
     sh1, gg1 = lanes_sum(r.add1[0]), lanes_sum(r.add1[1])
     sh2, gg2 = lanes_sum(r.add2[0]), lanes_sum(r.add2[1])
 
@@ -761,13 +800,9 @@
             call_copy(1, last, 2 * q + j).wait_recv()
 
         def between(m):
-            act_step(nd + 4 + 3 * q + m)
-
-            for o in range(nz):
-                pl.when(3 * q + m == 2 * o + 5)(lambda: ins_grad.spread(o))
-            for step in range(1, nz):
-                pl.when((q == step) & (m == 0))(lambda: meet(grads, step, lambda zs: over_chan_too(zs * ny + y)))
-                pl.when((q == step) & (m == 2))(lambda: meet_sides(step - 1))
+            u = nd + 3 * q + m
+            act_step(nd + 4 + u)
+            gather_grads(u)
 
         kernel_grad(
             [2 * q, 2 * q + 1],
@@ -782,17 +817,7 @@
     g2_copy.start()
 
     r.block_out[...] = ((r.xin[d] + outs.total()) * mine).T
-    meet_sides(nz - 1)
-    back = lambda j: send(r.xs.at[lax.rem(c + j, nc)], r.rx.at[c], r.in_s.at[j], r.in_r.at[c], (d, lax.rem(c + j, nc)))
-
-    def input_rows():
-        grad = (gain1 * rs1 * (ins_grad.total() * r.slope1[d]) + r.call[c, d]).T
-        for j in range(nc):
-            r.xs[j] = grad[j * rows : (j + 1) * rows]
-        for j in range(1, nc):
-            back(j).start()
-        r.rx[c] = r.xs[c]
-
+    gather_grads(20)
     g2_copy.wait()
     r.stage[...] = jnp.zeros_like(r.stage)
 
@@ -817,19 +842,19 @@
         q = jnp.where(j == 0, c, jnp.where(j == 1, across, jnp.where(j == 2, far, last)))
 
         def between(m):
-            pl.when((j == 2) & (m == 1))(input_rows)
-
-        kernel_grad([2 * q, 2 * q + 1], lambda i: r.act1[i], lambda i: [r.dall[s, i] for s in range(nd)], between)
+            gather_grads(21 + 3 * j + m)
+
+        kernel_grad([2 * q, 2 * q + 1], lambda i: r.act1[i], lambda i: [r.dall[s, i] for s in slots], between)
         return 0
 
     lax.fori_loop(0, nc, first_kernel, 0)
+    gather_grads(33)
     g1_copy = pltpu.make_async_copy(r.stage, r.g1_out, r.g1_sem)
     g1_copy.start()
 
     vectors.finish()
     total = vectors.total()
-    per = cb // db
-    rows_of = lambda j: jnp.concatenate([r.vecs[per * c + q, j : j + 1, :db] for q in range(per)], axis=1)
+    rows_of = lambda j: jnp.concatenate([r.vecs[start_z * ny + q, j : j + 1, :db] for q in range(ny)], axis=1)
     r.small[...] = stacked([total[0:1], total[1:2], rows_of(2), rows_of(3), jnp.broadcast_to(norm, (1, cb))], cb)
     for j in range(1, nc):
         back(j).wait_send()
@@ -842,7 +867,7 @@
     for line in (ins, cots, fars, grads):
         line.drain()
     for zs in range(nz):
-        far_side(zs).wait_send()
+        column(c, zs).wait_send()
 
     @pl.when(c == owner)
     def _():
@@ -852,8 +877,8 @@
     def sent(i, _):
         call_copy(0, c, i).wait_send()
         call_copy(1, far, i).wait_send()
-        pl.when((z >= c) & (z < nz - 1))(lambda: act_up(i).wait_send())
-        pl.when((z <= c) & (z > 0))(lambda: act_down(i).wait_send())
+        pl.when((z >= start_z) & (z < nz - 1))(lambda: act_up(i).wait_send())
+        pl.when((z <= start_z) & (z > 0))(lambda: act_down(i).wait_send())
         act_side(i).wait_send()
         return 0
 

time: 192 us -> 171 us (0.89)
  the two profiles are of different devices: /device:TPU:0 before, /device:TPU:28 now
where the time goes in v4:
time: 171 us
  Pallas kernels  170 us (99%)
    pallas_call x1, Pallas kernels, fused_on_device(): pl.pallas_call(functools.partial(step_kernel, p, ARGS + OUTS + tuple(scra...  163 us
    pallas_call x1, Pallas kernels, fused_on_device(): pl.pallas_call(functools.partial(close_kernel, pieces), out_shape=large +...  6.39 us

profile of v4, /device:TPU:28, one launch (start us, length us, event | category | flops | bytes accessed | tf_op | source)
XLA Modules:
  0.0 171.0 jit_solution(10392224694121423775)
XLA Ops:
  1.3 163.2 %shard_map.160 = (f32[256,160]{1,0:T(8,128)}, f32[64,640]{1,0:T(8,128)}, f32[1440,640]{1,0:T(8,128)}, f32[1440,640]{1,0:T(8,128)}, f32[8,160]{1,0:T(8,128)}) custom-call(f32[64,640]{1,0:T(8,128)} %bitcast.12, f32[256,160]{1,0:T(8,128)} %bitcast.11, f32[9,160,640]{2,1,0:T(8,128)} %bitcast.9, f32[9,160,640]{2,1,0:T(8,128)} %bitcast.10, f32[160]{0:T(256)} %refs_4_.1, ...), custom_call_target="tpu_custom_call" | custom-call | tf_op jit(solution)/shard_map/pallas_call | solution.py:931
  164.5 6.4 %shard_map.161 = (f32[256,160]{1,0:T(8,128)}, f32[64,640]{1,0:T(8,128)}, f32[1440,640]{1,0:T(8,128)}, f32[1440,640]{1,0:T(8,128)}, f32[160]{0:T(256)}, /*index=5...) custom-call(f32[8,160]{1,0:T(8,128)} %get-tuple-element.23.small, f32[256,160]{1,0:T(8,128)} %get-tuple-element.24.block_in, ...), custom_call_target="tpu_custom_call" | custom-call | tf_op jit(solution)/shard_map/pallas_call | solution.py:943

commit v5 on v4

--- a/solution.py
+++ b/solution.py
@@ -56,10 +56,10 @@
     return v if mask is None else v * mask
 
 
-def shifts(v, side, sign=1):
+def shifts(v, side, sign=1, taps=(-1, 0, 1)):
     rows, cols = edge_masks(side, v.shape[1])
     by_col = {s: moved(v, s, cols[s]) for s in (-1, 0, 1)}
-    return [moved(by_col[sign * s], sign * r * side, rows[sign * r]) for r in (-1, 0, 1) for s in (-1, 0, 1)]
+    return [moved(by_col[sign * s], sign * r * side, rows[sign * r]) for r in taps for s in (-1, 0, 1)]
 
 
 def gather_taps(prod, side, n):
@@ -312,11 +312,11 @@
 
 
 FARS = (3, 6, 12)
-OUTS_AT = (9, 10, 11, 13)
+OUTS_AT = (24, 25, 26, 27)
 ACT = (44, 8, 4)
 LINE_AT = (5, 9, 12)
 SIDE_AT = (6, 11, 14, 17)
-NEAR_AT = 14
+NEAR_AT = 15
 SUMS_AT = (18, 20, 22, 24)
 ROWS_AT = 28
 
@@ -394,7 +394,6 @@
         send(r.xs.at[other], r.rx.at[other], r.xs_s.at[j], r.xs_r.at[other], (d, other)).wait_recv()
     r.xin[d] = r.rx[...].reshape(px, cb).T
     ins = Line(p, lambda s: r.xin.at[s], r.x_s, r.x_r)
-    ins.hand_on(z)
 
     count = lanes_sum(mine)
     total = lanes_sum(r.xin[d] * mine)
@@ -402,6 +401,7 @@
     r.stat[...] = stacked([to_row(total), to_row(lanes_sum(mine * off * off)), jnp.broadcast_to(flag, (1, cb))], cb)
     stats = ToAll("dp", nd, r.stat, r.stats, r.stat_s, r.stat_r)
     stats.start()
+    ins.hand_on(z)
 
     piece = lambda j: send(r.ks.at[lax.rem(c + j, nc)], r.b2, r.ks_s.at[j], r.ks_r, (d, lax.rem(c + j, nc)))
 
@@ -567,8 +567,6 @@
     def settle(t):
         for step in range(1, nz):
             pl.when(t == FARS[step - 1])(lambda: meet(fars, step))
-        for zs in range(nz):
-            pl.when(t == OUTS_AT[zs])(lambda: outs.spread(zs))
 
     def gradients(i, carry):
         scaled = (r.sums[i] - center2) * rs2
@@ -751,6 +749,8 @@
         for o in range(nz):
             pl.when(u == SUMS_AT[o])(lambda: ins_grad.spread(nearest(z, nz - 1 - o)))
         pl.when(u == ROWS_AT)(input_rows)
+        for zs in range(nz):
+            pl.when(u == OUTS_AT[zs])(lambda: outs.spread(zs))
 
     def all_rows(i, _):
         rows_grad(i)
@@ -768,27 +768,35 @@
     vectors = ToAll("dp", nd, r.vec, r.vecs, r.vec_s, r.vec_r)
     vectors.start()
 
-    def kernel_grad(images, left_of, rights_of, between=None):
+    def kernel_grad(images, left_of, rights_of, between):
+        def put_left(m):
+            for j, i in enumerate(images):
+                lanes = slice(3 * j * px, 3 * (j + 1) * px)
+                for t, v in enumerate(shifts(left_of(i), side, 1, (m - 1,))):
+                    hi, lo = split(v)
+                    r.left[(3 * m + t) * cb : (3 * m + t + 1) * cb, lanes] = jnp.concatenate([hi, hi, lo], axis=1)
+
+        def add(m):
+            third = slice(3 * m * cb, 3 * (m + 1) * cb)
+            r.stage[third] += dot_nt(r.left[third], r.right[...])
+
         for j, i in enumerate(images):
             lanes = slice(3 * j * px, 3 * (j + 1) * px)
-            for t, m in enumerate(shifts(left_of(i), side)):
-                hi, lo = split(m)
-                r.left[t * cb : (t + 1) * cb, lanes] = jnp.concatenate([hi, hi, lo], axis=1)
             at = 0
             for v in rights_of(i):
                 n = v.shape[0]
                 hi, lo = split(v)
                 r.right[at : at + n, lanes] = jnp.concatenate([hi, lo, hi], axis=1)
                 at += n
-
-        def add(m, _):
-            third = pl.ds(pl.multiple_of(m * 3 * cb, 16), 3 * cb)
-            r.stage[third] += dot_nt(r.left[third], r.right[...])
-            if between is not None:
-                between(m)
-            return 0
-
-        lax.fori_loop(0, 3, add, 0)
+        put_left(0)
+        add(0)
+        put_left(1)
+        between(0)
+        add(1)
+        put_left(2)
+        between(1)
+        add(2)
+        between(2)
 
     r.stage[...] = jnp.zeros_like(r.stage)
 
@@ -816,7 +824,6 @@
     g2_copy = pltpu.make_async_copy(r.stage, r.g2_out, r.g2_sem)
     g2_copy.start()
 
-    r.block_out[...] = ((r.xin[d] + outs.total()) * mine).T
     gather_grads(20)
     g2_copy.wait()
     r.stage[...] = jnp.zeros_like(r.stage)
@@ -849,6 +856,7 @@
 
     lax.fori_loop(0, nc, first_kernel, 0)
     gather_grads(33)
+    r.block_out[...] = ((r.xin[d] + outs.total()) * mine).T
     g1_copy = pltpu.make_async_copy(r.stage, r.g1_out, r.g1_sem)
     g1_copy.start()
 

time: 171 us -> 167 us (0.977)
  the two profiles are of different devices: /device:TPU:28 before, /device:TPU:0 now
where the time goes in v5:
time: 167 us; the launch traced here: 165 us
  Pallas kernels  163 us (98%)
    pallas_call x1, Pallas kernels, fused_on_device(): pl.pallas_call(functools.partial(step_kernel, p, ARGS + OUTS + tuple(scra...  157 us
    pallas_call x1, Pallas kernels, fused_on_device(): pl.pallas_call(functools.partial(close_kernel, pieces), out_shape=large +...  6.39 us

profile of v5, /device:TPU:0, one launch (start us, length us, event | category | flops | bytes accessed | tf_op | source)
XLA Modules:
  0.0 164.6 jit_solution(2371511785143233311)
XLA Ops:
  1.3 156.8 %shard_map.160 = (f32[256,160]{1,0:T(8,128)}, f32[64,640]{1,0:T(8,128)}, f32[1440,640]{1,0:T(8,128)}, f32[1440,640]{1,0:T(8,128)}, f32[8,160]{1,0:T(8,128)}) custom-call(f32[64,640]{1,0:T(8,128)} %bitcast.12, f32[256,160]{1,0:T(8,128)} %bitcast.11, f32[9,160,640]{2,1,0:T(8,128)} %bitcast.9, f32[9,160,640]{2,1,0:T(8,128)} %bitcast.10, f32[160]{0:T(256)} %refs_4_.1, ...), custom_call_target="tpu_custom_call" | custom-call | tf_op jit(solution)/shard_map/pallas_call | solution.py:939
  158.1 6.4 %shard_map.161 = (f32[256,160]{1,0:T(8,128)}, f32[64,640]{1,0:T(8,128)}, f32[1440,640]{1,0:T(8,128)}, f32[1440,640]{1,0:T(8,128)}, f32[160]{0:T(256)}, /*index=5...) custom-call(f32[8,160]{1,0:T(8,128)} %get-tuple-element.23.small, f32[256,160]{1,0:T(8,128)} %get-tuple-element.24.block_in, ...), custom_call_target="tpu_custom_call" | custom-call | tf_op jit(solution)/shard_map/pallas_call | solution.py:951

commit v6 on v5

--- a/solution.py
+++ b/solution.py
@@ -311,7 +311,7 @@
     )
 
 
-FARS = (3, 6, 12)
+FARS = (3, 9, 13)
 OUTS_AT = (24, 25, 26, 27)
 ACT = (44, 8, 4)
 LINE_AT = (5, 9, 12)
@@ -578,7 +578,7 @@
         r.g1[...] += wgrad(1, r.act1[i])
         dpre1 = im2col_dot(1, (r.bm[0], r.bm[1])) * r.slope1[i]
         scaled1 = (r.xin[i] - center1) * rs1
-        pl.when(lax.rem(i, 2) == 1 - y)(lambda: outs.near(lax.div(i, 2)).start())
+        pl.when((lax.rem(i, 2) == 1 - y) & (i < 2 * nz - 2))(lambda: outs.near(lax.div(i, 2)).start())
         call_copy(0, c, i).start()
         settle(i)
         return carry[0] + lanes_sum(dpre1), carry[1] + lanes_sum(dpre1 * scaled1)
@@ -592,6 +592,7 @@
     r.msg[...] = stacked([to_row(sh1), to_row(gg1), jnp.broadcast_to(square, (1, cb))], cb)
     over_dp = ToAll("dp", nd, r.msg, r.msgs, r.msg_s, r.msg_r)
     over_dp.start()
+    outs.near(nz - 1).start()
 
     def change(j, _):
         second_back(j, 2 * nd)

time: 167 us -> 164 us (0.982)
  Pallas kernels: 163 us -> 160 us
    pallas_call x1, Pallas kernels: 157 us -> 154 us  [fused_on_device(): pl.pallas_call(functools.partial(step_kernel, p, ARGS + OUTS + tuple(scra...]
where the time goes in v6:
time: 164 us; the launch traced here: 162 us
  Pallas kernels  160 us (98%)
    pallas_call x1, Pallas kernels, fused_on_device(): pl.pallas_call(functools.partial(step_kernel, p, ARGS + OUTS + tuple(scra...  154 us
    pallas_call x1, Pallas kernels, fused_on_device(): pl.pallas_call(functools.partial(close_kernel, pieces), out_shape=large +...  6.39 us

profile of v6, /device:TPU:0, one launch (start us, length us, event | category | flops | bytes accessed | tf_op | source)
XLA Modules:
  0.0 161.9 jit_solution(7938891956738229412)
XLA Ops:
  1.3 154.0 %shard_map.160 = (f32[256,160]{1,0:T(8,128)}, f32[64,640]{1,0:T(8,128)}, f32[1440,640]{1,0:T(8,128)}, f32[1440,640]{1,0:T(8,128)}, f32[8,160]{1,0:T(8,128)}) custom-call(f32[64,640]{1,0:T(8,128)} %bitcast.12, f32[256,160]{1,0:T(8,128)} %bitcast.11, f32[9,160,640]{2,1,0:T(8,128)} %bitcast.9, f32[9,160,640]{2,1,0:T(8,128)} %bitcast.10, f32[160]{0:T(256)} %refs_4_.1, ...), custom_call_target="tpu_custom_call" | custom-call | tf_op jit(solution)/shard_map/pallas_call | solution.py:940
  155.3 6.4 %shard_map.161 = (f32[256,160]{1,0:T(8,128)}, f32[64,640]{1,0:T(8,128)}, f32[1440,640]{1,0:T(8,128)}, f32[1440,640]{1,0:T(8,128)}, f32[160]{0:T(256)}, /*index=5...) custom-call(f32[8,160]{1,0:T(8,128)} %get-tuple-element.23.small, f32[256,160]{1,0:T(8,128)} %get-tuple-element.24.block_in, ...), custom_call_target="tpu_custom_call" | custom-call | tf_op jit(solution)/shard_map/pallas_call | solution.py:952

commit v7 on v6

--- a/solution.py
+++ b/solution.py
@@ -710,7 +710,6 @@
         chan.advance(j, nd, same)
         settle(nd + j)
         inner_grad(j - 4)
-        far_to_core(j - 4)
         act_step(j)
         return 0
 
@@ -718,7 +717,6 @@
         chan.advance(j, nd, same)
         settle(nd + j)
         inner_grad(j - 4)
-        far_to_core(j - 4)
         act_step(j)
         return 0
 
@@ -754,6 +752,7 @@
             pl.when(u == OUTS_AT[zs])(lambda: outs.spread(zs))
 
     def all_rows(i, _):
+        far_to_core(i)
         rows_grad(i)
         act_step(nd + 4 + i)
         gather_grads(i)

time: 164 us -> 165 us (level)
  no operation moved by 1% of the time
where the time goes in v7:
time: 165 us; the launch traced here: 162 us
  Pallas kernels  160 us (97%)
    pallas_call x1, Pallas kernels, fused_on_device(): pl.pallas_call(functools.partial(step_kernel, p, ARGS + OUTS + tuple(scra...  154 us
    pallas_call x1, Pallas kernels, fused_on_device(): pl.pallas_call(functools.partial(close_kernel, pieces), out_shape=large +...  6.39 us

profile of v7, /device:TPU:0, one launch (start us, length us, event | category | flops | bytes accessed | tf_op | source)
XLA Modules:
  0.0 161.8 jit_solution(9115427561750368458)
XLA Ops:
  1.3 154.0 %shard_map.160 = (f32[256,160]{1,0:T(8,128)}, f32[64,640]{1,0:T(8,128)}, f32[1440,640]{1,0:T(8,128)}, f32[1440,640]{1,0:T(8,128)}, f32[8,160]{1,0:T(8,128)}) custom-call(f32[64,640]{1,0:T(8,128)} %bitcast.12, f32[256,160]{1,0:T(8,128)} %bitcast.11, f32[9,160,640]{2,1,0:T(8,128)} %bitcast.9, f32[9,160,640]{2,1,0:T(8,128)} %bitcast.10, f32[160]{0:T(256)} %refs_4_.1, ...), custom_call_target="tpu_custom_call" | custom-call | tf_op jit(solution)/shard_map/pallas_call | solution.py:939
  155.3 6.4 %shard_map.161 = (f32[256,160]{1,0:T(8,128)}, f32[64,640]{1,0:T(8,128)}, f32[1440,640]{1,0:T(8,128)}, f32[1440,640]{1,0:T(8,128)}, f32[160]{0:T(256)}, /*index=5...) custom-call(f32[8,160]{1,0:T(8,128)} %get-tuple-element.23.small, f32[256,160]{1,0:T(8,128)} %get-tuple-element.24.block_in, ...), custom_call_target="tpu_custom_call" | custom-call | tf_op jit(solution)/shard_map/pallas_call | solution.py:951
